TPU v7x, 256 devices: a whole 4x4x8 slice. The times are simulated.
256 devices in a mesh: seq: 64 (over x, z, core), head: 4 (over y).
Axes of the slice: x: 4, y: 4, z: 8, core: 2. Of those that a mesh axis runs over, the one named last changes fastest.
Arguments:
- queries: bfloat16 [8192, 1024], P(('seq', 'head')), may hold values from -20 to 20
- keys: bfloat16 [8192, 1024], P(('seq', 'head')), may hold values from -8 to 8
- values: bfloat16 [8192, 1024], P(('seq', 'head')), may hold values from -6 to 6
- block_mask: int32 [8, 64, 64], P('head', 'seq'), may hold values from 0 to 1, as said below
- out_weight: bfloat16 [1024, 5120], P('head'), may hold values from -1.5 to 1.5
Outputs:
- mixed: bfloat16 [8192, 5120], P(('seq', 'head'))
Inputs may be any that keep to these rules, and one draw needn't show every extreme that they name: `block_mask`: every head's diagonal blocks are 1.
All inputs are finite; a program needn't handle non-finite values.
Results may differ from a plain program's by a relative error of at most 0.015.
Values may be sent and summed in bfloat16 or wider, within the bound.
No kernel may reach another device: no remote copies, remote signals or barrier semaphores. Data moves between devices by JAX's collectives and lax.ppermute only.
A program may use at most 64 MiB of HBM per device.

v0:
```python
import math

import jax
import jax.numpy as jnp
from jax import lax
from jax.sharding import PartitionSpec as P

HD = 128
BLK = 128


def body(queries, keys, values, block_mask, out_weight):
    local_q, local_k, local_v = (
        lax.all_to_all(queries, "head", split_axis=1, concat_axis=0, tiled=True),
        lax.all_to_all(keys, "head", split_axis=1, concat_axis=0, tiled=True),
        lax.all_to_all(values, "head", split_axis=1, concat_axis=0, tiled=True),
    )
    rows_q = local_q.shape[0]
    group = local_q.shape[1] // HD
    blocks_q = rows_q // BLK
    n_blocks = block_mask.shape[2]
    scale = 1.0 / math.sqrt(HD)
    q_heads = local_q.reshape(rows_q, group, HD)
    mask_f = block_mask.astype(jnp.float32)
    k_piece = lax.all_gather(local_k, "seq", axis=0, tiled=True)
    v_piece = lax.all_gather(local_v, "seq", axis=0, tiled=True)
    count = k_piece.shape[0]
    k_index = jnp.arange(count, dtype=jnp.int32) // BLK
    onehot = (k_index[:, None] == jnp.arange(n_blocks, dtype=jnp.int32)[None, :]).astype(
        jnp.float32
    )
    open_blocks = jnp.einsum("hab,kb->hak", mask_f, onehot)
    top = jnp.full((group, rows_q), -1e30, jnp.float32)
    k_three = k_piece.reshape(count, group, HD)
    v_three = v_piece.reshape(count, group, HD)
    scores = (
        jnp.einsum("qhd,khd->hqk", q_heads, k_three, preferred_element_type=jnp.float32) * scale
    )
    allowed = jnp.broadcast_to((open_blocks > 0.5)[:, :, None, :], (group, blocks_q, BLK, count))
    allowed = allowed.reshape(group, rows_q, count)
    new_top = jnp.maximum(top, jnp.max(jnp.where(allowed, scores, -1e30), axis=2))
    weights = jnp.where(allowed, jnp.exp(scores - new_top[:, :, None]), 0.0)
    total = jnp.sum(weights, axis=2)
    update = jnp.einsum(
        "hqk,khd->qhd", weights.astype(jnp.bfloat16), v_three, preferred_element_type=jnp.float32
    )
    acc = update
    top, total, acc = (new_top, total, acc)
    attn_rows = (
        (acc / jnp.transpose(total)[:, :, None]).astype(jnp.bfloat16).reshape(rows_q, group * HD)
    )
    return lax.psum_scatter(
        jnp.dot(attn_rows, out_weight, preferred_element_type=jnp.float32).astype(jnp.bfloat16),
        "head",
        scatter_dimension=0,
        tiled=True,
    )


def solution(mesh):
    in_specs = (
        P(("seq", "head"), None),
        P(("seq", "head"), None),
        P(("seq", "head"), None),
        P("head", "seq", None),
        P("head", None),
    )
    out_specs = P(("seq", "head"), None)
    return jax.shard_map(body, mesh=mesh, in_specs=in_specs, out_specs=out_specs, check_vma=False)
```

profile of v0, /device:TPU:32, one launch (start us, length us, event | category | flops | bytes accessed | tf_op | source)
XLA Modules:
  0.0 221.3 jit_solution(1955990453732325243)
XLA Ops:
  6.5 0.0 copy-start
  6.5 0.0 all-gather.3.cloned.1.call-start
  6.5 1.0 copy.45
  7.5 10.0 %all_to_all.54 = bf16[32,4,256]{2,0,1:T(8,128)(2,1)} all-to-all(bf16[32,4,256]{2,0,1:T(8,128)(2,1)S(1)} %bitcast.42), channel_id=1, replica_groups=mesh['seq'=64,'head'=4] {'head'}, dimensions={1} | all-to-all | bytes 131072 | tf_op jit(solution)/shard_map/all_to_all | solution.py:15
  17.5 0.0 all-gather.3.cloned.1.call-update
  17.5 0.0 all-gather.5.cloned.1.call-start
  17.6 0.8 copy.44
  18.4 8.7 %all_to_all.55 = bf16[32,4,256]{2,0,1:T(8,128)(2,1)} all-to-all(bf16[32,4,256]{2,0,1:T(8,128)(2,1)S(1)} %bitcast.43), channel_id=1, replica_groups=mesh['seq'=64,'head'=4] {'head'}, dimensions={1} | all-to-all | bytes 131072 | tf_op jit(solution)/shard_map/all_to_all | solution.py:16
  27.1 0.0 all-gather.5.cloned.1.call-update
  27.1 1.5 copy.46
  28.6 3.3 %all-to-all-start = ((bf16[32,4,256]{2,0,1:T(8,128)(2,1)}), bf16[32,4,256]{2,0,1:T(8,128)(2,1)S(1)}, u32[]{:S(2)}, u32[]{:S(2)}) async-start(bf16[32,4,256]{2,0,1:T(8,128)(2,1)} %bitcast.36), calls=%async_computation | async-start | bytes 131072 | tf_op jit(solution)/shard_map/all_to_all | solution.py:14
  31.9 0.0 reduce-scatter.2.cloned.1.call-start
  31.9 0.7 convert_element_type.13
  32.6 0.4 fusion
  33.1 4.4 %all-to-all-done = bf16[32,4,256]{2,0,1:T(8,128)(2,1)S(1)} async-done(((bf16[32,4,256]{2,0,1:T(8,128)(2,1)}), bf16[32,4,256]{2,0,1:T(8,128)(2,1)S(1)}, u32[]{:S(2)}, u32[]{:S(2)}) %all-to-all-start) | async-done | bytes 65568 | tf_op jit(solution)/shard_map/all_to_all | solution.py:14
  37.5 59.0 %all-gather.3.cloned.1.call-done = bf16[8192,256]{1,0:T(8,128)(2,1)} async-done(((bf16[128,256]{1,0:T(8,128)(2,1)}), bf16[8192,256]{1,0:T(8,128)(2,1)}) %all-gather.3.cloned.1.call-update) | async-done | bytes 4194320 | tf_op jit(solution)/shard_map/all_gather | solution.py:25
  96.5 6.4 %copy.28 = bf16[8192,256]{0,1:T(8,128)(2,1)} copy(bf16[8192,256]{1,0:T(8,128)(2,1)} %all-gather.3.cloned.1.call-done) | data formatting | bytes 8388608 | tf_op jit(solution)/shard_map/all_gather | solution.py:25
  102.8 4.0 %select_reduce_fusion = (f32[2,128]{1,0:T(2,128)S(1)}, f32[2,128,8192]{2,1,0:T(8,128)S(1)}) fusion(pred[2,8192]{1,0:T(4,128)(4,1)S(1)} %fusion, bf16[8192,2,128]{0,2,1:T(8,128)(2,1)} %bitcast.37, bf16[128,2,128]{2,1,0:T(2,128)(2,1)S(1)} %reshape.53), kind=kOutput, calls=%fused_computation.4 | convolution fusion | flops 543162112 | bytes 12665856 | tf_op jit(solution)/shard_map/qhd,khd->hqk/dot_general | solution.py:37
  106.8 0.0 copy-start.1
  106.8 3.2 %copy-done.1 = f32[2,128,8192]{2,1,0:T(8,128)} copy-done((f32[2,128,8192]{2,1,0:T(8,128)}, f32[2,128,8192]{2,1,0:T(8,128)S(1)}, u32[]{:S(2)}) %copy-start.1) | copy-done | bytes 8388632
  110.0 1.9 fusion.1
  111.9 63.6 %all-gather.5.cloned.1.call-done = bf16[8192,256]{1,0:T(8,128)(2,1)} async-done(((bf16[128,256]{1,0:T(8,128)(2,1)}), bf16[8192,256]{1,0:T(8,128)(2,1)}) %all-gather.5.cloned.1.call-update) | async-done | bytes 4194320 | tf_op jit(solution)/shard_map/all_gather | solution.py:26
  175.6 6.3 %copy.32 = bf16[8192,256]{0,1:T(8,128)(2,1)} copy(bf16[8192,256]{1,0:T(8,128)(2,1)} %all-gather.5.cloned.1.call-done) | data formatting | bytes 8388608 | tf_op jit(solution)/shard_map/all_gather | solution.py:26
  181.9 6.0 %fusion.14 = bf16[128,2,128]{0,2,1:T(8,128)(2,1)S(1)} fusion(bf16[8192,2,128]{0,2,1:T(8,128)(2,1)} %bitcast.38, f32[2,128,8192]{2,1,0:T(8,128)} %copy-done.1, f32[2,128]{1,0:T(2,128)S(1)} %broadcast_maximum_fusion, pred[2,8192]{1,0:T(4,128)(4,1)S(1)} %fusion, f32[128,2]{0,1:T(2,128)S(1)} %bitcast.48), kind=kOutput, calls=%fused_computation.15 | convolution fusion | flops 543227904 | bytes 12666880 | tf_op jit(solution)/shard_map/hqk,khd->qhd/dot_general | solution.py:44
  187.9 0.0 copy-done
  187.9 1.6 convolution_convert_fusion
  189.5 0.0 reduce-scatter.2.cloned.1.call-update
  189.5 25.3 %reduce-scatter.2.cloned.1.call-done = bf16[32,5120]{1,0:T(8,128)(2,1)} async-done(((bf16[128,5120]{1,0:T(8,128)(2,1)}), bf16[32,5120]{1,0:T(8,128)(2,1)}) %reduce-scatter.2.cloned.1.call-update) | async-done | bytes 327696 | tf_op jit(solution)/shard_map/reduce_scatter | solution.py:52
  (3 shorter events, 0.0 us)
Async XLA Ops:
  6.5 181.3 %copy-start = (bf16[256,5120]{1,0:T(8,128)(2,1)S(1)}, bf16[256,5120]{1,0:T(8,128)(2,1)}, u32[]{:S(2)}) copy-start(bf16[256,5120]{1,0:T(8,128)(2,1)} %param.9) | copy-start | bytes 7864324
  6.5 89.9 %all-gather.3.cloned.1.call-start = ((), (), s32[]{:S(2)}) async-start(), calls=%async_computation.4 | async-start | bytes 4259840 | tf_op jit(solution)/shard_map/all_gather | solution.py:25
  17.5 158.0 %all-gather.5.cloned.1.call-start = ((), (), s32[]{:S(2)}) async-start(), calls=%async_computation.5 | async-start | bytes 4259840 | tf_op jit(solution)/shard_map/all_gather | solution.py:26
  28.6 8.9 %all-to-all-start = ((bf16[32,4,256]{2,0,1:T(8,128)(2,1)}), bf16[32,4,256]{2,0,1:T(8,128)(2,1)S(1)}, u32[]{:S(2)}, u32[]{:S(2)}) async-start(bf16[32,4,256]{2,0,1:T(8,128)(2,1)} %bitcast.36), calls=%async_computation | async-start | bytes 131072 | tf_op jit(solution)/shard_map/all_to_all | solution.py:14
  31.9 182.9 %reduce-scatter.2.cloned.1.call-start = ((), (), s32[]{:S(2)}) async-start(), calls=%async_computation.6 | async-start | bytes 1638400 | tf_op jit(solution)/shard_map/reduce_scatter | solution.py:52
  106.8 3.2 %copy-start.1 = (f32[2,128,8192]{2,1,0:T(8,128)}, f32[2,128,8192]{2,1,0:T(8,128)S(1)}, u32[]{:S(2)}) copy-start(f32[2,128,8192]{2,1,0:T(8,128)S(1)} %get-tuple-element.6) | copy-start | bytes 25165828
Sparse Core Ops, SparseCore 0:
  17.7 78.7 all-gather.2
  99.2 76.2 all-gather.4
  189.6 25.1 reduce-scatter.1
where the time goes:
time: 222 us; the launch traced here: 221 us
  waiting for transfers between devices  152 us (68%)
  local copies, waits for them, and re-layouts  19.2 us (9%)
  blocking collectives  18.6 us (8%)
  between operations  13.2 us (6%)
  matrix products  12 us (5%)
  starting transfers between devices  3.37 us (2%)
  other arithmetic  2.62 us (1%)
    all_gather x1, waiting for transfers between devices, body(): v_piece = lax.all_gather(local_v, 'seq', axis=0, tiled=True)  63.6 us
    all_gather x1, waiting for transfers between devices, body(): k_piece = lax.all_gather(local_k, 'seq', axis=0, tiled=True)  59 us
    reduce_scatter x1, waiting for transfers between devices, body(): lax.psum_scatter(jnp.dot(attn_rows, out_weight, preferred_element_type=jn...  25.3 us
    all_to_all x1, blocking collectives, body(): lax.all_to_all(keys, 'head', split_axis=1, concat_axis=0, tiled=True)  9.98 us
    all_to_all x1, blocking collectives, body(): lax.all_to_all(values, 'head', split_axis=1, concat_axis=0, tiled=True)  8.65 us
    all_gather x1, local copies, waits for them, and re-layouts, body(): k_piece = lax.all_gather(local_k, 'seq', axis=0, tiled=True)  6.36 us
    all_gather x1, local copies, waits for them, and re-layouts, body(): v_piece = lax.all_gather(local_v, 'seq', axis=0, tiled=True)  6.33 us
    dot_general x1, matrix products, body(): jnp.einsum('hqk,khd->qhd', weights.astype(jnp.bfloat16), v_three, preferr...  5.97 us
  transfers between devices with their start and end apart: 4, of which 4 were waited for; matrix products, arithmetic and copies ran while one was open for 7% of the time, Pallas kernels for 0%

commit v1 on v0

v1 whole, which is shorter than its diff:
```python
import functools
import math

import jax
import jax.numpy as jnp
from jax import lax
from jax.experimental import pallas as pl
from jax.experimental.pallas import tpu as pltpu
from jax.sharding import Mesh, PartitionSpec as P

HD = 128
BLK = 128
NX, NH, NL, NC, NY = 4, 4, 2, 2, 4
AXES = ("x", "zh", "zl", "c", "y")
SIZES = (NX, NH, NL, NC, NY)
BF = jnp.bfloat16
F32 = jnp.float32
SCALE2 = math.log2(math.e) / math.sqrt(HD)
NEG = -1e30
BIG = 1e30
VMEM = pl.BlockSpec(memory_space=pltpu.VMEM)
SMEM = pl.BlockSpec(memory_space=pltpu.SMEM)
PARAMS = pltpu.CompilerParams(vmem_limit_bytes=40 * 2**20)


def moved(value, axis, by):
    size = SIZES[AXES.index(axis)]
    return lax.ppermute(value, axis, [(i, (i + by) % size) for i in range(size)])


def prep_kernel(q_ref, k_ref, v_ref, out_ref):
    for c in range(NC):
        for y in range(NY):
            cols = pl.ds((2 * y + c) * HD, HD)
            for i, ref in enumerate((q_ref, k_ref, v_ref)):
                out_ref[c * NY + y, :, i * HD : (i + 1) * HD] = ref[:, cols]


def mid_kernel(where_ref, got_ref, own_ref, other_ref, q_ref, kv_ref):
    y, c = where_ref[4], where_ref[3]
    for part in range(NC):
        for p in range(NY):
            rows = pl.ds((part * NY + p) * 32, 32)
            q_ref[rows, :] = got_ref[part * NY + lax.rem(y + p, NY), :, :HD]
            kv_ref[rows, :] = got_ref[part * NY + p, :, HD:]
    own, other = own_ref[...].astype(F32), other_ref[...].astype(F32)
    first = lax.broadcasted_iota(jnp.int32, own.shape, 0) < 8
    q_ref[256:, :] = jnp.where(first == (c == 0), own, other).astype(BF)


def attend_kernel(where_ref, mask_ref, *refs):
    q_refs, kv_refs, out_refs = refs[:4], refs[4:12], refs[12:16]
    vt_ref, s_ref, p_ref = refs[16:]
    x, zh, zl = where_ref[0], where_ref[1], where_ref[2]
    for i in range(8):
        vt_ref[:, i * 256 : (i + 1) * 256] = kv_refs[i][:, HD:].T
    first = lax.broadcasted_iota(jnp.int32, (1, 256), 1) < BLK
    for j in range(4):
        q = q_refs[j][:256, :]
        opens = []
        top = jnp.full((1, 256), NEG, F32)
        for i in range(8):
            step, flip = i % 4, i // 4
            source = lax.rem(x + NX - step, NX) * 16 + zh * 4 + lax.rem(zl + flip, 2) * 2
            s = lax.dot_general(
                kv_refs[i][:, :HD], q, (((1,), (1,)), ((), ())), preferred_element_type=F32
            )
            s_ref[i * 256 : (i + 1) * 256, :] = s
            for part in range(2):
                open0 = mask_ref[2 * j, source + part]
                open1 = mask_ref[2 * j + 1, source + part]
                is_open = jnp.where(first, open0, open1) > 0
                opens.append(is_open)
                here = jnp.max(s[part * BLK : (part + 1) * BLK], axis=0, keepdims=True)
                top = jnp.maximum(top, jnp.where(is_open, here, NEG))
        top = top * SCALE2
        total = jnp.zeros((1, 256), F32)
        for b in range(16):
            less = jnp.where(opens[b], top, BIG)
            rows = slice(b * BLK, (b + 1) * BLK)
            w = jnp.exp2(s_ref[rows, :] * SCALE2 - less)
            total += jnp.sum(w, axis=0, keepdims=True)
            p_ref[rows, :] = w.astype(BF)
        acc = jnp.dot(vt_ref[...], p_ref[...], preferred_element_type=F32)
        some = total > 0.0
        safe = jnp.where(some, total, 1.0)
        out_refs[j][:HD, :] = (acc / safe).astype(BF)
        lse = jnp.where(some, top + jnp.log2(safe), NEG)
        hi = lse.astype(BF).astype(F32)
        mid = (lse - hi).astype(BF).astype(F32)
        low = lse - hi - mid
        row = lax.broadcasted_iota(jnp.int32, (16, 256), 0)
        out_refs[j][HD:, :] = jnp.where(row == 0, hi, jnp.where(row == 1, mid, low)).astype(BF)


def merge_kernel(where_ref, a_ref, b_ref, c_ref, d_ref, keep_ref, send_ref):
    refs = (a_ref, b_ref, c_ref, d_ref)
    lses = []
    for ref in refs:
        tail = ref[HD:, :].astype(F32)
        lses.append(tail[0:1] + tail[1:2] + tail[2:3])
    top = functools.reduce(jnp.maximum, lses)
    ws = [jnp.exp2(lse - top) for lse in lses]
    inv = 1.0 / sum(ws)
    acc = sum(ref[:HD, :].astype(F32) * (w * inv) for ref, w in zip(refs, ws))
    left, right = acc[:, :BLK].astype(BF), acc[:, BLK:].astype(BF)

    @pl.when(where_ref[3] == 0)
    def _():
        keep_ref[...] = left
        send_ref[...] = right

    @pl.when(where_ref[3] == 1)
    def _():
        keep_ref[...] = right
        send_ref[...] = left


def project_kernel(where_ref, own_ref, other_ref, w_ref, *refs):
    out_refs, lhs_ref = refs[:4], refs[4]

    @pl.when(pl.program_id(0) == 0)
    def _():
        own, other = own_ref[...].T, other_ref[...].T

        @pl.when(where_ref[3] == 0)
        def _():
            lhs_ref[:, :HD] = own
            lhs_ref[:, HD:] = other

        @pl.when(where_ref[3] == 1)
        def _():
            lhs_ref[:, :HD] = other
            lhs_ref[:, HD:] = own

    out = jnp.dot(lhs_ref[...], w_ref[...], preferred_element_type=F32).astype(BF)
    for p in range(NY):
        out_refs[p][...] = out[p * 32 : (p + 1) * 32]


def sum_kernel(a_ref, b_ref, c_ref, d_ref, out_ref):
    out_ref[...] = (
        a_ref[...].astype(F32)
        + b_ref[...].astype(F32)
        + c_ref[...].astype(F32)
        + d_ref[...].astype(F32)
    ).astype(BF)


def shape(*dims, dtype=BF):
    return jax.ShapeDtypeStruct(dims, dtype)


def body(queries, keys, values, block_mask, out_weight):
    where = jnp.stack([lax.axis_index(a) for a in AXES]).astype(jnp.int32)
    core = lax.axis_index("c")
    seen = jnp.pad(block_mask[:, 0, :].astype(BF), ((0, 0), (0, 64)))
    own_mask = jnp.broadcast_to(lax.dynamic_slice_in_dim(seen, core, 1), (16, 128))
    send_mask = jnp.broadcast_to(lax.dynamic_slice_in_dim(seen, 1 - core, 1), (16, 128))
    other_mask = moved(send_mask, "c", 1)

    packed = pl.pallas_call(
        prep_kernel,
        out_shape=shape(8, 32, 384),
        in_specs=[VMEM] * 3,
        out_specs=VMEM,
        compiler_params=PARAMS,
    )(queries, keys, values)
    got = lax.all_to_all(packed, ("c", "y"), split_axis=0, concat_axis=0, tiled=True)
    q, kv = pl.pallas_call(
        mid_kernel,
        out_shape=(shape(272, HD), shape(256, 256)),
        in_specs=[SMEM] + [VMEM] * 3,
        out_specs=(VMEM, VMEM),
        compiler_params=PARAMS,
    )(where, got, own_mask, other_mask)

    pair = moved(kv, "zl", 1)
    kvs = [kv] + [moved(kv, "x", k) for k in (1, 2, 3)]
    qs = [q] + [moved(q, "zh", k) for k in (1, 2, 3)]
    kvs += [pair] + [moved(pair, "x", k) for k in (1, 2, 3)]
    mask = jnp.concatenate([t[r : r + 1, :64] for t in qs for r in (256, 264)]).astype(jnp.int32)

    parts = pl.pallas_call(
        attend_kernel,
        out_shape=tuple(shape(144, 256) for _ in range(4)),
        in_specs=[SMEM] * 2 + [VMEM] * 12,
        out_specs=(VMEM,) * 4,
        scratch_shapes=[
            pltpu.VMEM((HD, 2048), BF),
            pltpu.VMEM((2048, 256), F32),
            pltpu.VMEM((2048, 256), BF),
        ],
        compiler_params=PARAMS,
        cost_estimate=pl.CostEstimate(
            flops=2 * 2 * 1024 * 2048 * HD, bytes_accessed=2**21, transcendentals=2**21
        ),
    )(where, mask, *qs, *kvs)
    back = [parts[0]] + [moved(parts[k], "zh", -k) for k in (1, 2, 3)]

    keep, send = pl.pallas_call(
        merge_kernel,
        out_shape=(shape(HD, BLK), shape(HD, BLK)),
        in_specs=[SMEM] + [VMEM] * 4,
        out_specs=(VMEM, VMEM),
        compiler_params=PARAMS,
    )(where, *back)
    other = moved(send, "c", 1)

    cols = 1280
    width = out_weight.shape[1]
    pieces = pl.pallas_call(
        project_kernel,
        out_shape=tuple(shape(32, width) for _ in range(4)),
        grid=(width // cols,),
        in_specs=[
            SMEM,
            pl.BlockSpec((HD, BLK), lambda i: (0, 0)),
            pl.BlockSpec((HD, BLK), lambda i: (0, 0)),
            pl.BlockSpec((2 * HD, cols), lambda i: (0, i)),
        ],
        out_specs=tuple(pl.BlockSpec((32, cols), lambda i: (0, i)) for _ in range(4)),
        scratch_shapes=[pltpu.VMEM((BLK, 2 * HD), BF)],
        compiler_params=PARAMS,
        cost_estimate=pl.CostEstimate(
            flops=2 * 128 * 256 * width, bytes_accessed=2**22, transcendentals=0
        ),
    )(where, keep, other, out_weight)
    arrived = [moved(pieces[k], "y", k) for k in (2, 1, 3)]
    return pl.pallas_call(
        sum_kernel,
        out_shape=shape(32, width),
        in_specs=[VMEM] * 4,
        out_specs=VMEM,
        compiler_params=PARAMS,
    )(pieces[0], *arrived)


def solution(mesh):
    grid = Mesh(mesh.devices.reshape(SIZES), AXES)
    rows = P(AXES, None)
    in_specs = (rows, rows, rows, P("y", AXES[:4], None), P("y", None))
    return jax.shard_map(body, mesh=grid, in_specs=in_specs, out_specs=rows, check_vma=False)
```

time: 222 us -> 86.6 us (0.39)
  waiting for transfers between devices: 152 us -> 35.9 us
  starting transfers between devices: 3.37 us -> 36.9 us
  blocking collectives: 18.6 us -> 0 us
  local copies, waits for them, and re-layouts: 19.2 us -> 2.69 us
  between operations: 13.2 us -> 0.08 us
  matrix products: 12 us -> 0 us
  Pallas kernels: 0 us -> 9.75 us
    all_gather x2 -> x0, waiting for transfers between devices: 123 us -> none  [the longest x1 63.6 us: body(): v_piece = lax.all_gather(local_v, 'seq', axis=0, tiled=True)]
    ppermute x0 -> x18, starting transfers between devices: none -> 32.3 us  [moved(): lax.ppermute(value, axis, [(i, (i + by) % size) for i in range(size)])]
    ppermute x0 -> x18, waiting for transfers between devices: none -> 31.7 us  [moved(): lax.ppermute(value, axis, [(i, (i + by) % size) for i in range(size)])]
    reduce_scatter x1 -> x0, waiting for transfers between devices: 25.3 us -> none  [body(): lax.psum_scatter(jnp.dot(attn_rows, out_weight, preferred_element_type=jn...]
    all_to_all x2 -> x0, blocking collectives: 18.6 us -> none  [the longest x1 9.98 us: body(): lax.all_to_all(keys, 'head', split_axis=1, concat_axis=0, tiled=True)]
    all_gather x2 -> x0, local copies, waits for them, and re-layouts: 12.7 us -> none  [the longest x1 6.36 us: body(): k_piece = lax.all_gather(local_k, 'seq', axis=0, tiled=True)]
    dot_general x4 -> x0, matrix products: 12 us -> none  [the longest x1 5.97 us: body(): jnp.einsum('hqk,khd->qhd', weights.astype(jnp.bfloat16), v_three, preferr...]
    pallas_call x0 -> x6, Pallas kernels: none -> 9.75 us  [the longest x1 4.98 us: body(): pl.pallas_call(attend_kernel, out_shape=tuple((shape(144, 256) for _ in r...]
  transfers between devices with their start and end apart: 4 -> 19, of which waited for: 4 -> 13; matrix products, arithmetic and copies ran while one was open for 7% -> 1% of each run, Pallas kernels for 0% -> 0%
where the time goes in v1:
time: 86.6 us; the launch traced here: 85.9 us
  starting transfers between devices  36.9 us (43%)
  waiting for transfers between devices  35.9 us (41%)
  Pallas kernels  9.75 us (11%)
  local copies, waits for them, and re-layouts  2.69 us (3%)
    ppermute x18, starting transfers between devices, moved(): lax.ppermute(value, axis, [(i, (i + by) % size) for i in range(size)])  32.3 us
    ppermute x18, waiting for transfers between devices, moved(): lax.ppermute(value, axis, [(i, (i + by) % size) for i in range(size)])  31.7 us
    pallas_call x1, Pallas kernels, body(): pl.pallas_call(attend_kernel, out_shape=tuple((shape(144, 256) for _ in r...  4.98 us
    all_to_all x1, starting transfers between devices, body(): lax.all_to_all(packed, ('c', 'y'), split_axis=0, concat_axis=0, tiled=True)  4.6 us
    all_to_all x1, waiting for transfers between devices, body(): lax.all_to_all(packed, ('c', 'y'), split_axis=0, concat_axis=0, tiled=True)  4.15 us
    unnamed x9, local copies, waits for them, and re-layouts  2.53 us
    pallas_call x1, Pallas kernels, body(): pl.pallas_call(project_kernel, out_shape=tuple((shape(32, width) for _ in...  1.98 us
  transfers between devices with their start and end apart: 19, of which 13 were waited for; matrix products, arithmetic and copies ran while one was open for 1% of the time, Pallas kernels for 0%

profile of v1, /device:TPU:32, one launch (start us, length us, event | category | flops | bytes accessed | tf_op | source)
XLA Modules:
  0.0 85.9 jit_solution(13131424882836744927)
XLA Ops:
  0.0 0.8 copy-done.1
  0.8 0.8 copy-done.2
  1.7 0.8 copy-done.3
  3.2 4.6 %all-to-all-start = ((bf16[8,32,384]{2,1,0:T(8,128)(2,1)}), bf16[8,32,384]{2,1,0:T(8,128)(2,1)S(1)}, u32[]{:S(2)}, u32[]{:S(2)}) async-start(bf16[8,32,384]{2,1,0:T(8,128)(2,1)} %shard_map.55), calls=%async_computation | async-start | bytes 393216 | tf_op jit(solution)/shard_map/all_to_all | solution.py:169
  10.0 4.2 %all-to-all-done.got_ref = bf16[8,32,384]{2,1,0:T(8,128)(2,1)S(1)} async-done(((bf16[8,32,384]{2,1,0:T(8,128)(2,1)}), bf16[8,32,384]{2,1,0:T(8,128)(2,1)S(1)}, u32[]{:S(2)}, u32[]{:S(2)}) %all-to-all-start) | async-done | bytes 196640 | tf_op jit(solution)/shard_map/all_to_all | solution.py:169
  14.7 5.5 %collective-permute-start.3 = (bf16[272,128]{1,0:T(8,128)(2,1)S(1)}, bf16[272,128]{1,0:T(8,128)(2,1)S(1)}, u32[]{:S(2)}, u32[]{:S(2)}) collective-permute-start(bf16[272,128]{1,0:T(8,128)(2,1)S(1)} %get-tuple-element.17.refs_0_), channel_id=1, source_target_pairs={{0,48},{16,0},{32,16},{48,32},{1,49},{17,1},{33,17},{49,33},{2,50}... | collective-permute-start | bytes 208904 | tf_op jit(solution)/shard_map/ppermute | solution.py:28
  20.2 1.4 %collective-permute-start.2 = (bf16[272,128]{1,0:T(8,128)(2,1)S(1)}, bf16[272,128]{1,0:T(8,128)(2,1)S(1)}, u32[]{:S(2)}, u32[]{:S(2)}) collective-permute-start(bf16[272,128]{1,0:T(8,128)(2,1)S(1)} %get-tuple-element.17.refs_0_), channel_id=1, source_target_pairs={{0,32},{16,48},{32,0},{48,16},{1,33},{17,49},{33,1},{49,17},{2,34}... | collective-permute-start | bytes 208904 | tf_op jit(solution)/shard_map/ppermute | solution.py:28
  21.6 2.4 %collective-permute-start.1 = (bf16[272,128]{1,0:T(8,128)(2,1)S(1)}, bf16[272,128]{1,0:T(8,128)(2,1)S(1)}, u32[]{:S(2)}, u32[]{:S(2)}) collective-permute-start(bf16[272,128]{1,0:T(8,128)(2,1)S(1)} %get-tuple-element.17.refs_0_), channel_id=1, source_target_pairs={{0,16},{16,32},{32,48},{48,0},{1,17},{17,33},{33,49},{49,1},{2,18}... | collective-permute-start | bytes 208904 | tf_op jit(solution)/shard_map/ppermute | solution.py:28
  24.0 1.0 %collective-permute-start.7 = (bf16[256,256]{1,0:T(8,128)(2,1)S(1)}, bf16[256,256]{1,0:T(8,128)(2,1)S(1)}, u32[]{:S(2)}, u32[]{:S(2)}) collective-permute-start(bf16[256,256]{1,0:T(8,128)(2,1)S(1)} %get-tuple-element.18.refs_4_), channel_id=1, source_target_pairs={{0,8},{8,0},{1,9},{9,1},{2,10},{10,2},{3,11},{11,3},{4,12},{12,4},... | collective-permute-start | bytes 393224 | tf_op jit(solution)/shard_map/ppermute | solution.py:28
  25.0 2.8 %collective-permute-start.6 = (bf16[256,256]{1,0:T(8,128)(2,1)S(1)}, bf16[256,256]{1,0:T(8,128)(2,1)S(1)}, u32[]{:S(2)}, u32[]{:S(2)}) collective-permute-start(bf16[256,256]{1,0:T(8,128)(2,1)S(1)} %get-tuple-element.18.refs_4_), channel_id=1, source_target_pairs={{0,192},{64,0},{128,64},{192,128},{1,193},{65,1},{129,65},{193,129... | collective-permute-start | bytes 393224 | tf_op jit(solution)/shard_map/ppermute | solution.py:28
  27.8 0.8 collective-permute-start.5
  28.6 1.2 %collective-permute-done.2.refs_2_ = bf16[272,128]{1,0:T(8,128)(2,1)S(1)} collective-permute-done((bf16[272,128]{1,0:T(8,128)(2,1)S(1)}, bf16[272,128]{1,0:T(8,128)(2,1)S(1)}, u32[]{:S(2)}, u32[]{:S(2)}) %collective-permute-start.2) | collective-permute-done | bytes 69664 | tf_op jit(solution)/shard_map/ppermute | solution.py:28
  29.7 1.5 %collective-permute-start.4 = (bf16[256,256]{1,0:T(8,128)(2,1)S(1)}, bf16[256,256]{1,0:T(8,128)(2,1)}, u32[]{:S(2)}, u32[]{:S(2)}) collective-permute-start(bf16[256,256]{1,0:T(8,128)(2,1)S(1)} %get-tuple-element.18.refs_4_), channel_id=1, source_target_pairs={{0,64},{64,128},{128,192},{192,0},{1,65},{65,129},{129,193},{193,1... | collective-permute-start | bytes 393224 | tf_op jit(solution)/shard_map/ppermute | solution.py:28
  31.5 2.8 %collective-permute-start.10 = (bf16[256,256]{1,0:T(8,128)(2,1)S(1)}, bf16[256,256]{1,0:T(8,128)(2,1)}, u32[]{:S(2)}, u32[]{:S(2)}) collective-permute-start(bf16[256,256]{1,0:T(8,128)(2,1)S(1)} %collective-permute-done.7.refs_8_), channel_id=1, source_target_pairs={{0,192},{64,0},{128,64},{192,128},{1,193},{65,1},{129,65},{193,129... | collective-permute-start | bytes 393224 | tf_op jit(solution)/shard_map/ppermute | solution.py:28
  34.3 0.8 collective-permute-start.9
  35.1 0.9 %collective-permute-start.8 = (bf16[256,256]{1,0:T(8,128)(2,1)S(1)}, bf16[256,256]{1,0:T(8,128)(2,1)}, u32[]{:S(2)}, u32[]{:S(2)}) collective-permute-start(bf16[256,256]{1,0:T(8,128)(2,1)S(1)} %collective-permute-done.7.refs_8_), channel_id=1, source_target_pairs={{0,64},{64,128},{128,192},{192,0},{1,65},{65,129},{129,193},{193,1... | collective-permute-start | bytes 393224 | tf_op jit(solution)/shard_map/ppermute | solution.py:28
  36.0 0.9 collective-permute-done.4.refs_5_
  36.9 2.8 %collective-permute-done.10.refs_11_ = bf16[256,256]{1,0:T(8,128)(2,1)} collective-permute-done((bf16[256,256]{1,0:T(8,128)(2,1)S(1)}, bf16[256,256]{1,0:T(8,128)(2,1)}, u32[]{:S(2)}, u32[]{:S(2)}) %collective-permute-start.10) | collective-permute-done | bytes 131104 | tf_op jit(solution)/shard_map/ppermute | solution.py:28
  39.7 2.4 %collective-permute-done.9.refs_10_ = bf16[256,256]{1,0:T(8,128)(2,1)} collective-permute-done((bf16[256,256]{1,0:T(8,128)(2,1)S(1)}, bf16[256,256]{1,0:T(8,128)(2,1)}, u32[]{:S(2)}, u32[]{:S(2)}) %collective-permute-start.9) | collective-permute-done | bytes 131104 | tf_op jit(solution)/shard_map/ppermute | solution.py:28
  42.1 1.4 %collective-permute-done.8.refs_9_ = bf16[256,256]{1,0:T(8,128)(2,1)} collective-permute-done((bf16[256,256]{1,0:T(8,128)(2,1)S(1)}, bf16[256,256]{1,0:T(8,128)(2,1)}, u32[]{:S(2)}, u32[]{:S(2)}) %collective-permute-start.8) | collective-permute-done | bytes 131104 | tf_op jit(solution)/shard_map/ppermute | solution.py:28
  43.5 5.0 %shard_map.57 = (bf16[144,256]{1,0:T(8,128)(2,1)S(1)}, bf16[144,256]{1,0:T(8,128)(2,1)S(1)}, bf16[144,256]{1,0:T(8,128)(2,1)S(1)}, bf16[144,256]{1,0:T(8,128)(2,1)S(1)}) custom-call(s32[5]{0:T(128)S(1)} %stack.23.where_ref, s32[8,64]{1,0:T(8,128)S(1)} %convert_element_type.13.mask_ref, bf16[272,128]{1,0:T(8,128)(2,1)S(1)} %get-tuple-element.17.refs_0_, ...), custom_call_target="tpu_custom_call" | custom-call | flops 1073741824 | bytes 2097152 | tf_op jit(solution)/shard_map/pallas_call | solution.py:184
  48.5 2.7 %collective-permute-start.11 = (bf16[144,256]{1,0:T(8,128)(2,1)S(1)}, bf16[144,256]{1,0:T(8,128)(2,1)S(1)}, u32[]{:S(2)}, u32[]{:S(2)}) collective-permute-start(bf16[144,256]{1,0:T(8,128)(2,1)S(1)} %get-tuple-element.20), channel_id=1, source_target_pairs={{0,48},{16,0},{32,16},{48,32},{1,49},{17,1},{33,17},{49,33},{2,50}... | collective-permute-start | bytes 221192 | tf_op jit(solution)/shard_map/ppermute | solution.py:28
  51.2 4.0 %collective-permute-start.12 = (bf16[144,256]{1,0:T(8,128)(2,1)S(1)}, bf16[144,256]{1,0:T(8,128)(2,1)S(1)}, u32[]{:S(2)}, u32[]{:S(2)}) collective-permute-start(bf16[144,256]{1,0:T(8,128)(2,1)S(1)} %get-tuple-element.21), channel_id=1, source_target_pairs={{0,32},{16,48},{32,0},{48,16},{1,33},{17,49},{33,1},{49,17},{2,34}... | collective-permute-start | bytes 221192 | tf_op jit(solution)/shard_map/ppermute | solution.py:28
  56.0 4.7 %collective-permute-done.12.c_ref = bf16[144,256]{1,0:T(8,128)(2,1)S(1)} collective-permute-done((bf16[144,256]{1,0:T(8,128)(2,1)S(1)}, bf16[144,256]{1,0:T(8,128)(2,1)S(1)}, u32[]{:S(2)}, u32[]{:S(2)}) %collective-permute-start.12) | collective-permute-done | bytes 73760 | tf_op jit(solution)/shard_map/ppermute | solution.py:28
  60.7 2.0 %collective-permute-done.13.d_ref = bf16[144,256]{1,0:T(8,128)(2,1)S(1)} collective-permute-done((bf16[144,256]{1,0:T(8,128)(2,1)S(1)}, bf16[144,256]{1,0:T(8,128)(2,1)S(1)}, u32[]{:S(2)}, u32[]{:S(2)}) %collective-permute-start.13) | collective-permute-done | bytes 73760 | tf_op jit(solution)/shard_map/ppermute | solution.py:28
  63.4 1.2 %collective-permute-done.14.other_ref = bf16[128,128]{1,0:T(8,128)(2,1)S(1)} collective-permute-done((bf16[128,128]{1,0:T(8,128)(2,1)S(1)}, bf16[128,128]{1,0:T(8,128)(2,1)S(1)}, u32[]{:S(2)}, u32[]{:S(2)}) %collective-permute-start.14) | collective-permute-done | bytes 32800 | tf_op jit(solution)/shard_map/ppermute | solution.py:28
  64.6 2.0 %shard_map.59 = (bf16[32,5120]{1,0:T(8,128)(2,1)S(1)}, bf16[32,5120]{1,0:T(8,128)(2,1)S(1)}, bf16[32,5120]{1,0:T(8,128)(2,1)S(1)}, bf16[32,5120]{1,0:T(8,128)(2,1)S(1)}) custom-call(s32[5]{0:T(128)S(1)} %stack.23.where_ref, bf16[128,128]{1,0:T(8,128)(2,1)S(1)} %get-tuple-element.23.own_ref, bf16[128,128]{1,0:T(8,128)(2,1)S(1)} %collective-permute-done.14.other_ref, ...), custom_call_target="tpu_custom_call" | custom-call | flops 335544320 | bytes 4194304 | tf_op jit(solution)/shard_map/pallas_call | solution.py:212
  66.6 1.0 %collective-permute-start.15 = (bf16[32,5120]{1,0:T(8,128)(2,1)S(1)}, bf16[32,5120]{1,0:T(8,128)(2,1)S(1)}, u32[]{:S(2)}, u32[]{:S(2)}) collective-permute-start(bf16[32,5120]{1,0:T(8,128)(2,1)S(1)} %get-tuple-element.26), channel_id=1, source_target_pairs={{0,2},{1,3},{2,0},{3,1},{4,6},{5,7},{6,4},{7,5},{8,10},{9,11},{10,... | collective-permute-start | bytes 983048 | tf_op jit(solution)/shard_map/ppermute | solution.py:28
  67.9 3.0 %collective-permute-start.17 = (bf16[32,5120]{1,0:T(8,128)(2,1)S(1)}, bf16[32,5120]{1,0:T(8,128)(2,1)S(1)}, u32[]{:S(2)}, u32[]{:S(2)}) collective-permute-start(bf16[32,5120]{1,0:T(8,128)(2,1)S(1)} %get-tuple-element.28), channel_id=1, source_target_pairs={{0,3},{1,0},{2,1},{3,2},{4,7},{5,4},{6,5},{7,6},{8,11},{9,8},{10,9... | collective-permute-start | bytes 983048 | tf_op jit(solution)/shard_map/ppermute | solution.py:28
  70.9 7.9 %collective-permute-done.15.b_ref = bf16[32,5120]{1,0:T(8,128)(2,1)S(1)} collective-permute-done((bf16[32,5120]{1,0:T(8,128)(2,1)S(1)}, bf16[32,5120]{1,0:T(8,128)(2,1)S(1)}, u32[]{:S(2)}, u32[]{:S(2)}) %collective-permute-start.15) | collective-permute-done | bytes 327712 | tf_op jit(solution)/shard_map/ppermute | solution.py:28
  78.8 6.2 %collective-permute-done.16.c_ref = bf16[32,5120]{1,0:T(8,128)(2,1)S(1)} collective-permute-done((bf16[32,5120]{1,0:T(8,128)(2,1)S(1)}, bf16[32,5120]{1,0:T(8,128)(2,1)S(1)}, u32[]{:S(2)}, u32[]{:S(2)}) %collective-permute-start.16) | collective-permute-done | bytes 327712 | tf_op jit(solution)/shard_map/ppermute | solution.py:28
  85.0 0.9 %shard_map.60 = bf16[32,5120]{1,0:T(8,128)(2,1)} custom-call(bf16[32,5120]{1,0:T(8,128)(2,1)S(1)} %get-tuple-element.25.a_ref, bf16[32,5120]{1,0:T(8,128)(2,1)S(1)} %collective-permute-done.15.b_ref, bf16[32,5120]{1,0:T(8,128)(2,1)S(1)} %collective-permute-done.16.c_ref, bf16[32,5120]{1,0:T(8,128)(2,1)S(1)} %collective-permute-done.17.d_ref), custom_call_target="tpu_custom_call" | custom-call | tf_op jit(solution)/shard_map/pallas_call | solution.py:230
  (32 shorter events, 5.5 us)
Async XLA Ops:
  0.0 0.8 copy-start.1
  0.8 0.8 copy-start.2
  1.7 0.8 copy-start.3
  2.5 62.1 %copy-start = (bf16[256,5120]{1,0:T(8,128)(2,1)S(1)}, bf16[256,5120]{1,0:T(8,128)(2,1)}, u32[]{:S(2)}) copy-start(bf16[256,5120]{1,0:T(8,128)(2,1)} %w_ref.1) | copy-start | bytes 7864324
  3.2 10.9 %all-to-all-start = ((bf16[8,32,384]{2,1,0:T(8,128)(2,1)}), bf16[8,32,384]{2,1,0:T(8,128)(2,1)S(1)}, u32[]{:S(2)}, u32[]{:S(2)}) async-start(bf16[8,32,384]{2,1,0:T(8,128)(2,1)} %shard_map.55), calls=%async_computation | async-start | bytes 393216 | tf_op jit(solution)/shard_map/all_to_all | solution.py:169
  8.6 1.4 %collective-permute-start = (bf16[16,128]{1,0:T(8,128)(2,1)S(1)}, bf16[16,128]{1,0:T(8,128)(2,1)S(1)}, u32[]{:S(2)}, u32[]{:S(2)}) collective-permute-start(bf16[16,128]{1,0:T(8,128)(2,1)S(1)} %broadcast_in_dim.17), channel_id=1, source_target_pairs={{0,4},{4,0},{1,5},{5,1},{2,6},{6,2},{3,7},{7,3},{8,12},{12,8},{9,1... | collective-permute-start | bytes 12296 | tf_op jit(solution)/shard_map/ppermute | solution.py:28
  14.7 13.1 %collective-permute-start.3 = (bf16[272,128]{1,0:T(8,128)(2,1)S(1)}, bf16[272,128]{1,0:T(8,128)(2,1)S(1)}, u32[]{:S(2)}, u32[]{:S(2)}) collective-permute-start(bf16[272,128]{1,0:T(8,128)(2,1)S(1)} %get-tuple-element.17.refs_0_), channel_id=1, source_target_pairs={{0,48},{16,0},{32,16},{48,32},{1,49},{17,1},{33,17},{49,33},{2,50}... | collective-permute-start | bytes 208904 | tf_op jit(solution)/shard_map/ppermute | solution.py:28
  20.2 9.6 %collective-permute-start.2 = (bf16[272,128]{1,0:T(8,128)(2,1)S(1)}, bf16[272,128]{1,0:T(8,128)(2,1)S(1)}, u32[]{:S(2)}, u32[]{:S(2)}) collective-permute-start(bf16[272,128]{1,0:T(8,128)(2,1)S(1)} %get-tuple-element.17.refs_0_), channel_id=1, source_target_pairs={{0,32},{16,48},{32,0},{48,16},{1,33},{17,49},{33,1},{49,17},{2,34}... | collective-permute-start | bytes 208904 | tf_op jit(solution)/shard_map/ppermute | solution.py:28
  21.6 12.7 %collective-permute-start.1 = (bf16[272,128]{1,0:T(8,128)(2,1)S(1)}, bf16[272,128]{1,0:T(8,128)(2,1)S(1)}, u32[]{:S(2)}, u32[]{:S(2)}) collective-permute-start(bf16[272,128]{1,0:T(8,128)(2,1)S(1)} %get-tuple-element.17.refs_0_), channel_id=1, source_target_pairs={{0,16},{16,32},{32,48},{48,0},{1,17},{17,33},{33,49},{49,1},{2,18}... | collective-permute-start | bytes 208904 | tf_op jit(solution)/shard_map/ppermute | solution.py:28
  24.0 7.5 %collective-permute-start.7 = (bf16[256,256]{1,0:T(8,128)(2,1)S(1)}, bf16[256,256]{1,0:T(8,128)(2,1)S(1)}, u32[]{:S(2)}, u32[]{:S(2)}) collective-permute-start(bf16[256,256]{1,0:T(8,128)(2,1)S(1)} %get-tuple-element.18.refs_4_), channel_id=1, source_target_pairs={{0,8},{8,0},{1,9},{9,1},{2,10},{10,2},{3,11},{11,3},{4,12},{12,4},... | collective-permute-start | bytes 393224 | tf_op jit(solution)/shard_map/ppermute | solution.py:28
  25.0 10.1 %collective-permute-start.6 = (bf16[256,256]{1,0:T(8,128)(2,1)S(1)}, bf16[256,256]{1,0:T(8,128)(2,1)S(1)}, u32[]{:S(2)}, u32[]{:S(2)}) collective-permute-start(bf16[256,256]{1,0:T(8,128)(2,1)S(1)} %get-tuple-element.18.refs_4_), channel_id=1, source_target_pairs={{0,192},{64,0},{128,64},{192,128},{1,193},{65,1},{129,65},{193,129... | collective-permute-start | bytes 393224 | tf_op jit(solution)/shard_map/ppermute | solution.py:28
  27.8 8.3 %collective-permute-start.5 = (bf16[256,256]{1,0:T(8,128)(2,1)S(1)}, bf16[256,256]{1,0:T(8,128)(2,1)S(1)}, u32[]{:S(2)}, u32[]{:S(2)}) collective-permute-start(bf16[256,256]{1,0:T(8,128)(2,1)S(1)} %get-tuple-element.18.refs_4_), channel_id=1, source_target_pairs={{0,128},{64,192},{128,0},{192,64},{1,129},{65,193},{129,1},{193,65... | collective-permute-start | bytes 393224 | tf_op jit(solution)/shard_map/ppermute | solution.py:28
  29.7 7.2 %collective-permute-start.4 = (bf16[256,256]{1,0:T(8,128)(2,1)S(1)}, bf16[256,256]{1,0:T(8,128)(2,1)}, u32[]{:S(2)}, u32[]{:S(2)}) collective-permute-start(bf16[256,256]{1,0:T(8,128)(2,1)S(1)} %get-tuple-element.18.refs_4_), channel_id=1, source_target_pairs={{0,64},{64,128},{128,192},{192,0},{1,65},{65,129},{129,193},{193,1... | collective-permute-start | bytes 393224 | tf_op jit(solution)/shard_map/ppermute | solution.py:28
  31.5 8.1 %collective-permute-start.10 = (bf16[256,256]{1,0:T(8,128)(2,1)S(1)}, bf16[256,256]{1,0:T(8,128)(2,1)}, u32[]{:S(2)}, u32[]{:S(2)}) collective-permute-start(bf16[256,256]{1,0:T(8,128)(2,1)S(1)} %collective-permute-done.7.refs_8_), channel_id=1, source_target_pairs={{0,192},{64,0},{128,64},{192,128},{1,193},{65,1},{129,65},{193,129... | collective-permute-start | bytes 393224 | tf_op jit(solution)/shard_map/ppermute | solution.py:28
  34.3 7.8 %collective-permute-start.9 = (bf16[256,256]{1,0:T(8,128)(2,1)S(1)}, bf16[256,256]{1,0:T(8,128)(2,1)}, u32[]{:S(2)}, u32[]{:S(2)}) collective-permute-start(bf16[256,256]{1,0:T(8,128)(2,1)S(1)} %collective-permute-done.7.refs_8_), channel_id=1, source_target_pairs={{0,128},{64,192},{128,0},{192,64},{1,129},{65,193},{129,1},{193,65... | collective-permute-start | bytes 393224 | tf_op jit(solution)/shard_map/ppermute | solution.py:28
  35.1 8.4 %collective-permute-start.8 = (bf16[256,256]{1,0:T(8,128)(2,1)S(1)}, bf16[256,256]{1,0:T(8,128)(2,1)}, u32[]{:S(2)}, u32[]{:S(2)}) collective-permute-start(bf16[256,256]{1,0:T(8,128)(2,1)S(1)} %collective-permute-done.7.refs_8_), channel_id=1, source_target_pairs={{0,64},{64,128},{128,192},{192,0},{1,65},{65,129},{129,193},{193,1... | collective-permute-start | bytes 393224 | tf_op jit(solution)/shard_map/ppermute | solution.py:28
  48.5 7.5 %collective-permute-start.11 = (bf16[144,256]{1,0:T(8,128)(2,1)S(1)}, bf16[144,256]{1,0:T(8,128)(2,1)S(1)}, u32[]{:S(2)}, u32[]{:S(2)}) collective-permute-start(bf16[144,256]{1,0:T(8,128)(2,1)S(1)} %get-tuple-element.20), channel_id=1, source_target_pairs={{0,48},{16,0},{32,16},{48,32},{1,49},{17,1},{33,17},{49,33},{2,50}... | collective-permute-start | bytes 221192 | tf_op jit(solution)/shard_map/ppermute | solution.py:28
  51.2 9.5 %collective-permute-start.12 = (bf16[144,256]{1,0:T(8,128)(2,1)S(1)}, bf16[144,256]{1,0:T(8,128)(2,1)S(1)}, u32[]{:S(2)}, u32[]{:S(2)}) collective-permute-start(bf16[144,256]{1,0:T(8,128)(2,1)S(1)} %get-tuple-element.21), channel_id=1, source_target_pairs={{0,32},{16,48},{32,0},{48,16},{1,33},{17,49},{33,1},{49,17},{2,34}... | collective-permute-start | bytes 221192 | tf_op jit(solution)/shard_map/ppermute | solution.py:28
  55.2 7.5 %collective-permute-start.13 = (bf16[144,256]{1,0:T(8,128)(2,1)S(1)}, bf16[144,256]{1,0:T(8,128)(2,1)S(1)}, u32[]{:S(2)}, u32[]{:S(2)}) collective-permute-start(bf16[144,256]{1,0:T(8,128)(2,1)S(1)} %get-tuple-element.22), channel_id=1, source_target_pairs={{0,16},{16,32},{32,48},{48,0},{1,17},{17,33},{33,49},{49,1},{2,18}... | collective-permute-start | bytes 221192 | tf_op jit(solution)/shard_map/ppermute | solution.py:28
  63.3 1.3 %collective-permute-start.14 = (bf16[128,128]{1,0:T(8,128)(2,1)S(1)}, bf16[128,128]{1,0:T(8,128)(2,1)S(1)}, u32[]{:S(2)}, u32[]{:S(2)}) collective-permute-start(bf16[128,128]{1,0:T(8,128)(2,1)S(1)} %get-tuple-element.24), channel_id=1, source_target_pairs={{0,4},{4,0},{1,5},{5,1},{2,6},{6,2},{3,7},{7,3},{8,12},{12,8},{9,1... | collective-permute-start | bytes 98312 | tf_op jit(solution)/shard_map/ppermute | solution.py:28
  66.6 12.2 %collective-permute-start.15 = (bf16[32,5120]{1,0:T(8,128)(2,1)S(1)}, bf16[32,5120]{1,0:T(8,128)(2,1)S(1)}, u32[]{:S(2)}, u32[]{:S(2)}) collective-permute-start(bf16[32,5120]{1,0:T(8,128)(2,1)S(1)} %get-tuple-element.26), channel_id=1, source_target_pairs={{0,2},{1,3},{2,0},{3,1},{4,6},{5,7},{6,4},{7,5},{8,10},{9,11},{10,... | collective-permute-start | bytes 983048 | tf_op jit(solution)/shard_map/ppermute | solution.py:28
  67.6 17.4 %collective-permute-start.16 = (bf16[32,5120]{1,0:T(8,128)(2,1)S(1)}, bf16[32,5120]{1,0:T(8,128)(2,1)S(1)}, u32[]{:S(2)}, u32[]{:S(2)}) collective-permute-start(bf16[32,5120]{1,0:T(8,128)(2,1)S(1)} %get-tuple-element.27), channel_id=1, source_target_pairs={{0,1},{1,2},{2,3},{3,0},{4,5},{5,6},{6,7},{7,4},{8,9},{9,10},{10,1... | collective-permute-start | bytes 983048 | tf_op jit(solution)/shard_map/ppermute | solution.py:28
  67.9 17.1 %collective-permute-start.17 = (bf16[32,5120]{1,0:T(8,128)(2,1)S(1)}, bf16[32,5120]{1,0:T(8,128)(2,1)S(1)}, u32[]{:S(2)}, u32[]{:S(2)}) collective-permute-start(bf16[32,5120]{1,0:T(8,128)(2,1)S(1)} %get-tuple-element.28), channel_id=1, source_target_pairs={{0,3},{1,0},{2,1},{3,2},{4,7},{5,4},{6,5},{7,6},{8,11},{9,8},{10,9... | collective-permute-start | bytes 983048 | tf_op jit(solution)/shard_map/ppermute | solution.py:28

commit v2 on v1

--- a/solution.py
+++ b/solution.py
@@ -28,12 +28,28 @@
     return lax.ppermute(value, axis, [(i, (i + by) % size) for i in range(size)])
 
 
-def prep_kernel(q_ref, k_ref, v_ref, out_ref):
-    for c in range(NC):
-        for y in range(NY):
-            cols = pl.ds((2 * y + c) * HD, HD)
-            for i, ref in enumerate((q_ref, k_ref, v_ref)):
-                out_ref[c * NY + y, :, i * HD : (i + 1) * HD] = ref[:, cols]
+def moved_by_core(value, axis):
+    size = SIZES[AXES.index(axis)]
+    pairs = []
+    for i in range(size):
+        pairs.append((i * 2, (i + 1) % size * 2))
+        pairs.append((i * 2 + 1, (i - 1) % size * 2 + 1))
+    return lax.ppermute(value, (axis, "c"), pairs)
+
+
+def prep_kernel(q_ref, k_ref, v_ref, out_ref, held_ref, sem):
+    copies = [
+        pltpu.make_async_copy(ref, held_ref.at[i], sem.at[i])
+        for i, ref in enumerate((q_ref, k_ref, v_ref))
+    ]
+    for copy in copies:
+        copy.start()
+    for i, copy in enumerate(copies):
+        copy.wait()
+        for c in range(NC):
+            for y in range(NY):
+                cols = slice((2 * y + c) * HD, (2 * y + c + 1) * HD)
+                out_ref[c * NY + y, :, i * HD : (i + 1) * HD] = held_ref[i, :, cols]
 
 
 def mid_kernel(where_ref, got_ref, own_ref, other_ref, q_ref, kv_ref):
@@ -48,15 +64,23 @@
     q_ref[256:, :] = jnp.where(first == (c == 0), own, other).astype(BF)
 
 
-def attend_kernel(where_ref, mask_ref, *refs):
-    q_refs, kv_refs, out_refs = refs[:4], refs[4:12], refs[12:16]
-    vt_ref, s_ref, p_ref = refs[16:]
-    x, zh, zl = where_ref[0], where_ref[1], where_ref[2]
+def attend_kernel(where_ref, *refs):
+    q_refs, kv_refs = refs[:4], refs[4:12]
+    own_ref, plus_ref, minus_ref, across_ref = refs[12:16]
+    vt_ref, s_ref, p_ref, open_ref = refs[16:]
+    x, zh, zl, core = where_ref[0], where_ref[1], where_ref[2], where_ref[3]
     for i in range(8):
         vt_ref[:, i * 256 : (i + 1) * 256] = kv_refs[i][:, HD:].T
-    first = lax.broadcasted_iota(jnp.int32, (1, 256), 1) < BLK
+    masks = jnp.concatenate([ref[256:272, :] for ref in q_refs], axis=0)
+    row = lax.broadcasted_iota(jnp.int32, (64, 1024), 0)
+    block = lax.broadcasted_iota(jnp.int32, (64, 1024), 1) // BLK
+    pick = jnp.where(row == block * 8, 1.0, 0.0).astype(BF)
+    open_ref[...] = lax.dot_general(
+        masks, pick, (((0,), (0,)), ((), ())), preferred_element_type=F32
+    )
     for j in range(4):
         q = q_refs[j][:256, :]
+        slot = j % 2
         opens = []
         top = jnp.full((1, 256), NEG, F32)
         for i in range(8):
@@ -65,11 +89,9 @@
             s = lax.dot_general(
                 kv_refs[i][:, :HD], q, (((1,), (1,)), ((), ())), preferred_element_type=F32
             )
-            s_ref[i * 256 : (i + 1) * 256, :] = s
+            s_ref[slot, i * 256 : (i + 1) * 256, :] = s
             for part in range(2):
-                open0 = mask_ref[2 * j, source + part]
-                open1 = mask_ref[2 * j + 1, source + part]
-                is_open = jnp.where(first, open0, open1) > 0
+                is_open = open_ref[pl.ds(source + part, 1), j * 256 : (j + 1) * 256] > 0.5
                 opens.append(is_open)
                 here = jnp.max(s[part * BLK : (part + 1) * BLK], axis=0, keepdims=True)
                 top = jnp.maximum(top, jnp.where(is_open, here, NEG))
@@ -78,19 +100,31 @@
         for b in range(16):
             less = jnp.where(opens[b], top, BIG)
             rows = slice(b * BLK, (b + 1) * BLK)
-            w = jnp.exp2(s_ref[rows, :] * SCALE2 - less)
+            w = jnp.exp2(s_ref[slot, rows, :] * SCALE2 - less)
             total += jnp.sum(w, axis=0, keepdims=True)
-            p_ref[rows, :] = w.astype(BF)
-        acc = jnp.dot(vt_ref[...], p_ref[...], preferred_element_type=F32)
+            p_ref[slot, rows, :] = w.astype(BF)
+        acc = jnp.dot(vt_ref[...], p_ref[slot], preferred_element_type=F32)
         some = total > 0.0
         safe = jnp.where(some, total, 1.0)
-        out_refs[j][:HD, :] = (acc / safe).astype(BF)
+        out = (acc / safe).astype(BF)
         lse = jnp.where(some, top + jnp.log2(safe), NEG)
         hi = lse.astype(BF).astype(F32)
         mid = (lse - hi).astype(BF).astype(F32)
         low = lse - hi - mid
         row = lax.broadcasted_iota(jnp.int32, (16, 256), 0)
-        out_refs[j][HD:, :] = jnp.where(row == 0, hi, jnp.where(row == 1, mid, low)).astype(BF)
+        tail = jnp.where(row == 0, hi, jnp.where(row == 1, mid, low)).astype(BF)
+
+        def put(ref, out=out, tail=tail):
+            ref[:HD, :] = out
+            ref[HD:, :] = tail
+
+        if j == 0:
+            put(own_ref)
+        elif j == 2:
+            put(across_ref)
+        else:
+            pl.when(core == (j == 3))(functools.partial(put, minus_ref))
+            pl.when(core != (j == 3))(functools.partial(put, plus_ref))
 
 
 def merge_kernel(where_ref, a_ref, b_ref, c_ref, d_ref, keep_ref, send_ref):
@@ -138,13 +172,19 @@
         out_refs[p][...] = out[p * 32 : (p + 1) * 32]
 
 
-def sum_kernel(a_ref, b_ref, c_ref, d_ref, out_ref):
-    out_ref[...] = (
-        a_ref[...].astype(F32)
-        + b_ref[...].astype(F32)
-        + c_ref[...].astype(F32)
-        + d_ref[...].astype(F32)
-    ).astype(BF)
+def pass_kernel(next_ref, prev_ref, a_ref, b_ref, to_next_ref, to_prev_ref):
+    half = a_ref.shape[1]
+    to_next_ref[...] = (next_ref[:, :half].astype(F32) + a_ref[...].astype(F32)).astype(BF)
+    to_prev_ref[...] = (prev_ref[:, half:].astype(F32) + b_ref[...].astype(F32)).astype(BF)
+
+
+def sum_kernel(own_ref, a_ref, b_ref, c_ref, d_ref, out_ref):
+    half = a_ref.shape[1]
+    own = own_ref[...].astype(F32)
+    left = own[:, :half] + a_ref[...].astype(F32) + b_ref[...].astype(F32)
+    right = own[:, half:] + c_ref[...].astype(F32) + d_ref[...].astype(F32)
+    out_ref[:, :half] = left.astype(BF)
+    out_ref[:, half:] = right.astype(BF)
 
 
 def shape(*dims, dtype=BF):
@@ -162,9 +202,10 @@
     packed = pl.pallas_call(
         prep_kernel,
         out_shape=shape(8, 32, 384),
-        in_specs=[VMEM] * 3,
+        in_specs=[pl.BlockSpec(memory_space=pl.ANY)] * 3,
         out_specs=VMEM,
-        compiler_params=PARAMS,
+        scratch_shapes=[pltpu.VMEM((3, 32, 1024), BF), pltpu.SemaphoreType.DMA((3,))],
+        compiler_params=pltpu.CompilerParams(vmem_limit_bytes=60 * 2**20),
     )(queries, keys, values)
     got = lax.all_to_all(packed, ("c", "y"), split_axis=0, concat_axis=0, tiled=True)
     q, kv = pl.pallas_call(
@@ -176,27 +217,33 @@
     )(where, got, own_mask, other_mask)
 
     pair = moved(kv, "zl", 1)
-    kvs = [kv] + [moved(kv, "x", k) for k in (1, 2, 3)]
-    qs = [q] + [moved(q, "zh", k) for k in (1, 2, 3)]
-    kvs += [pair] + [moved(pair, "x", k) for k in (1, 2, 3)]
-    mask = jnp.concatenate([t[r : r + 1, :64] for t in qs for r in (256, 264)]).astype(jnp.int32)
+    near = [moved(kv, "x", k) for k in (1, 3, 2)]
+    far = [moved(pair, "x", k) for k in (1, 3, 2)]
+    kvs = [kv, near[0], near[2], near[1], pair, far[0], far[2], far[1]]
+    mate = moved(q, "c", 1)
+    first = moved_by_core(jnp.concatenate([q, mate]), "zh")
+    across = moved_by_core(first[:272], "zh")
+    second = moved(first[272:], "c", 1)
+    qs = [q, first, across, second]
 
     parts = pl.pallas_call(
         attend_kernel,
         out_shape=tuple(shape(144, 256) for _ in range(4)),
-        in_specs=[SMEM] * 2 + [VMEM] * 12,
+        in_specs=[SMEM] + [VMEM] * 12,
         out_specs=(VMEM,) * 4,
         scratch_shapes=[
             pltpu.VMEM((HD, 2048), BF),
-            pltpu.VMEM((2048, 256), F32),
-            pltpu.VMEM((2048, 256), BF),
+            pltpu.VMEM((2, 2048, 256), F32),
+            pltpu.VMEM((2, 2048, 256), BF),
+            pltpu.VMEM((HD, 1024), F32),
         ],
         compiler_params=PARAMS,
         cost_estimate=pl.CostEstimate(
             flops=2 * 2 * 1024 * 2048 * HD, bytes_accessed=2**21, transcendentals=2**21
         ),
-    )(where, mask, *qs, *kvs)
-    back = [parts[0]] + [moved(parts[k], "zh", -k) for k in (1, 2, 3)]
+    )(where, *qs, *kvs)
+    own, plus, minus, across = parts
+    back = [own, moved(across, "zh", 2), moved(plus, "zh", 1), moved(minus, "zh", -1)]
 
     keep, send = pl.pallas_call(
         merge_kernel,
@@ -226,14 +273,28 @@
             flops=2 * 128 * 256 * width, bytes_accessed=2**22, transcendentals=0
         ),
     )(where, keep, other, out_weight)
-    arrived = [moved(pieces[k], "y", k) for k in (2, 1, 3)]
+    own, to_next, across, to_prev = pieces
+    half = width // 2
+    a = moved(across[:, :half], "y", 1)
+    b = moved(across[:, half:], "y", -1)
+    right_from_prev = moved(to_next[:, half:], "y", 1)
+    left_from_next = moved(to_prev[:, :half], "y", -1)
+    next_sum, prev_sum = pl.pallas_call(
+        pass_kernel,
+        out_shape=(shape(32, half), shape(32, half)),
+        in_specs=[VMEM] * 4,
+        out_specs=(VMEM, VMEM),
+        compiler_params=PARAMS,
+    )(to_next, to_prev, a, b)
+    left_from_prev = moved(next_sum, "y", 1)
+    right_from_next = moved(prev_sum, "y", -1)
     return pl.pallas_call(
         sum_kernel,
         out_shape=shape(32, width),
-        in_specs=[VMEM] * 4,
+        in_specs=[VMEM] * 5,
         out_specs=VMEM,
         compiler_params=PARAMS,
-    )(pieces[0], *arrived)
+    )(own, left_from_prev, left_from_next, right_from_prev, right_from_next)
 
 
 def solution(mesh):

time: 86.6 us -> 74.9 us (0.86)
  waiting for transfers between devices: 35.9 us -> 21.8 us
  starting transfers between devices: 36.9 us -> 40.2 us
  local copies, waits for them, and re-layouts: 2.69 us -> 0.17 us
  Pallas kernels: 9.75 us -> 11.1 us
    ppermute x18 -> x20, waiting for transfers between devices: 31.7 us -> 16.6 us  [moved(): lax.ppermute(value, axis, [(i, (i + by) % size) for i in range(size)])]
    ppermute x0 -> x2, starting transfers between devices: none -> 5.99 us  [moved_by_core(): return lax.ppermute(value, (axis, 'c'), pairs)]
    ppermute x18 -> x20, starting transfers between devices: 32.3 us -> 29.7 us  [moved(): lax.ppermute(value, axis, [(i, (i + by) % size) for i in range(size)])]
    unnamed x9 -> x3, local copies, waits for them, and re-layouts: 2.53 us -> 0.01 us
    ppermute x0 -> x2, waiting for transfers between devices: none -> 1.18 us  [moved_by_core(): return lax.ppermute(value, (axis, 'c'), pairs)]
    pallas_call x1 -> x2, Pallas kernels: 0.71 us -> 1.69 us  [the longest x1 1.61 us: body(): pl.pallas_call(prep_kernel, out_shape=shape(8, 32, 384), in_specs=[pl.Blo...]
  transfers between devices with their start and end apart: 19 -> 23, of which waited for: 13 -> 13; matrix products, arithmetic and copies ran while one was open for 1% -> 1% of each run, Pallas kernels for 0% -> 0%
where the time goes in v2:
time: 74.9 us; the launch traced here: 74.2 us
  starting transfers between devices  40.2 us (54%)
  waiting for transfers between devices  21.8 us (29%)
  Pallas kernels  11.1 us (15%)
  other arithmetic  0.84 us (1%)
    ppermute x20, starting transfers between devices, moved(): lax.ppermute(value, axis, [(i, (i + by) % size) for i in range(size)])  29.7 us
    ppermute x20, waiting for transfers between devices, moved(): lax.ppermute(value, axis, [(i, (i + by) % size) for i in range(size)])  16.6 us
    ppermute x2, starting transfers between devices, moved_by_core(): return lax.ppermute(value, (axis, 'c'), pairs)  5.99 us
    pallas_call x1, Pallas kernels, body(): pl.pallas_call(attend_kernel, out_shape=tuple((shape(144, 256) for _ in r...  5.36 us
    all_to_all x1, starting transfers between devices, body(): lax.all_to_all(packed, ('c', 'y'), split_axis=0, concat_axis=0, tiled=True)  4.48 us
    all_to_all x1, waiting for transfers between devices, body(): lax.all_to_all(packed, ('c', 'y'), split_axis=0, concat_axis=0, tiled=True)  4 us
    pallas_call x1, Pallas kernels, body(): pl.pallas_call(project_kernel, out_shape=tuple((shape(32, width) for _ in...  1.98 us
    pallas_call x1, Pallas kernels, body(): pl.pallas_call(prep_kernel, out_shape=shape(8, 32, 384), in_specs=[pl.Blo...  1.61 us
  transfers between devices with their start and end apart: 23, of which 13 were waited for; matrix products, arithmetic and copies ran while one was open for 1% of the time, Pallas kernels for 0%

profile of v2, /device:TPU:32, one launch (start us, length us, event | category | flops | bytes accessed | tf_op | source)
XLA Modules:
  0.0 74.2 jit_solution(16440352249120660387)
XLA Ops:
  0.0 1.6 %shard_map.55 = bf16[8,32,384]{2,1,0:T(8,128)(2,1)} custom-call(bf16[32,1024]{1,0:T(8,128)(2,1)} %q_ref.1, bf16[32,1024]{1,0:T(8,128)(2,1)} %k_ref.1, bf16[32,1024]{1,0:T(8,128)(2,1)} %v_ref.1), custom_call_target="tpu_custom_call" | custom-call | tf_op jit(solution)/shard_map/pallas_call | solution.py:202
  1.6 4.5 %all-to-all-start = ((bf16[8,32,384]{2,1,0:T(8,128)(2,1)}), bf16[8,32,384]{2,1,0:T(8,128)(2,1)S(1)}, u32[]{:S(2)}, u32[]{:S(2)}) async-start(bf16[8,32,384]{2,1,0:T(8,128)(2,1)} %shard_map.55), calls=%async_computation | async-start | bytes 393216 | tf_op jit(solution)/shard_map/all_to_all | solution.py:210
  6.1 0.8 %convert_element_type.8 = bf16[2,1,64]{2,1,0:T(2,128)(2,1)S(1)} convert(s32[2,1,64]{2,1,0:T(1,128)} %param.8) | non-fusion elementwise | flops 128 | bytes 768 | tf_op jit(solution)/shard_map/convert_element_type | solution.py:197
  7.6 0.7 collective-permute-done.other_ref
  8.4 4.0 %all-to-all-done.got_ref = bf16[8,32,384]{2,1,0:T(8,128)(2,1)S(1)} async-done(((bf16[8,32,384]{2,1,0:T(8,128)(2,1)}), bf16[8,32,384]{2,1,0:T(8,128)(2,1)S(1)}, u32[]{:S(2)}, u32[]{:S(2)}) %all-to-all-start) | async-done | bytes 196640 | tf_op jit(solution)/shard_map/all_to_all | solution.py:210
  13.2 1.1 %collective-permute-done.1 = bf16[272,128]{1,0:T(8,128)(2,1)S(1)} collective-permute-done((bf16[272,128]{1,0:T(8,128)(2,1)S(1)}, bf16[272,128]{1,0:T(8,128)(2,1)S(1)}, u32[]{:S(2)}, u32[]{:S(2)}) %collective-permute-start.1) | collective-permute-done | bytes 69664 | tf_op jit(solution)/shard_map/ppermute | solution.py:28
  14.3 3.3 %collective-permute-start.2 = (bf16[544,128]{1,0:T(8,128)(2,1)S(1)}, bf16[544,128]{1,0:T(8,128)(2,1)S(1)}, u32[]{:S(2)}, u32[]{:S(2)}) collective-permute-start(bf16[544,128]{1,0:T(8,128)(2,1)S(1)} %pad_maximum_fusion), channel_id=1, source_target_pairs={{0,16},{4,52},{16,32},{20,4},{32,48},{36,20},{48,0},{52,36},{1,17}... | collective-permute-start | bytes 417800 | tf_op jit(solution)/shard_map/ppermute | solution.py:37
  17.8 1.5 %collective-permute-start.5 = (bf16[256,256]{1,0:T(8,128)(2,1)S(1)}, bf16[256,256]{1,0:T(8,128)(2,1)S(1)}, u32[]{:S(2)}, u32[]{:S(2)}) collective-permute-start(bf16[256,256]{1,0:T(8,128)(2,1)S(1)} %get-tuple-element.20.refs_4_), channel_id=1, source_target_pairs={{0,64},{64,128},{128,192},{192,0},{1,65},{65,129},{129,193},{193,1... | collective-permute-start | bytes 393224 | tf_op jit(solution)/shard_map/ppermute | solution.py:28
  19.3 2.7 %collective-permute-start.6 = (bf16[256,256]{1,0:T(8,128)(2,1)S(1)}, bf16[256,256]{1,0:T(8,128)(2,1)S(1)}, u32[]{:S(2)}, u32[]{:S(2)}) collective-permute-start(bf16[256,256]{1,0:T(8,128)(2,1)S(1)} %get-tuple-element.20.refs_4_), channel_id=1, source_target_pairs={{0,128},{64,192},{128,0},{192,64},{1,129},{65,193},{129,1},{193,65... | collective-permute-start | bytes 393224 | tf_op jit(solution)/shard_map/ppermute | solution.py:28
  22.0 1.4 %collective-permute-start.7 = (bf16[256,256]{1,0:T(8,128)(2,1)S(1)}, bf16[256,256]{1,0:T(8,128)(2,1)S(1)}, u32[]{:S(2)}, u32[]{:S(2)}) collective-permute-start(bf16[256,256]{1,0:T(8,128)(2,1)S(1)} %get-tuple-element.20.refs_4_), channel_id=1, source_target_pairs={{0,192},{64,0},{128,64},{192,128},{1,193},{65,1},{129,65},{193,129... | collective-permute-start | bytes 393224 | tf_op jit(solution)/shard_map/ppermute | solution.py:28
  23.4 1.6 %collective-permute-done.8.refs_8_ = bf16[256,256]{1,0:T(8,128)(2,1)S(1)} collective-permute-done((bf16[256,256]{1,0:T(8,128)(2,1)S(1)}, bf16[256,256]{1,0:T(8,128)(2,1)S(1)}, u32[]{:S(2)}, u32[]{:S(2)}) %collective-permute-start.8) | collective-permute-done | bytes 131104 | tf_op jit(solution)/shard_map/ppermute | solution.py:28
  25.0 3.0 %collective-permute-start.10 = (bf16[256,256]{1,0:T(8,128)(2,1)S(1)}, bf16[256,256]{1,0:T(8,128)(2,1)S(1)}, u32[]{:S(2)}, u32[]{:S(2)}) collective-permute-start(bf16[256,256]{1,0:T(8,128)(2,1)S(1)} %collective-permute-done.8.refs_8_), channel_id=1, source_target_pairs={{0,128},{64,192},{128,0},{192,64},{1,129},{65,193},{129,1},{193,65... | collective-permute-start | bytes 393224 | tf_op jit(solution)/shard_map/ppermute | solution.py:28
  28.1 1.1 %collective-permute-start.11 = (bf16[256,256]{1,0:T(8,128)(2,1)S(1)}, bf16[256,256]{1,0:T(8,128)(2,1)S(1)}, u32[]{:S(2)}, u32[]{:S(2)}) collective-permute-start(bf16[256,256]{1,0:T(8,128)(2,1)S(1)} %collective-permute-done.8.refs_8_), channel_id=1, source_target_pairs={{0,192},{64,0},{128,64},{192,128},{1,193},{65,1},{129,65},{193,129... | collective-permute-start | bytes 393224 | tf_op jit(solution)/shard_map/ppermute | solution.py:28
  29.2 0.9 %collective-permute-start.9 = (bf16[256,256]{1,0:T(8,128)(2,1)S(1)}, bf16[256,256]{1,0:T(8,128)(2,1)S(1)}, u32[]{:S(2)}, u32[]{:S(2)}) collective-permute-start(bf16[256,256]{1,0:T(8,128)(2,1)S(1)} %collective-permute-done.8.refs_8_), channel_id=1, source_target_pairs={{0,64},{64,128},{128,192},{192,0},{1,65},{65,129},{129,193},{193,1... | collective-permute-start | bytes 393224 | tf_op jit(solution)/shard_map/ppermute | solution.py:28
  30.1 2.6 %collective-permute-start.3 = (bf16[272,128]{1,0:T(8,128)(2,1)S(1)}, bf16[272,128]{1,0:T(8,128)(2,1)S(1)}, u32[]{:S(2)}, u32[]{:S(2)}) collective-permute-start(bf16[272,128]{1,0:T(8,128)(2,1)S(1)} %get-tuple-element.36), channel_id=1, source_target_pairs={{0,16},{4,52},{16,32},{20,4},{32,48},{36,20},{48,0},{52,36},{1,17}... | collective-permute-start | bytes 208904 | tf_op jit(solution)/shard_map/ppermute | solution.py:37
  32.8 2.7 %collective-permute-done.11.refs_11_ = bf16[256,256]{1,0:T(8,128)(2,1)S(1)} collective-permute-done((bf16[256,256]{1,0:T(8,128)(2,1)S(1)}, bf16[256,256]{1,0:T(8,128)(2,1)S(1)}, u32[]{:S(2)}, u32[]{:S(2)}) %collective-permute-start.11) | collective-permute-done | bytes 131104 | tf_op jit(solution)/shard_map/ppermute | solution.py:28
  35.9 1.2 %collective-permute-done.3.refs_2_ = bf16[272,128]{1,0:T(8,128)(2,1)S(1)} collective-permute-done((bf16[272,128]{1,0:T(8,128)(2,1)S(1)}, bf16[272,128]{1,0:T(8,128)(2,1)S(1)}, u32[]{:S(2)}, u32[]{:S(2)}) %collective-permute-start.3) | collective-permute-done | bytes 69664 | tf_op jit(solution)/shard_map/ppermute | solution.py:37
  37.1 5.4 %shard_map.57 = (bf16[144,256]{1,0:T(8,128)(2,1)S(1)}, bf16[144,256]{1,0:T(8,128)(2,1)S(1)}, bf16[144,256]{1,0:T(8,128)(2,1)S(1)}, bf16[144,256]{1,0:T(8,128)(2,1)S(1)}) custom-call(s32[5]{0:T(128)S(1)} %stack.23.where_ref, bf16[272,128]{1,0:T(8,128)(2,1)S(1)} %get-tuple-element.19.refs_0_, bf16[544,128]{1,0:T(8,128)(2,1)S(1)} %collective-permute-done.2.refs_1_, ...), custom_call_target="tpu_custom_call" | custom-call | flops 1073741824 | bytes 2097152 | tf_op jit(solution)/shard_map/pallas_call | solution.py:229
  42.4 4.6 %collective-permute-start.12 = (bf16[144,256]{1,0:T(8,128)(2,1)S(1)}, bf16[144,256]{1,0:T(8,128)(2,1)S(1)}, u32[]{:S(2)}, u32[]{:S(2)}) collective-permute-start(bf16[144,256]{1,0:T(8,128)(2,1)S(1)} %get-tuple-element.22), channel_id=1, source_target_pairs={{0,32},{16,48},{32,0},{48,16},{1,33},{17,49},{33,1},{49,17},{2,34}... | collective-permute-start | bytes 221192 | tf_op jit(solution)/shard_map/ppermute | solution.py:28
  47.1 4.1 %collective-permute-start.14 = (bf16[144,256]{1,0:T(8,128)(2,1)S(1)}, bf16[144,256]{1,0:T(8,128)(2,1)S(1)}, u32[]{:S(2)}, u32[]{:S(2)}) collective-permute-start(bf16[144,256]{1,0:T(8,128)(2,1)S(1)} %get-tuple-element.24), channel_id=1, source_target_pairs={{0,48},{16,0},{32,16},{48,32},{1,49},{17,1},{33,17},{49,33},{2,50}... | collective-permute-start | bytes 221192 | tf_op jit(solution)/shard_map/ppermute | solution.py:28
  51.2 1.4 %collective-permute-done.12.b_ref = bf16[144,256]{1,0:T(8,128)(2,1)S(1)} collective-permute-done((bf16[144,256]{1,0:T(8,128)(2,1)S(1)}, bf16[144,256]{1,0:T(8,128)(2,1)S(1)}, u32[]{:S(2)}, u32[]{:S(2)}) %collective-permute-start.12) | collective-permute-done | bytes 73760 | tf_op jit(solution)/shard_map/ppermute | solution.py:28
  52.6 1.7 %collective-permute-done.13.c_ref = bf16[144,256]{1,0:T(8,128)(2,1)S(1)} collective-permute-done((bf16[144,256]{1,0:T(8,128)(2,1)S(1)}, bf16[144,256]{1,0:T(8,128)(2,1)S(1)}, u32[]{:S(2)}, u32[]{:S(2)}) %collective-permute-start.13) | collective-permute-done | bytes 73760 | tf_op jit(solution)/shard_map/ppermute | solution.py:28
  54.3 0.6 shard_map.58
  55.0 1.2 %collective-permute-done.15.other_ref = bf16[128,128]{1,0:T(8,128)(2,1)S(1)} collective-permute-done((bf16[128,128]{1,0:T(8,128)(2,1)S(1)}, bf16[128,128]{1,0:T(8,128)(2,1)S(1)}, u32[]{:S(2)}, u32[]{:S(2)}) %collective-permute-start.15) | collective-permute-done | bytes 32800 | tf_op jit(solution)/shard_map/ppermute | solution.py:28
  56.2 2.0 %shard_map.59 = (bf16[32,5120]{1,0:T(8,128)(2,1)S(1)}, bf16[32,5120]{1,0:T(8,128)(2,1)S(1)}, bf16[32,5120]{1,0:T(8,128)(2,1)S(1)}, bf16[32,5120]{1,0:T(8,128)(2,1)S(1)}) custom-call(s32[5]{0:T(128)S(1)} %stack.23.where_ref, bf16[128,128]{1,0:T(8,128)(2,1)S(1)} %get-tuple-element.25.own_ref, bf16[128,128]{1,0:T(8,128)(2,1)S(1)} %collective-permute-done.15.other_ref, ...), custom_call_target="tpu_custom_call" | custom-call | flops 335544320 | bytes 4194304 | tf_op jit(solution)/shard_map/pallas_call | solution.py:259
  58.3 0.9 %collective-permute-start.16 = (bf16[32,2560]{1,0:T(8,128)(2,1)S(1)}, bf16[32,2560]{1,0:T(8,128)(2,1)S(1)}, u32[]{:S(2)}, u32[]{:S(2)}) collective-permute-start(bf16[32,2560]{1,0:T(8,128)(2,1)S(1)} %get-tuple-element.34), channel_id=1, source_target_pairs={{0,1},{1,2},{2,3},{3,0},{4,5},{5,6},{6,7},{7,4},{8,9},{9,10},{10,1... | collective-permute-start | bytes 491528 | tf_op jit(solution)/shard_map/ppermute | solution.py:28
  59.2 2.4 %collective-permute-start.17 = (bf16[32,2560]{1,0:T(8,128)(2,1)S(1)}, bf16[32,2560]{1,0:T(8,128)(2,1)S(1)}, u32[]{:S(2)}, u32[]{:S(2)}) collective-permute-start(bf16[32,2560]{1,0:T(8,128)(2,1)S(1)} %get-tuple-element.33), channel_id=1, source_target_pairs={{0,3},{1,0},{2,1},{3,2},{4,7},{5,4},{6,5},{7,6},{8,11},{9,8},{10,9... | collective-permute-start | bytes 491528 | tf_op jit(solution)/shard_map/ppermute | solution.py:28
  62.2 1.6 %collective-permute-start.20 = (bf16[32,2560]{1,0:T(8,128)(2,1)S(1)}, bf16[32,2560]{1,0:T(8,128)(2,1)S(1)}, u32[]{:S(2)}, u32[]{:S(2)}) collective-permute-start(bf16[32,2560]{1,0:T(8,128)(2,1)S(1)} %slice.23), channel_id=1, source_target_pairs={{0,1},{1,2},{2,3},{3,0},{4,5},{5,6},{6,7},{7,4},{8,9},{9,10},{10,1... | collective-permute-start | bytes 491528 | tf_op jit(solution)/shard_map/ppermute | solution.py:28
  63.8 2.4 %collective-permute-done.16.a_ref = bf16[32,2560]{1,0:T(8,128)(2,1)S(1)} collective-permute-done((bf16[32,2560]{1,0:T(8,128)(2,1)S(1)}, bf16[32,2560]{1,0:T(8,128)(2,1)S(1)}, u32[]{:S(2)}, u32[]{:S(2)}) %collective-permute-start.16) | collective-permute-done | bytes 163872 | tf_op jit(solution)/shard_map/ppermute | solution.py:28
  66.7 3.5 %collective-permute-start.21 = (bf16[32,2560]{1,0:T(8,128)(2,1)S(1)}, bf16[32,2560]{1,0:T(8,128)(2,1)S(1)}, u32[]{:S(2)}, u32[]{:S(2)}) collective-permute-start(bf16[32,2560]{1,0:T(8,128)(2,1)S(1)} %get-tuple-element.32), channel_id=1, source_target_pairs={{0,3},{1,0},{2,1},{3,2},{4,7},{5,4},{6,5},{7,6},{8,11},{9,8},{10,9... | collective-permute-start | bytes 491528 | tf_op jit(solution)/shard_map/ppermute | solution.py:28
  70.1 3.2 %collective-permute-done.18.a_ref = bf16[32,2560]{1,0:T(8,128)(2,1)S(1)} collective-permute-done((bf16[32,2560]{1,0:T(8,128)(2,1)S(1)}, bf16[32,2560]{1,0:T(8,128)(2,1)S(1)}, u32[]{:S(2)}, u32[]{:S(2)}) %collective-permute-start.18) | collective-permute-done | bytes 163872 | tf_op jit(solution)/shard_map/ppermute | solution.py:28
  73.3 0.8 %shard_map.61 = bf16[32,5120]{1,0:T(8,128)(2,1)} custom-call(bf16[32,5120]{1,0:T(8,128)(2,1)S(1)} %get-tuple-element.27.own_ref, bf16[32,2560]{1,0:T(8,128)(2,1)S(1)} %collective-permute-done.18.a_ref, bf16[32,2560]{1,0:T(8,128)(2,1)S(1)} %collective-permute-done.19.b_ref, bf16[32,2560]{1,0:T(8,128)(2,1)S(1)} %collective-permute-done.20.c_ref, ...), custom_call_target="tpu_custom_call" | custom-call | tf_op jit(solution)/shard_map/pallas_call | solution.py:291
  (34 shorter events, 3.3 us)
Async XLA Ops:
  1.6 10.8 %all-to-all-start = ((bf16[8,32,384]{2,1,0:T(8,128)(2,1)}), bf16[8,32,384]{2,1,0:T(8,128)(2,1)S(1)}, u32[]{:S(2)}, u32[]{:S(2)}) async-start(bf16[8,32,384]{2,1,0:T(8,128)(2,1)} %shard_map.55), calls=%async_computation | async-start | bytes 393216 | tf_op jit(solution)/shard_map/all_to_all | solution.py:210
  6.1 50.1 %copy-start = (bf16[256,5120]{1,0:T(8,128)(2,1)S(1)}, bf16[256,5120]{1,0:T(8,128)(2,1)}, u32[]{:S(2)}) copy-start(bf16[256,5120]{1,0:T(8,128)(2,1)} %w_ref.1) | copy-start | bytes 7864324
  7.0 1.4 %collective-permute-start = (bf16[16,128]{1,0:T(8,128)(2,1)S(1)}, bf16[16,128]{1,0:T(8,128)(2,1)S(1)}, u32[]{:S(2)}, u32[]{:S(2)}) collective-permute-start(bf16[16,128]{1,0:T(8,128)(2,1)S(1)} %broadcast_in_dim.17), channel_id=1, source_target_pairs={{0,4},{4,0},{1,5},{5,1},{2,6},{6,2},{3,7},{7,3},{8,12},{12,8},{9,1... | collective-permute-start | bytes 12296 | tf_op jit(solution)/shard_map/ppermute | solution.py:28
  13.0 1.3 %collective-permute-start.1 = (bf16[272,128]{1,0:T(8,128)(2,1)S(1)}, bf16[272,128]{1,0:T(8,128)(2,1)S(1)}, u32[]{:S(2)}, u32[]{:S(2)}) collective-permute-start(bf16[272,128]{1,0:T(8,128)(2,1)S(1)} %get-tuple-element.19.refs_0_), channel_id=1, source_target_pairs={{0,4},{4,0},{1,5},{5,1},{2,6},{6,2},{3,7},{7,3},{8,12},{12,8},{9,1... | collective-permute-start | bytes 208904 | tf_op jit(solution)/shard_map/ppermute | solution.py:28
  14.3 14.9 %collective-permute-start.2 = (bf16[544,128]{1,0:T(8,128)(2,1)S(1)}, bf16[544,128]{1,0:T(8,128)(2,1)S(1)}, u32[]{:S(2)}, u32[]{:S(2)}) collective-permute-start(bf16[544,128]{1,0:T(8,128)(2,1)S(1)} %pad_maximum_fusion), channel_id=1, source_target_pairs={{0,16},{4,52},{16,32},{20,4},{32,48},{36,20},{48,0},{52,36},{1,17}... | collective-permute-start | bytes 417800 | tf_op jit(solution)/shard_map/ppermute | solution.py:37
  17.7 7.4 %collective-permute-start.8 = (bf16[256,256]{1,0:T(8,128)(2,1)S(1)}, bf16[256,256]{1,0:T(8,128)(2,1)S(1)}, u32[]{:S(2)}, u32[]{:S(2)}) collective-permute-start(bf16[256,256]{1,0:T(8,128)(2,1)S(1)} %get-tuple-element.20.refs_4_), channel_id=1, source_target_pairs={{0,8},{8,0},{1,9},{9,1},{2,10},{10,2},{3,11},{11,3},{4,12},{12,4},... | collective-permute-start | bytes 393224 | tf_op jit(solution)/shard_map/ppermute | solution.py:28
  17.8 10.3 %collective-permute-start.5 = (bf16[256,256]{1,0:T(8,128)(2,1)S(1)}, bf16[256,256]{1,0:T(8,128)(2,1)S(1)}, u32[]{:S(2)}, u32[]{:S(2)}) collective-permute-start(bf16[256,256]{1,0:T(8,128)(2,1)S(1)} %get-tuple-element.20.refs_4_), channel_id=1, source_target_pairs={{0,64},{64,128},{128,192},{192,0},{1,65},{65,129},{129,193},{193,1... | collective-permute-start | bytes 393224 | tf_op jit(solution)/shard_map/ppermute | solution.py:28
  19.3 10.8 %collective-permute-start.6 = (bf16[256,256]{1,0:T(8,128)(2,1)S(1)}, bf16[256,256]{1,0:T(8,128)(2,1)S(1)}, u32[]{:S(2)}, u32[]{:S(2)}) collective-permute-start(bf16[256,256]{1,0:T(8,128)(2,1)S(1)} %get-tuple-element.20.refs_4_), channel_id=1, source_target_pairs={{0,128},{64,192},{128,0},{192,64},{1,129},{65,193},{129,1},{193,65... | collective-permute-start | bytes 393224 | tf_op jit(solution)/shard_map/ppermute | solution.py:28
  22.0 10.8 %collective-permute-start.7 = (bf16[256,256]{1,0:T(8,128)(2,1)S(1)}, bf16[256,256]{1,0:T(8,128)(2,1)S(1)}, u32[]{:S(2)}, u32[]{:S(2)}) collective-permute-start(bf16[256,256]{1,0:T(8,128)(2,1)S(1)} %get-tuple-element.20.refs_4_), channel_id=1, source_target_pairs={{0,192},{64,0},{128,64},{192,128},{1,193},{65,1},{129,65},{193,129... | collective-permute-start | bytes 393224 | tf_op jit(solution)/shard_map/ppermute | solution.py:28
  25.0 7.8 %collective-permute-start.10 = (bf16[256,256]{1,0:T(8,128)(2,1)S(1)}, bf16[256,256]{1,0:T(8,128)(2,1)S(1)}, u32[]{:S(2)}, u32[]{:S(2)}) collective-permute-start(bf16[256,256]{1,0:T(8,128)(2,1)S(1)} %collective-permute-done.8.refs_8_), channel_id=1, source_target_pairs={{0,128},{64,192},{128,0},{192,64},{1,129},{65,193},{129,1},{193,65... | collective-permute-start | bytes 393224 | tf_op jit(solution)/shard_map/ppermute | solution.py:28
  28.1 7.4 %collective-permute-start.11 = (bf16[256,256]{1,0:T(8,128)(2,1)S(1)}, bf16[256,256]{1,0:T(8,128)(2,1)S(1)}, u32[]{:S(2)}, u32[]{:S(2)}) collective-permute-start(bf16[256,256]{1,0:T(8,128)(2,1)S(1)} %collective-permute-done.8.refs_8_), channel_id=1, source_target_pairs={{0,192},{64,0},{128,64},{192,128},{1,193},{65,1},{129,65},{193,129... | collective-permute-start | bytes 393224 | tf_op jit(solution)/shard_map/ppermute | solution.py:28
  29.2 6.7 %collective-permute-start.9 = (bf16[256,256]{1,0:T(8,128)(2,1)S(1)}, bf16[256,256]{1,0:T(8,128)(2,1)S(1)}, u32[]{:S(2)}, u32[]{:S(2)}) collective-permute-start(bf16[256,256]{1,0:T(8,128)(2,1)S(1)} %collective-permute-done.8.refs_8_), channel_id=1, source_target_pairs={{0,64},{64,128},{128,192},{192,0},{1,65},{65,129},{129,193},{193,1... | collective-permute-start | bytes 393224 | tf_op jit(solution)/shard_map/ppermute | solution.py:28
  30.1 6.9 %collective-permute-start.3 = (bf16[272,128]{1,0:T(8,128)(2,1)S(1)}, bf16[272,128]{1,0:T(8,128)(2,1)S(1)}, u32[]{:S(2)}, u32[]{:S(2)}) collective-permute-start(bf16[272,128]{1,0:T(8,128)(2,1)S(1)} %get-tuple-element.36), channel_id=1, source_target_pairs={{0,16},{4,52},{16,32},{20,4},{32,48},{36,20},{48,0},{52,36},{1,17}... | collective-permute-start | bytes 208904 | tf_op jit(solution)/shard_map/ppermute | solution.py:37
  32.8 4.3 %collective-permute-start.4 = (bf16[272,128]{1,0:T(8,128)(2,1)S(1)}, bf16[272,128]{1,0:T(8,128)(2,1)S(1)}, u32[]{:S(2)}, u32[]{:S(2)}) collective-permute-start(bf16[272,128]{1,0:T(8,128)(2,1)S(1)} %get-tuple-element.35), channel_id=1, source_target_pairs={{0,4},{4,0},{1,5},{5,1},{2,6},{6,2},{3,7},{7,3},{8,12},{12,8},{9,1... | collective-permute-start | bytes 208904 | tf_op jit(solution)/shard_map/ppermute | solution.py:28
  42.4 10.2 %collective-permute-start.12 = (bf16[144,256]{1,0:T(8,128)(2,1)S(1)}, bf16[144,256]{1,0:T(8,128)(2,1)S(1)}, u32[]{:S(2)}, u32[]{:S(2)}) collective-permute-start(bf16[144,256]{1,0:T(8,128)(2,1)S(1)} %get-tuple-element.22), channel_id=1, source_target_pairs={{0,32},{16,48},{32,0},{48,16},{1,33},{17,49},{33,1},{49,17},{2,34}... | collective-permute-start | bytes 221192 | tf_op jit(solution)/shard_map/ppermute | solution.py:28
  47.1 7.2 %collective-permute-start.13 = (bf16[144,256]{1,0:T(8,128)(2,1)S(1)}, bf16[144,256]{1,0:T(8,128)(2,1)S(1)}, u32[]{:S(2)}, u32[]{:S(2)}) collective-permute-start(bf16[144,256]{1,0:T(8,128)(2,1)S(1)} %get-tuple-element.23), channel_id=1, source_target_pairs={{0,16},{16,32},{32,48},{48,0},{1,17},{17,33},{33,49},{49,1},{2,18}... | collective-permute-start | bytes 221192 | tf_op jit(solution)/shard_map/ppermute | solution.py:28
  47.1 7.2 %collective-permute-start.14 = (bf16[144,256]{1,0:T(8,128)(2,1)S(1)}, bf16[144,256]{1,0:T(8,128)(2,1)S(1)}, u32[]{:S(2)}, u32[]{:S(2)}) collective-permute-start(bf16[144,256]{1,0:T(8,128)(2,1)S(1)} %get-tuple-element.24), channel_id=1, source_target_pairs={{0,48},{16,0},{32,16},{48,32},{1,49},{17,1},{33,17},{49,33},{2,50}... | collective-permute-start | bytes 221192 | tf_op jit(solution)/shard_map/ppermute | solution.py:28
  54.9 1.3 %collective-permute-start.15 = (bf16[128,128]{1,0:T(8,128)(2,1)S(1)}, bf16[128,128]{1,0:T(8,128)(2,1)S(1)}, u32[]{:S(2)}, u32[]{:S(2)}) collective-permute-start(bf16[128,128]{1,0:T(8,128)(2,1)S(1)} %get-tuple-element.26), channel_id=1, source_target_pairs={{0,4},{4,0},{1,5},{5,1},{2,6},{6,2},{3,7},{7,3},{8,12},{12,8},{9,1... | collective-permute-start | bytes 98312 | tf_op jit(solution)/shard_map/ppermute | solution.py:28
  58.3 7.9 %collective-permute-start.16 = (bf16[32,2560]{1,0:T(8,128)(2,1)S(1)}, bf16[32,2560]{1,0:T(8,128)(2,1)S(1)}, u32[]{:S(2)}, u32[]{:S(2)}) collective-permute-start(bf16[32,2560]{1,0:T(8,128)(2,1)S(1)} %get-tuple-element.34), channel_id=1, source_target_pairs={{0,1},{1,2},{2,3},{3,0},{4,5},{5,6},{6,7},{7,4},{8,9},{9,10},{10,1... | collective-permute-start | bytes 491528 | tf_op jit(solution)/shard_map/ppermute | solution.py:28
  59.2 7.1 %collective-permute-start.17 = (bf16[32,2560]{1,0:T(8,128)(2,1)S(1)}, bf16[32,2560]{1,0:T(8,128)(2,1)S(1)}, u32[]{:S(2)}, u32[]{:S(2)}) collective-permute-start(bf16[32,2560]{1,0:T(8,128)(2,1)S(1)} %get-tuple-element.33), channel_id=1, source_target_pairs={{0,3},{1,0},{2,1},{3,2},{4,7},{5,4},{6,5},{7,6},{8,11},{9,8},{10,9... | collective-permute-start | bytes 491528 | tf_op jit(solution)/shard_map/ppermute | solution.py:28
  61.6 8.5 %collective-permute-start.19 = (bf16[32,2560]{1,0:T(8,128)(2,1)S(1)}, bf16[32,2560]{1,0:T(8,128)(2,1)S(1)}, u32[]{:S(2)}, u32[]{:S(2)}) collective-permute-start(bf16[32,2560]{1,0:T(8,128)(2,1)S(1)} %slice.22), channel_id=1, source_target_pairs={{0,3},{1,0},{2,1},{3,2},{4,7},{5,4},{6,5},{7,6},{8,11},{9,8},{10,9... | collective-permute-start | bytes 491528 | tf_op jit(solution)/shard_map/ppermute | solution.py:28
  62.2 7.9 %collective-permute-start.20 = (bf16[32,2560]{1,0:T(8,128)(2,1)S(1)}, bf16[32,2560]{1,0:T(8,128)(2,1)S(1)}, u32[]{:S(2)}, u32[]{:S(2)}) collective-permute-start(bf16[32,2560]{1,0:T(8,128)(2,1)S(1)} %slice.23), channel_id=1, source_target_pairs={{0,1},{1,2},{2,3},{3,0},{4,5},{5,6},{6,7},{7,4},{8,9},{9,10},{10,1... | collective-permute-start | bytes 491528 | tf_op jit(solution)/shard_map/ppermute | solution.py:28
  66.4 7.0 %collective-permute-start.18 = (bf16[32,2560]{1,0:T(8,128)(2,1)S(1)}, bf16[32,2560]{1,0:T(8,128)(2,1)S(1)}, u32[]{:S(2)}, u32[]{:S(2)}) collective-permute-start(bf16[32,2560]{1,0:T(8,128)(2,1)S(1)} %get-tuple-element.31), channel_id=1, source_target_pairs={{0,1},{1,2},{2,3},{3,0},{4,5},{5,6},{6,7},{7,4},{8,9},{9,10},{10,1... | collective-permute-start | bytes 491528 | tf_op jit(solution)/shard_map/ppermute | solution.py:28
  66.7 6.7 %collective-permute-start.21 = (bf16[32,2560]{1,0:T(8,128)(2,1)S(1)}, bf16[32,2560]{1,0:T(8,128)(2,1)S(1)}, u32[]{:S(2)}, u32[]{:S(2)}) collective-permute-start(bf16[32,2560]{1,0:T(8,128)(2,1)S(1)} %get-tuple-element.32), channel_id=1, source_target_pairs={{0,3},{1,0},{2,1},{3,2},{4,7},{5,4},{6,5},{7,6},{8,11},{9,8},{10,9... | collective-permute-start | bytes 491528 | tf_op jit(solution)/shard_map/ppermute | solution.py:28

commit v3 on v2

--- a/solution.py
+++ b/solution.py
@@ -19,7 +19,6 @@
 NEG = -1e30
 BIG = 1e30
 VMEM = pl.BlockSpec(memory_space=pltpu.VMEM)
-SMEM = pl.BlockSpec(memory_space=pltpu.SMEM)
 PARAMS = pltpu.CompilerParams(vmem_limit_bytes=40 * 2**20)
 
 
@@ -48,27 +47,40 @@
         copy.wait()
         for c in range(NC):
             for y in range(NY):
-                cols = slice((2 * y + c) * HD, (2 * y + c + 1) * HD)
-                out_ref[c * NY + y, :, i * HD : (i + 1) * HD] = held_ref[i, :, cols]
-
-
-def mid_kernel(where_ref, got_ref, own_ref, other_ref, q_ref, kv_ref):
-    y, c = where_ref[4], where_ref[3]
+                head, slot = 2 * y + c, c * NY + y
+                mine = held_ref[i, :, head * HD : (head + 1) * HD]
+                if i == 0:
+                    mate = head + 1 - 2 * c
+                    out_ref[slot, :, :HD] = mine
+                    out_ref[slot, :, HD : 2 * HD] = held_ref[i, :, mate * HD : (mate + 1) * HD]
+                else:
+                    out_ref[slot, :, (i + 1) * HD : (i + 2) * HD] = mine
+
+
+def mid_kernel(got_ref, local_ref, other_ref, q_ref, kv_ref):
+    y, c = lax.axis_index("y"), lax.axis_index("c")
     for part in range(NC):
         for p in range(NY):
-            rows = pl.ds((part * NY + p) * 32, 32)
-            q_ref[rows, :] = got_ref[part * NY + lax.rem(y + p, NY), :, :HD]
-            kv_ref[rows, :] = got_ref[part * NY + p, :, HD:]
-    own, other = own_ref[...].astype(F32), other_ref[...].astype(F32)
-    first = lax.broadcasted_iota(jnp.int32, own.shape, 0) < 8
-    q_ref[256:, :] = jnp.where(first == (c == 0), own, other).astype(BF)
-
-
-def attend_kernel(where_ref, *refs):
+            row = (part * NY + p) * 32
+            source = part * NY + lax.rem(y + p, NY)
+            q_ref[row : row + 32, :] = got_ref[source, :, :HD]
+            q_ref[272 + row : 304 + row, :] = got_ref[source, :, HD : 2 * HD]
+            kv_ref[row : row + 32, :] = got_ref[part * NY + p, :, 2 * HD :]
+    local, other = local_ref[...].astype(F32), other_ref[...].astype(F32)
+    low, is_zero = lax.broadcasted_iota(jnp.int32, (16, HD), 0) < 8, c == 0
+    blocks = (jnp.where(is_zero, local, other), jnp.where(is_zero, other, local))
+    for head in range(2):
+        rows = slice(head * 8, head * 8 + 1)
+        marks = jnp.where(low, blocks[0][rows], blocks[1][rows]).astype(BF)
+        pl.when(c == head)(functools.partial(q_ref.__setitem__, slice(256, 272), marks))
+        pl.when(c != head)(functools.partial(q_ref.__setitem__, slice(528, 544), marks))
+
+
+def attend_kernel(*refs):
     q_refs, kv_refs = refs[:4], refs[4:12]
     own_ref, plus_ref, minus_ref, across_ref = refs[12:16]
     vt_ref, s_ref, p_ref, open_ref = refs[16:]
-    x, zh, zl, core = where_ref[0], where_ref[1], where_ref[2], where_ref[3]
+    x, zh, zl, core = (lax.axis_index(a) for a in ("x", "zh", "zl", "c"))
     for i in range(8):
         vt_ref[:, i * 256 : (i + 1) * 256] = kv_refs[i][:, HD:].T
     masks = jnp.concatenate([ref[256:272, :] for ref in q_refs], axis=0)
@@ -78,9 +90,9 @@
     open_ref[...] = lax.dot_general(
         masks, pick, (((0,), (0,)), ((), ())), preferred_element_type=F32
     )
-    for j in range(4):
+
+    def score(j):
         q = q_refs[j][:256, :]
-        slot = j % 2
         opens = []
         top = jnp.full((1, 256), NEG, F32)
         for i in range(8):
@@ -89,21 +101,28 @@
             s = lax.dot_general(
                 kv_refs[i][:, :HD], q, (((1,), (1,)), ((), ())), preferred_element_type=F32
             )
-            s_ref[slot, i * 256 : (i + 1) * 256, :] = s
+            s_ref[j % 2, i * 256 : (i + 1) * 256, :] = s
             for part in range(2):
                 is_open = open_ref[pl.ds(source + part, 1), j * 256 : (j + 1) * 256] > 0.5
                 opens.append(is_open)
                 here = jnp.max(s[part * BLK : (part + 1) * BLK], axis=0, keepdims=True)
                 top = jnp.maximum(top, jnp.where(is_open, here, NEG))
-        top = top * SCALE2
-        total = jnp.zeros((1, 256), F32)
+        return opens, top * SCALE2
+
+    following = score(0)
+    for j in range(4):
+        opens, top = following
+        if j < 3:
+            following = score(j + 1)
+        sums = jnp.zeros((8, 256), F32)
         for b in range(16):
             less = jnp.where(opens[b], top, BIG)
             rows = slice(b * BLK, (b + 1) * BLK)
-            w = jnp.exp2(s_ref[slot, rows, :] * SCALE2 - less)
-            total += jnp.sum(w, axis=0, keepdims=True)
-            p_ref[slot, rows, :] = w.astype(BF)
-        acc = jnp.dot(vt_ref[...], p_ref[slot], preferred_element_type=F32)
+            w = jnp.exp2(s_ref[j % 2, rows, :] * SCALE2 - less)
+            sums += jnp.sum(w.reshape(16, 8, 256), axis=0)
+            p_ref[j % 2, rows, :] = w.astype(BF)
+        total = jnp.sum(sums, axis=0, keepdims=True)
+        acc = jnp.dot(vt_ref[...], p_ref[j % 2], preferred_element_type=F32)
         some = total > 0.0
         safe = jnp.where(some, total, 1.0)
         out = (acc / safe).astype(BF)
@@ -127,7 +146,7 @@
             pl.when(core != (j == 3))(functools.partial(put, plus_ref))
 
 
-def merge_kernel(where_ref, a_ref, b_ref, c_ref, d_ref, keep_ref, send_ref):
+def merge_kernel(a_ref, b_ref, c_ref, d_ref, keep_ref, send_ref):
     refs = (a_ref, b_ref, c_ref, d_ref)
     lses = []
     for ref in refs:
@@ -139,30 +158,30 @@
     acc = sum(ref[:HD, :].astype(F32) * (w * inv) for ref, w in zip(refs, ws))
     left, right = acc[:, :BLK].astype(BF), acc[:, BLK:].astype(BF)
 
-    @pl.when(where_ref[3] == 0)
+    @pl.when(lax.axis_index("c") == 0)
     def _():
         keep_ref[...] = left
         send_ref[...] = right
 
-    @pl.when(where_ref[3] == 1)
+    @pl.when(lax.axis_index("c") == 1)
     def _():
         keep_ref[...] = right
         send_ref[...] = left
 
 
-def project_kernel(where_ref, own_ref, other_ref, w_ref, *refs):
+def project_kernel(own_ref, other_ref, w_ref, *refs):
     out_refs, lhs_ref = refs[:4], refs[4]
 
     @pl.when(pl.program_id(0) == 0)
     def _():
         own, other = own_ref[...].T, other_ref[...].T
 
-        @pl.when(where_ref[3] == 0)
+        @pl.when(lax.axis_index("c") == 0)
         def _():
             lhs_ref[:, :HD] = own
             lhs_ref[:, HD:] = other
 
-        @pl.when(where_ref[3] == 1)
+        @pl.when(lax.axis_index("c") == 1)
         def _():
             lhs_ref[:, :HD] = other
             lhs_ref[:, HD:] = own
@@ -192,16 +211,13 @@
 
 
 def body(queries, keys, values, block_mask, out_weight):
-    where = jnp.stack([lax.axis_index(a) for a in AXES]).astype(jnp.int32)
-    core = lax.axis_index("c")
     seen = jnp.pad(block_mask[:, 0, :].astype(BF), ((0, 0), (0, 64)))
-    own_mask = jnp.broadcast_to(lax.dynamic_slice_in_dim(seen, core, 1), (16, 128))
-    send_mask = jnp.broadcast_to(lax.dynamic_slice_in_dim(seen, 1 - core, 1), (16, 128))
-    other_mask = moved(send_mask, "c", 1)
+    local = jnp.repeat(seen, 8, axis=0)
+    other = moved(local, "c", 1)
 
     packed = pl.pallas_call(
         prep_kernel,
-        out_shape=shape(8, 32, 384),
+        out_shape=shape(8, 32, 512),
         in_specs=[pl.BlockSpec(memory_space=pl.ANY)] * 3,
         out_specs=VMEM,
         scratch_shapes=[pltpu.VMEM((3, 32, 1024), BF), pltpu.SemaphoreType.DMA((3,))],
@@ -210,18 +226,17 @@
     got = lax.all_to_all(packed, ("c", "y"), split_axis=0, concat_axis=0, tiled=True)
     q, kv = pl.pallas_call(
         mid_kernel,
-        out_shape=(shape(272, HD), shape(256, 256)),
-        in_specs=[SMEM] + [VMEM] * 3,
+        out_shape=(shape(544, HD), shape(256, 256)),
+        in_specs=[VMEM] * 3,
         out_specs=(VMEM, VMEM),
         compiler_params=PARAMS,
-    )(where, got, own_mask, other_mask)
+    )(got, local, other)
 
     pair = moved(kv, "zl", 1)
     near = [moved(kv, "x", k) for k in (1, 3, 2)]
     far = [moved(pair, "x", k) for k in (1, 3, 2)]
     kvs = [kv, near[0], near[2], near[1], pair, far[0], far[2], far[1]]
-    mate = moved(q, "c", 1)
-    first = moved_by_core(jnp.concatenate([q, mate]), "zh")
+    first = moved_by_core(q, "zh")
     across = moved_by_core(first[:272], "zh")
     second = moved(first[272:], "c", 1)
     qs = [q, first, across, second]
@@ -229,7 +244,7 @@
     parts = pl.pallas_call(
         attend_kernel,
         out_shape=tuple(shape(144, 256) for _ in range(4)),
-        in_specs=[SMEM] + [VMEM] * 12,
+        in_specs=[VMEM] * 12,
         out_specs=(VMEM,) * 4,
         scratch_shapes=[
             pltpu.VMEM((HD, 2048), BF),
@@ -241,17 +256,17 @@
         cost_estimate=pl.CostEstimate(
             flops=2 * 2 * 1024 * 2048 * HD, bytes_accessed=2**21, transcendentals=2**21
         ),
-    )(where, *qs, *kvs)
+    )(*qs, *kvs)
     own, plus, minus, across = parts
     back = [own, moved(across, "zh", 2), moved(plus, "zh", 1), moved(minus, "zh", -1)]
 
     keep, send = pl.pallas_call(
         merge_kernel,
         out_shape=(shape(HD, BLK), shape(HD, BLK)),
-        in_specs=[SMEM] + [VMEM] * 4,
+        in_specs=[VMEM] * 4,
         out_specs=(VMEM, VMEM),
         compiler_params=PARAMS,
-    )(where, *back)
+    )(*back)
     other = moved(send, "c", 1)
 
     cols = 1280
@@ -261,7 +276,6 @@
         out_shape=tuple(shape(32, width) for _ in range(4)),
         grid=(width // cols,),
         in_specs=[
-            SMEM,
             pl.BlockSpec((HD, BLK), lambda i: (0, 0)),
             pl.BlockSpec((HD, BLK), lambda i: (0, 0)),
             pl.BlockSpec((2 * HD, cols), lambda i: (0, i)),
@@ -272,7 +286,7 @@
         cost_estimate=pl.CostEstimate(
             flops=2 * 128 * 256 * width, bytes_accessed=2**22, transcendentals=0
         ),
-    )(where, keep, other, out_weight)
+    )(keep, other, out_weight)
     own, to_next, across, to_prev = pieces
     half = width // 2
     a = moved(across[:, :half], "y", 1)

time: 74.9 us -> 72.6 us (0.969)
  the two profiles are of different devices: /device:TPU:32 before, /device:TPU:24 now
where the time goes in v3:
time: 72.6 us; the launch traced here: 72.4 us
  starting transfers between devices  39.6 us (55%)
  waiting for transfers between devices  24.1 us (33%)
  Pallas kernels  7.86 us (11%)
    ppermute x19, starting transfers between devices, moved(): lax.ppermute(value, axis, [(i, (i + by) % size) for i in range(size)])  27.9 us
    ppermute x19, waiting for transfers between devices, moved(): lax.ppermute(value, axis, [(i, (i + by) % size) for i in range(size)])  17.6 us
    ppermute x2, starting transfers between devices, moved_by_core(): return lax.ppermute(value, (axis, 'c'), pairs)  6.26 us
    all_to_all x1, starting transfers between devices, body(): lax.all_to_all(packed, ('c', 'y'), split_axis=0, concat_axis=0, tiled=True)  5.43 us
    pallas_call x1, Pallas kernels, body(): pl.pallas_call(attend_kernel, out_shape=tuple((shape(144, 256) for _ in r...  3.69 us
    all_to_all x1, waiting for transfers between devices, body(): lax.all_to_all(packed, ('c', 'y'), split_axis=0, concat_axis=0, tiled=True)  3.51 us
    ppermute x2, waiting for transfers between devices, moved_by_core(): return lax.ppermute(value, (axis, 'c'), pairs)  2.99 us
    pallas_call x1, Pallas kernels, body(): pl.pallas_call(prep_kernel, out_shape=shape(8, 32, 512), in_specs=[pl.Blo...  1.64 us
  transfers between devices with their start and end apart: 22, of which 13 were waited for; matrix products, arithmetic and copies ran while one was open for 1% of the time, Pallas kernels for 0%

profile of v3, /device:TPU:24, one launch (start us, length us, event | category | flops | bytes accessed | tf_op | source)
XLA Modules:
  0.0 72.4 jit_solution(12559523791758224582)
XLA Ops:
  0.0 1.6 %shard_map.55 = bf16[8,32,512]{2,1,0:T(8,128)(2,1)} custom-call(bf16[32,1024]{1,0:T(8,128)(2,1)} %q_ref.1, bf16[32,1024]{1,0:T(8,128)(2,1)} %k_ref.1, bf16[32,1024]{1,0:T(8,128)(2,1)} %v_ref.1), custom_call_target="tpu_custom_call" | custom-call | tf_op jit(solution)/shard_map/pallas_call | solution.py:218
  1.7 5.4 %all-to-all-start = ((bf16[8,32,512]{2,1,0:T(8,128)(2,1)}), bf16[8,32,512]{2,1,0:T(8,128)(2,1)S(1)}, u32[]{:S(2)}, u32[]{:S(2)}) async-start(bf16[8,32,512]{2,1,0:T(8,128)(2,1)} %shard_map.55), calls=%async_computation | async-start | bytes 524288 | tf_op jit(solution)/shard_map/all_to_all | solution.py:226
  7.1 0.7 convert_element_type.8
  8.0 1.0 %collective-permute-done.other_ref = bf16[16,128]{1,0:T(8,128)(2,1)S(1)} collective-permute-done((bf16[16,128]{1,0:T(8,128)(2,1)S(1)}, bf16[16,128]{1,0:T(8,128)(2,1)S(1)}, u32[]{:S(2)}, u32[]{:S(2)}) %collective-permute-start) | collective-permute-done | bytes 4128 | tf_op jit(solution)/shard_map/ppermute | solution.py:27
  9.0 3.5 %all-to-all-done.got_ref = bf16[8,32,512]{2,1,0:T(8,128)(2,1)S(1)} async-done(((bf16[8,32,512]{2,1,0:T(8,128)(2,1)}), bf16[8,32,512]{2,1,0:T(8,128)(2,1)S(1)}, u32[]{:S(2)}, u32[]{:S(2)}) %all-to-all-start) | async-done | bytes 262176 | tf_op jit(solution)/shard_map/all_to_all | solution.py:226
  12.6 2.8 %collective-permute-start.1 = (bf16[544,128]{1,0:T(8,128)(2,1)S(1)}, bf16[544,128]{1,0:T(8,128)(2,1)S(1)}, u32[]{:S(2)}, u32[]{:S(2)}) collective-permute-start(bf16[544,128]{1,0:T(8,128)(2,1)S(1)} %get-tuple-element.19.refs_0_), channel_id=1, source_target_pairs={{0,16},{4,52},{16,32},{20,4},{32,48},{36,20},{48,0},{52,36},{1,17}... | collective-permute-start | bytes 417800 | tf_op jit(solution)/shard_map/ppermute | solution.py:36
  15.4 1.9 %collective-permute-start.7 = (bf16[256,256]{1,0:T(8,128)(2,1)S(1)}, bf16[256,256]{1,0:T(8,128)(2,1)S(1)}, u32[]{:S(2)}, u32[]{:S(2)}) collective-permute-start(bf16[256,256]{1,0:T(8,128)(2,1)S(1)} %get-tuple-element.20.refs_4_), channel_id=1, source_target_pairs={{0,8},{8,0},{1,9},{9,1},{2,10},{10,2},{3,11},{11,3},{4,12},{12,4},... | collective-permute-start | bytes 393224 | tf_op jit(solution)/shard_map/ppermute | solution.py:27
  17.3 1.5 %collective-permute-start.4 = (bf16[256,256]{1,0:T(8,128)(2,1)S(1)}, bf16[256,256]{1,0:T(8,128)(2,1)S(1)}, u32[]{:S(2)}, u32[]{:S(2)}) collective-permute-start(bf16[256,256]{1,0:T(8,128)(2,1)S(1)} %get-tuple-element.20.refs_4_), channel_id=1, source_target_pairs={{0,64},{64,128},{128,192},{192,0},{1,65},{65,129},{129,193},{193,1... | collective-permute-start | bytes 393224 | tf_op jit(solution)/shard_map/ppermute | solution.py:27
  18.8 2.7 %collective-permute-start.5 = (bf16[256,256]{1,0:T(8,128)(2,1)S(1)}, bf16[256,256]{1,0:T(8,128)(2,1)S(1)}, u32[]{:S(2)}, u32[]{:S(2)}) collective-permute-start(bf16[256,256]{1,0:T(8,128)(2,1)S(1)} %get-tuple-element.20.refs_4_), channel_id=1, source_target_pairs={{0,128},{64,192},{128,0},{192,64},{1,129},{65,193},{129,1},{193,65... | collective-permute-start | bytes 393224 | tf_op jit(solution)/shard_map/ppermute | solution.py:27
  21.5 1.4 %collective-permute-start.6 = (bf16[256,256]{1,0:T(8,128)(2,1)S(1)}, bf16[256,256]{1,0:T(8,128)(2,1)S(1)}, u32[]{:S(2)}, u32[]{:S(2)}) collective-permute-start(bf16[256,256]{1,0:T(8,128)(2,1)S(1)} %get-tuple-element.20.refs_4_), channel_id=1, source_target_pairs={{0,192},{64,0},{128,64},{192,128},{1,193},{65,1},{129,65},{193,129... | collective-permute-start | bytes 393224 | tf_op jit(solution)/shard_map/ppermute | solution.py:27
  22.9 2.3 %collective-permute-start.10 = (bf16[256,256]{1,0:T(8,128)(2,1)S(1)}, bf16[256,256]{1,0:T(8,128)(2,1)S(1)}, u32[]{:S(2)}, u32[]{:S(2)}) collective-permute-start(bf16[256,256]{1,0:T(8,128)(2,1)S(1)} %collective-permute-done.7.refs_8_), channel_id=1, source_target_pairs={{0,192},{64,0},{128,64},{192,128},{1,193},{65,1},{129,65},{193,129... | collective-permute-start | bytes 393224 | tf_op jit(solution)/shard_map/ppermute | solution.py:27
  25.2 2.6 %collective-permute-start.9 = (bf16[256,256]{1,0:T(8,128)(2,1)S(1)}, bf16[256,256]{1,0:T(8,128)(2,1)S(1)}, u32[]{:S(2)}, u32[]{:S(2)}) collective-permute-start(bf16[256,256]{1,0:T(8,128)(2,1)S(1)} %collective-permute-done.7.refs_8_), channel_id=1, source_target_pairs={{0,128},{64,192},{128,0},{192,64},{1,129},{65,193},{129,1},{193,65... | collective-permute-start | bytes 393224 | tf_op jit(solution)/shard_map/ppermute | solution.py:27
  27.8 0.8 %collective-permute-done.5.refs_6_ = bf16[256,256]{1,0:T(8,128)(2,1)S(1)} collective-permute-done((bf16[256,256]{1,0:T(8,128)(2,1)S(1)}, bf16[256,256]{1,0:T(8,128)(2,1)S(1)}, u32[]{:S(2)}, u32[]{:S(2)}) %collective-permute-start.5) | collective-permute-done | bytes 131104 | tf_op jit(solution)/shard_map/ppermute | solution.py:27
  28.6 3.5 %collective-permute-start.2 = (bf16[272,128]{1,0:T(8,128)(2,1)S(1)}, bf16[272,128]{1,0:T(8,128)(2,1)S(1)}, u32[]{:S(2)}, u32[]{:S(2)}) collective-permute-start(bf16[272,128]{1,0:T(8,128)(2,1)S(1)} %get-tuple-element.36), channel_id=1, source_target_pairs={{0,16},{4,52},{16,32},{20,4},{32,48},{36,20},{48,0},{52,36},{1,17}... | collective-permute-start | bytes 208904 | tf_op jit(solution)/shard_map/ppermute | solution.py:36
  32.1 3.0 %collective-permute-done.2.refs_2_ = bf16[272,128]{1,0:T(8,128)(2,1)S(1)} collective-permute-done((bf16[272,128]{1,0:T(8,128)(2,1)S(1)}, bf16[272,128]{1,0:T(8,128)(2,1)S(1)}, u32[]{:S(2)}, u32[]{:S(2)}) %collective-permute-start.2) | collective-permute-done | bytes 69664 | tf_op jit(solution)/shard_map/ppermute | solution.py:36
  35.3 3.7 %shard_map.57 = (bf16[144,256]{1,0:T(8,128)(2,1)S(1)}, bf16[144,256]{1,0:T(8,128)(2,1)S(1)}, bf16[144,256]{1,0:T(8,128)(2,1)S(1)}, bf16[144,256]{1,0:T(8,128)(2,1)S(1)}) custom-call(bf16[544,128]{1,0:T(8,128)(2,1)S(1)} %get-tuple-element.19.refs_0_, bf16[544,128]{1,0:T(8,128)(2,1)S(1)} %collective-permute-done.1.refs_1_, ...), custom_call_target="tpu_custom_call" | custom-call | flops 1073741824 | bytes 2097152 | tf_op jit(solution)/shard_map/pallas_call | solution.py:244
  39.0 3.2 %collective-permute-start.11 = (bf16[144,256]{1,0:T(8,128)(2,1)S(1)}, bf16[144,256]{1,0:T(8,128)(2,1)S(1)}, u32[]{:S(2)}, u32[]{:S(2)}) collective-permute-start(bf16[144,256]{1,0:T(8,128)(2,1)S(1)} %get-tuple-element.22), channel_id=1, source_target_pairs={{0,32},{16,48},{32,0},{48,16},{1,33},{17,49},{33,1},{49,17},{2,34}... | collective-permute-start | bytes 221192 | tf_op jit(solution)/shard_map/ppermute | solution.py:27
  42.1 2.8 %collective-permute-start.12 = (bf16[144,256]{1,0:T(8,128)(2,1)S(1)}, bf16[144,256]{1,0:T(8,128)(2,1)S(1)}, u32[]{:S(2)}, u32[]{:S(2)}) collective-permute-start(bf16[144,256]{1,0:T(8,128)(2,1)S(1)} %get-tuple-element.23), channel_id=1, source_target_pairs={{0,16},{16,32},{32,48},{48,0},{1,17},{17,33},{33,49},{49,1},{2,18}... | collective-permute-start | bytes 221192 | tf_op jit(solution)/shard_map/ppermute | solution.py:27
  44.9 1.4 %collective-permute-start.13 = (bf16[144,256]{1,0:T(8,128)(2,1)S(1)}, bf16[144,256]{1,0:T(8,128)(2,1)S(1)}, u32[]{:S(2)}, u32[]{:S(2)}) collective-permute-start(bf16[144,256]{1,0:T(8,128)(2,1)S(1)} %get-tuple-element.24), channel_id=1, source_target_pairs={{0,48},{16,0},{32,16},{48,32},{1,49},{17,1},{33,17},{49,33},{2,50}... | collective-permute-start | bytes 221192 | tf_op jit(solution)/shard_map/ppermute | solution.py:27
  46.3 2.7 %collective-permute-done.11.b_ref = bf16[144,256]{1,0:T(8,128)(2,1)S(1)} collective-permute-done((bf16[144,256]{1,0:T(8,128)(2,1)S(1)}, bf16[144,256]{1,0:T(8,128)(2,1)S(1)}, u32[]{:S(2)}, u32[]{:S(2)}) %collective-permute-start.11) | collective-permute-done | bytes 73760 | tf_op jit(solution)/shard_map/ppermute | solution.py:27
  49.0 2.3 %collective-permute-done.13.d_ref = bf16[144,256]{1,0:T(8,128)(2,1)S(1)} collective-permute-done((bf16[144,256]{1,0:T(8,128)(2,1)S(1)}, bf16[144,256]{1,0:T(8,128)(2,1)S(1)}, u32[]{:S(2)}, u32[]{:S(2)}) %collective-permute-start.13) | collective-permute-done | bytes 73760 | tf_op jit(solution)/shard_map/ppermute | solution.py:27
  51.5 1.2 %collective-permute-done.14.other_ref = bf16[128,128]{1,0:T(8,128)(2,1)S(1)} collective-permute-done((bf16[128,128]{1,0:T(8,128)(2,1)S(1)}, bf16[128,128]{1,0:T(8,128)(2,1)S(1)}, u32[]{:S(2)}, u32[]{:S(2)}) %collective-permute-start.14) | collective-permute-done | bytes 32800 | tf_op jit(solution)/shard_map/ppermute | solution.py:27
  52.7 1.5 %shard_map.59 = (bf16[32,5120]{1,0:T(8,128)(2,1)S(1)}, bf16[32,5120]{1,0:T(8,128)(2,1)S(1)}, bf16[32,5120]{1,0:T(8,128)(2,1)S(1)}, bf16[32,5120]{1,0:T(8,128)(2,1)S(1)}) custom-call(bf16[128,128]{1,0:T(8,128)(2,1)S(1)} %get-tuple-element.25.own_ref, bf16[128,128]{1,0:T(8,128)(2,1)S(1)} %collective-permute-done.14.other_ref, bf16[256,5120]{1,0:T(8,128)(2,1)S(1)} %copy-done), custom_call_target="tpu_custom_call" | custom-call | flops 335544320 | bytes 4194304 | tf_op jit(solution)/shard_map/pallas_call | solution.py:274
  54.2 2.3 %collective-permute-start.15 = (bf16[32,2560]{1,0:T(8,128)(2,1)S(1)}, bf16[32,2560]{1,0:T(8,128)(2,1)S(1)}, u32[]{:S(2)}, u32[]{:S(2)}) collective-permute-start(bf16[32,2560]{1,0:T(8,128)(2,1)S(1)} %get-tuple-element.34), channel_id=1, source_target_pairs={{0,1},{1,2},{2,3},{3,0},{4,5},{5,6},{6,7},{7,4},{8,9},{9,10},{10,1... | collective-permute-start | bytes 491528 | tf_op jit(solution)/shard_map/ppermute | solution.py:27
  56.5 0.4 collective-permute-start.18
  56.9 3.0 %collective-permute-start.19 = (bf16[32,2560]{1,0:T(8,128)(2,1)S(1)}, bf16[32,2560]{1,0:T(8,128)(2,1)S(1)}, u32[]{:S(2)}, u32[]{:S(2)}) collective-permute-start(bf16[32,2560]{1,0:T(8,128)(2,1)S(1)} %slice.23), channel_id=1, source_target_pairs={{0,1},{1,2},{2,3},{3,0},{4,5},{5,6},{6,7},{7,4},{8,9},{9,10},{10,1... | collective-permute-start | bytes 491528 | tf_op jit(solution)/shard_map/ppermute | solution.py:27
  59.9 1.4 %collective-permute-done.15.a_ref = bf16[32,2560]{1,0:T(8,128)(2,1)S(1)} collective-permute-done((bf16[32,2560]{1,0:T(8,128)(2,1)S(1)}, bf16[32,2560]{1,0:T(8,128)(2,1)S(1)}, u32[]{:S(2)}, u32[]{:S(2)}) %collective-permute-start.15) | collective-permute-done | bytes 163872 | tf_op jit(solution)/shard_map/ppermute | solution.py:27
  61.3 3.4 %collective-permute-done.16.b_ref = bf16[32,2560]{1,0:T(8,128)(2,1)S(1)} collective-permute-done((bf16[32,2560]{1,0:T(8,128)(2,1)S(1)}, bf16[32,2560]{1,0:T(8,128)(2,1)S(1)}, u32[]{:S(2)}, u32[]{:S(2)}) %collective-permute-start.16) | collective-permute-done | bytes 163872 | tf_op jit(solution)/shard_map/ppermute | solution.py:27
  64.9 2.0 %collective-permute-start.20 = (bf16[32,2560]{1,0:T(8,128)(2,1)S(1)}, bf16[32,2560]{1,0:T(8,128)(2,1)S(1)}, u32[]{:S(2)}, u32[]{:S(2)}) collective-permute-start(bf16[32,2560]{1,0:T(8,128)(2,1)S(1)} %get-tuple-element.32), channel_id=1, source_target_pairs={{0,3},{1,0},{2,1},{3,2},{4,7},{5,4},{6,5},{7,6},{8,11},{9,8},{10,9... | collective-permute-start | bytes 491528 | tf_op jit(solution)/shard_map/ppermute | solution.py:27
  67.3 2.9 %collective-permute-done.17.a_ref = bf16[32,2560]{1,0:T(8,128)(2,1)S(1)} collective-permute-done((bf16[32,2560]{1,0:T(8,128)(2,1)S(1)}, bf16[32,2560]{1,0:T(8,128)(2,1)S(1)}, u32[]{:S(2)}, u32[]{:S(2)}) %collective-permute-start.17) | collective-permute-done | bytes 163872 | tf_op jit(solution)/shard_map/ppermute | solution.py:27
  70.2 1.3 %collective-permute-done.20.d_ref = bf16[32,2560]{1,0:T(8,128)(2,1)S(1)} collective-permute-done((bf16[32,2560]{1,0:T(8,128)(2,1)S(1)}, bf16[32,2560]{1,0:T(8,128)(2,1)S(1)}, u32[]{:S(2)}, u32[]{:S(2)}) %collective-permute-start.20) | collective-permute-done | bytes 163872 | tf_op jit(solution)/shard_map/ppermute | solution.py:27
  71.5 0.8 %shard_map.61 = bf16[32,5120]{1,0:T(8,128)(2,1)} custom-call(bf16[32,5120]{1,0:T(8,128)(2,1)S(1)} %get-tuple-element.27.own_ref, bf16[32,2560]{1,0:T(8,128)(2,1)S(1)} %collective-permute-done.17.a_ref, bf16[32,2560]{1,0:T(8,128)(2,1)S(1)} %collective-permute-done.18.b_ref, bf16[32,2560]{1,0:T(8,128)(2,1)S(1)} %collective-permute-done.19.c_ref, ...), custom_call_target="tpu_custom_call" | custom-call | tf_op jit(solution)/shard_map/pallas_call | solution.py:305
  (29 shorter events, 1.3 us)
Async XLA Ops:
  1.6 51.0 %copy-start = (bf16[256,5120]{1,0:T(8,128)(2,1)S(1)}, bf16[256,5120]{1,0:T(8,128)(2,1)}, u32[]{:S(2)}) copy-start(bf16[256,5120]{1,0:T(8,128)(2,1)} %w_ref.1) | copy-start | bytes 7864324
  1.7 10.9 %all-to-all-start = ((bf16[8,32,512]{2,1,0:T(8,128)(2,1)}), bf16[8,32,512]{2,1,0:T(8,128)(2,1)S(1)}, u32[]{:S(2)}, u32[]{:S(2)}) async-start(bf16[8,32,512]{2,1,0:T(8,128)(2,1)} %shard_map.55), calls=%async_computation | async-start | bytes 524288 | tf_op jit(solution)/shard_map/all_to_all | solution.py:226
  7.8 1.3 %collective-permute-start = (bf16[16,128]{1,0:T(8,128)(2,1)S(1)}, bf16[16,128]{1,0:T(8,128)(2,1)S(1)}, u32[]{:S(2)}, u32[]{:S(2)}) collective-permute-start(bf16[16,128]{1,0:T(8,128)(2,1)S(1)} %broadcast_bitcast_fusion.local_ref), channel_id=1, source_target_pairs={{0,4},{4,0},{1,5},{5,1},{2,6},{6,2},{3,7},{7,3},{8,12},{12,8},{9,1... | collective-permute-start | bytes 12296 | tf_op jit(solution)/shard_map/ppermute | solution.py:27
  12.6 12.6 %collective-permute-start.1 = (bf16[544,128]{1,0:T(8,128)(2,1)S(1)}, bf16[544,128]{1,0:T(8,128)(2,1)S(1)}, u32[]{:S(2)}, u32[]{:S(2)}) collective-permute-start(bf16[544,128]{1,0:T(8,128)(2,1)S(1)} %get-tuple-element.19.refs_0_), channel_id=1, source_target_pairs={{0,16},{4,52},{16,32},{20,4},{32,48},{36,20},{48,0},{52,36},{1,17}... | collective-permute-start | bytes 417800 | tf_op jit(solution)/shard_map/ppermute | solution.py:36
  15.4 7.6 %collective-permute-start.7 = (bf16[256,256]{1,0:T(8,128)(2,1)S(1)}, bf16[256,256]{1,0:T(8,128)(2,1)S(1)}, u32[]{:S(2)}, u32[]{:S(2)}) collective-permute-start(bf16[256,256]{1,0:T(8,128)(2,1)S(1)} %get-tuple-element.20.refs_4_), channel_id=1, source_target_pairs={{0,8},{8,0},{1,9},{9,1},{2,10},{10,2},{3,11},{11,3},{4,12},{12,4},... | collective-permute-start | bytes 393224 | tf_op jit(solution)/shard_map/ppermute | solution.py:27
  17.3 7.9 %collective-permute-start.4 = (bf16[256,256]{1,0:T(8,128)(2,1)S(1)}, bf16[256,256]{1,0:T(8,128)(2,1)S(1)}, u32[]{:S(2)}, u32[]{:S(2)}) collective-permute-start(bf16[256,256]{1,0:T(8,128)(2,1)S(1)} %get-tuple-element.20.refs_4_), channel_id=1, source_target_pairs={{0,64},{64,128},{128,192},{192,0},{1,65},{65,129},{129,193},{193,1... | collective-permute-start | bytes 393224 | tf_op jit(solution)/shard_map/ppermute | solution.py:27
  18.8 9.8 %collective-permute-start.5 = (bf16[256,256]{1,0:T(8,128)(2,1)S(1)}, bf16[256,256]{1,0:T(8,128)(2,1)S(1)}, u32[]{:S(2)}, u32[]{:S(2)}) collective-permute-start(bf16[256,256]{1,0:T(8,128)(2,1)S(1)} %get-tuple-element.20.refs_4_), channel_id=1, source_target_pairs={{0,128},{64,192},{128,0},{192,64},{1,129},{65,193},{129,1},{193,65... | collective-permute-start | bytes 393224 | tf_op jit(solution)/shard_map/ppermute | solution.py:27
  21.5 10.6 %collective-permute-start.6 = (bf16[256,256]{1,0:T(8,128)(2,1)S(1)}, bf16[256,256]{1,0:T(8,128)(2,1)S(1)}, u32[]{:S(2)}, u32[]{:S(2)}) collective-permute-start(bf16[256,256]{1,0:T(8,128)(2,1)S(1)} %get-tuple-element.20.refs_4_), channel_id=1, source_target_pairs={{0,192},{64,0},{128,64},{192,128},{1,193},{65,1},{129,65},{193,129... | collective-permute-start | bytes 393224 | tf_op jit(solution)/shard_map/ppermute | solution.py:27
  22.9 12.1 %collective-permute-start.10 = (bf16[256,256]{1,0:T(8,128)(2,1)S(1)}, bf16[256,256]{1,0:T(8,128)(2,1)S(1)}, u32[]{:S(2)}, u32[]{:S(2)}) collective-permute-start(bf16[256,256]{1,0:T(8,128)(2,1)S(1)} %collective-permute-done.7.refs_8_), channel_id=1, source_target_pairs={{0,192},{64,0},{128,64},{192,128},{1,193},{65,1},{129,65},{193,129... | collective-permute-start | bytes 393224 | tf_op jit(solution)/shard_map/ppermute | solution.py:27
  25.2 10.0 %collective-permute-start.8 = (bf16[256,256]{1,0:T(8,128)(2,1)S(1)}, bf16[256,256]{1,0:T(8,128)(2,1)S(1)}, u32[]{:S(2)}, u32[]{:S(2)}) collective-permute-start(bf16[256,256]{1,0:T(8,128)(2,1)S(1)} %collective-permute-done.7.refs_8_), channel_id=1, source_target_pairs={{0,64},{64,128},{128,192},{192,0},{1,65},{65,129},{129,193},{193,1... | collective-permute-start | bytes 393224 | tf_op jit(solution)/shard_map/ppermute | solution.py:27
  25.2 10.0 %collective-permute-start.9 = (bf16[256,256]{1,0:T(8,128)(2,1)S(1)}, bf16[256,256]{1,0:T(8,128)(2,1)S(1)}, u32[]{:S(2)}, u32[]{:S(2)}) collective-permute-start(bf16[256,256]{1,0:T(8,128)(2,1)S(1)} %collective-permute-done.7.refs_8_), channel_id=1, source_target_pairs={{0,128},{64,192},{128,0},{192,64},{1,129},{65,193},{129,1},{193,65... | collective-permute-start | bytes 393224 | tf_op jit(solution)/shard_map/ppermute | solution.py:27
  28.6 6.5 %collective-permute-start.2 = (bf16[272,128]{1,0:T(8,128)(2,1)S(1)}, bf16[272,128]{1,0:T(8,128)(2,1)S(1)}, u32[]{:S(2)}, u32[]{:S(2)}) collective-permute-start(bf16[272,128]{1,0:T(8,128)(2,1)S(1)} %get-tuple-element.36), channel_id=1, source_target_pairs={{0,16},{4,52},{16,32},{20,4},{32,48},{36,20},{48,0},{52,36},{1,17}... | collective-permute-start | bytes 208904 | tf_op jit(solution)/shard_map/ppermute | solution.py:36
  32.1 3.0 %collective-permute-start.3 = (bf16[272,128]{1,0:T(8,128)(2,1)S(1)}, bf16[272,128]{1,0:T(8,128)(2,1)S(1)}, u32[]{:S(2)}, u32[]{:S(2)}) collective-permute-start(bf16[272,128]{1,0:T(8,128)(2,1)S(1)} %get-tuple-element.35), channel_id=1, source_target_pairs={{0,4},{4,0},{1,5},{5,1},{2,6},{6,2},{3,7},{7,3},{8,12},{12,8},{9,1... | collective-permute-start | bytes 208904 | tf_op jit(solution)/shard_map/ppermute | solution.py:27
  39.0 10.1 %collective-permute-start.11 = (bf16[144,256]{1,0:T(8,128)(2,1)S(1)}, bf16[144,256]{1,0:T(8,128)(2,1)S(1)}, u32[]{:S(2)}, u32[]{:S(2)}) collective-permute-start(bf16[144,256]{1,0:T(8,128)(2,1)S(1)} %get-tuple-element.22), channel_id=1, source_target_pairs={{0,32},{16,48},{32,0},{48,16},{1,33},{17,49},{33,1},{49,17},{2,34}... | collective-permute-start | bytes 221192 | tf_op jit(solution)/shard_map/ppermute | solution.py:27
  42.1 6.9 %collective-permute-start.12 = (bf16[144,256]{1,0:T(8,128)(2,1)S(1)}, bf16[144,256]{1,0:T(8,128)(2,1)S(1)}, u32[]{:S(2)}, u32[]{:S(2)}) collective-permute-start(bf16[144,256]{1,0:T(8,128)(2,1)S(1)} %get-tuple-element.23), channel_id=1, source_target_pairs={{0,16},{16,32},{32,48},{48,0},{1,17},{17,33},{33,49},{49,1},{2,18}... | collective-permute-start | bytes 221192 | tf_op jit(solution)/shard_map/ppermute | solution.py:27
  44.9 6.4 %collective-permute-start.13 = (bf16[144,256]{1,0:T(8,128)(2,1)S(1)}, bf16[144,256]{1,0:T(8,128)(2,1)S(1)}, u32[]{:S(2)}, u32[]{:S(2)}) collective-permute-start(bf16[144,256]{1,0:T(8,128)(2,1)S(1)} %get-tuple-element.24), channel_id=1, source_target_pairs={{0,48},{16,0},{32,16},{48,32},{1,49},{17,1},{33,17},{49,33},{2,50}... | collective-permute-start | bytes 221192 | tf_op jit(solution)/shard_map/ppermute | solution.py:27
  51.4 1.3 %collective-permute-start.14 = (bf16[128,128]{1,0:T(8,128)(2,1)S(1)}, bf16[128,128]{1,0:T(8,128)(2,1)S(1)}, u32[]{:S(2)}, u32[]{:S(2)}) collective-permute-start(bf16[128,128]{1,0:T(8,128)(2,1)S(1)} %get-tuple-element.26), channel_id=1, source_target_pairs={{0,4},{4,0},{1,5},{5,1},{2,6},{6,2},{3,7},{7,3},{8,12},{12,8},{9,1... | collective-permute-start | bytes 98312 | tf_op jit(solution)/shard_map/ppermute | solution.py:27
  54.2 7.1 %collective-permute-start.15 = (bf16[32,2560]{1,0:T(8,128)(2,1)S(1)}, bf16[32,2560]{1,0:T(8,128)(2,1)S(1)}, u32[]{:S(2)}, u32[]{:S(2)}) collective-permute-start(bf16[32,2560]{1,0:T(8,128)(2,1)S(1)} %get-tuple-element.34), channel_id=1, source_target_pairs={{0,1},{1,2},{2,3},{3,0},{4,5},{5,6},{6,7},{7,4},{8,9},{9,10},{10,1... | collective-permute-start | bytes 491528 | tf_op jit(solution)/shard_map/ppermute | solution.py:27
  56.5 8.3 %collective-permute-start.16 = (bf16[32,2560]{1,0:T(8,128)(2,1)S(1)}, bf16[32,2560]{1,0:T(8,128)(2,1)S(1)}, u32[]{:S(2)}, u32[]{:S(2)}) collective-permute-start(bf16[32,2560]{1,0:T(8,128)(2,1)S(1)} %get-tuple-element.33), channel_id=1, source_target_pairs={{0,3},{1,0},{2,1},{3,2},{4,7},{5,4},{6,5},{7,6},{8,11},{9,8},{10,9... | collective-permute-start | bytes 491528 | tf_op jit(solution)/shard_map/ppermute | solution.py:27
  56.5 10.8 %collective-permute-start.18 = (bf16[32,2560]{1,0:T(8,128)(2,1)S(1)}, bf16[32,2560]{1,0:T(8,128)(2,1)S(1)}, u32[]{:S(2)}, u32[]{:S(2)}) collective-permute-start(bf16[32,2560]{1,0:T(8,128)(2,1)S(1)} %slice.22), channel_id=1, source_target_pairs={{0,3},{1,0},{2,1},{3,2},{4,7},{5,4},{6,5},{7,6},{8,11},{9,8},{10,9... | collective-permute-start | bytes 491528 | tf_op jit(solution)/shard_map/ppermute | solution.py:27
  56.9 10.4 %collective-permute-start.19 = (bf16[32,2560]{1,0:T(8,128)(2,1)S(1)}, bf16[32,2560]{1,0:T(8,128)(2,1)S(1)}, u32[]{:S(2)}, u32[]{:S(2)}) collective-permute-start(bf16[32,2560]{1,0:T(8,128)(2,1)S(1)} %slice.23), channel_id=1, source_target_pairs={{0,1},{1,2},{2,3},{3,0},{4,5},{5,6},{6,7},{7,4},{8,9},{9,10},{10,1... | collective-permute-start | bytes 491528 | tf_op jit(solution)/shard_map/ppermute | solution.py:27
  64.8 5.4 %collective-permute-start.17 = (bf16[32,2560]{1,0:T(8,128)(2,1)S(1)}, bf16[32,2560]{1,0:T(8,128)(2,1)S(1)}, u32[]{:S(2)}, u32[]{:S(2)}) collective-permute-start(bf16[32,2560]{1,0:T(8,128)(2,1)S(1)} %get-tuple-element.31), channel_id=1, source_target_pairs={{0,1},{1,2},{2,3},{3,0},{4,5},{5,6},{6,7},{7,4},{8,9},{9,10},{10,1... | collective-permute-start | bytes 491528 | tf_op jit(solution)/shard_map/ppermute | solution.py:27
  64.9 6.6 %collective-permute-start.20 = (bf16[32,2560]{1,0:T(8,128)(2,1)S(1)}, bf16[32,2560]{1,0:T(8,128)(2,1)S(1)}, u32[]{:S(2)}, u32[]{:S(2)}) collective-permute-start(bf16[32,2560]{1,0:T(8,128)(2,1)S(1)} %get-tuple-element.32), channel_id=1, source_target_pairs={{0,3},{1,0},{2,1},{3,2},{4,7},{5,4},{6,5},{7,6},{8,11},{9,8},{10,9... | collective-permute-start | bytes 491528 | tf_op jit(solution)/shard_map/ppermute | solution.py:27

commit v4 on v0

v4 whole, which is shorter than its diff:
```python
import functools
import math

import jax
import jax.numpy as jnp
from jax import lax
from jax.experimental import pallas as pl
from jax.experimental.pallas import tpu as pltpu
from jax.sharding import Mesh, PartitionSpec as P

HD = 128
BLK = 128
NX, NH, NL, NC, NY = 4, 4, 2, 2, 4
AXES = ("x", "zh", "zl", "c", "y")
SIZES = (NX, NH, NL, NC, NY)
BF = jnp.bfloat16
F32 = jnp.float32
SCALE2 = math.log2(math.e) / math.sqrt(HD)
NEG = -1e30
BIG = 1e30
VMEM = pl.BlockSpec(memory_space=pltpu.VMEM)
PARAMS = pltpu.CompilerParams(vmem_limit_bytes=40 * 2**20)


def moved(value, axis, by):
    size = SIZES[AXES.index(axis)]
    return lax.ppermute(value, axis, [(i, (i + by) % size) for i in range(size)])


def swapped(value, axis, mask):
    size = SIZES[AXES.index(axis)]
    return lax.ppermute(value, axis, [(i, i ^ mask) for i in range(size)])


def swapped_by_core(value, axis, masks):
    size = SIZES[AXES.index(axis)]
    pairs = [(i * NC + c, (i ^ masks[c]) * NC + c) for i in range(size) for c in range(NC)]
    return lax.ppermute(value, (axis, "c"), pairs)


def prep_kernel(q_ref, k_ref, v_ref, mask_ref, *refs):
    out_refs, marks_ref, held_ref, seen_ref, sem = refs[:4], *refs[4:]
    y, c = lax.axis_index("y"), lax.axis_index("c")
    copies = [
        pltpu.make_async_copy(ref, held_ref.at[i], sem.at[i])
        for i, ref in enumerate((q_ref, k_ref, v_ref))
    ]
    copies.append(pltpu.make_async_copy(mask_ref, seen_ref, sem.at[3]))
    for copy in copies:
        copy.start()
    copies.pop().wait()
    seen = seen_ref[:, 0, :].astype(F32)
    seen = jnp.concatenate([seen, jnp.zeros_like(seen)], axis=1)
    low = lax.broadcasted_iota(jnp.int32, (16, HD), 0) < 8
    marks_ref[...] = jnp.where(low, seen[0:1], seen[1:2]).astype(BF)
    for i, copy in enumerate(copies):
        copy.wait()
        for mask, out_ref in enumerate(out_refs):
            for mate in range(2):
                head = (y ^ mask) * 2 + (c ^ mate)
                cols = pl.ds(pl.multiple_of(head * HD, HD), HD)
                slot = mate if i == 0 else 1 + 2 * mate + i
                out_ref[:, slot * HD : (slot + 1) * HD] = held_ref[i, :, cols]


def pack_kernel(marks_ref, *refs):
    piece_refs, (mine_ref, send_ref) = refs[:4], refs[4:]
    for mask, ref in enumerate(piece_refs):
        rows = slice(mask * 32, (mask + 1) * 32)
        mine_ref[rows, :] = ref[:, : 4 * HD]
        send_ref[rows, :HD] = ref[:, HD : 2 * HD]
        send_ref[rows, HD : 2 * HD] = ref[:, :HD]
        send_ref[rows, 2 * HD :] = ref[:, 4 * HD :]
    for ref in (mine_ref, send_ref):
        for slot in range(4):
            ref[BLK:, slot * HD : (slot + 1) * HD] = marks_ref[...]


def mid_kernel(mine_ref, got_ref, q_ref, kv_ref):
    for core in range(NC):

        @pl.when(lax.axis_index("c") == core)
        def _():
            for part, ref in enumerate((mine_ref, got_ref)):
                row = (core ^ part) * BLK
                q_ref[row : row + BLK, :] = ref[:BLK, :HD]
                q_ref[272 + row : 272 + row + BLK, :] = ref[:BLK, HD : 2 * HD]
                kv_ref[row : row + BLK, :] = ref[:BLK, 2 * HD :]
            marks = [ref[BLK:, :HD].astype(F32) for ref in (mine_ref, got_ref)]
            low = lax.broadcasted_iota(jnp.int32, (16, HD), 0) < 8
            for mate in range(2):
                row = (core ^ mate) * 8
                both = [marks[core][row : row + 1], marks[1 - core][row : row + 1]]
                q_ref[256 + 272 * mate : 272 + 272 * mate, :] = jnp.where(low, *both).astype(BF)


def attend_kernel(count, merging, *refs):
    q_refs, kv_refs = refs[:count], refs[count : count + 8]
    met_ref = refs[count + 8] if merging else None
    refs = refs[count + 8 + merging :]
    out_refs, (vt_ref, s_ref, p_ref, open_ref) = refs[:count], refs[count:]
    x, zh, zl = (lax.axis_index(a) for a in ("x", "zh", "zl"))
    for i in range(8):
        vt_ref[:, i * 256 : (i + 1) * 256] = kv_refs[i][:, HD:].T
    masks = [ref[256:272, :] for ref in q_refs]
    masks = jnp.concatenate(masks, axis=0) if count > 1 else masks[0]
    row = lax.broadcasted_iota(jnp.int32, (16 * count, 256 * count), 0)
    block = lax.broadcasted_iota(jnp.int32, (16 * count, 256 * count), 1) // BLK
    pick = jnp.where(row == block * 8, 1.0, 0.0).astype(BF)
    open_ref[...] = lax.dot_general(
        masks, pick, (((0,), (0,)), ((), ())), preferred_element_type=F32
    )

    def score(j):
        q = q_refs[j][:256, :]
        opens = []
        top = jnp.full((1, 256), NEG, F32)
        for i in range(8):
            source = (x ^ (i % 4)) * 16 + zh * 4 + (zl ^ (i // 4)) * 2
            s = lax.dot_general(
                kv_refs[i][:, :HD], q, (((1,), (1,)), ((), ())), preferred_element_type=F32
            )
            s_ref[j % 2, i * 256 : (i + 1) * 256, :] = s
            for part in range(2):
                is_open = open_ref[pl.ds(source + part, 1), j * 256 : (j + 1) * 256] > 0.5
                opens.append(is_open)
                here = jnp.max(s[part * BLK : (part + 1) * BLK], axis=0, keepdims=True)
                top = jnp.maximum(top, jnp.where(is_open, here, NEG))
        return opens, top * SCALE2

    following = score(0)
    for j in range(count):
        opens, top = following
        if j < count - 1:
            following = score(j + 1)
        sums = jnp.zeros((8, 256), F32)
        for b in range(16):
            less = jnp.where(opens[b], top, BIG)
            rows = slice(b * BLK, (b + 1) * BLK)
            w = jnp.exp2(s_ref[j % 2, rows, :] * SCALE2 - less)
            sums += jnp.sum(w.reshape(16, 8, 256), axis=0)
            p_ref[j % 2, rows, :] = w.astype(BF)
        total = jnp.sum(sums, axis=0, keepdims=True)
        acc = jnp.dot(vt_ref[...], p_ref[j % 2], preferred_element_type=F32)
        some = total > 0.0
        safe = jnp.where(some, total, 1.0)
        acc = acc / safe
        lse = jnp.where(some, top + jnp.log2(safe), NEG)
        if merging:
            tail = met_ref[HD:, :].astype(F32)
            met = tail[0:1] + tail[1:2] + tail[2:3]
            top = jnp.maximum(lse, met)
            mine, theirs = jnp.exp2(lse - top), jnp.exp2(met - top)
            total = mine + theirs
            acc = acc * (mine / total) + met_ref[:HD, :].astype(F32) * (theirs / total)
            lse = top + jnp.log2(total)
        out_refs[j][:HD, :] = acc.astype(BF)
        out_refs[j][HD:, :] = packed_tail(lse)


def packed_tail(lse):
    hi = lse.astype(BF).astype(F32)
    mid = (lse - hi).astype(BF).astype(F32)
    row = lax.broadcasted_iota(jnp.int32, (16, lse.shape[1]), 0)
    return jnp.where(row == 0, hi, jnp.where(row == 1, mid, lse - hi - mid)).astype(BF)


def merged(parts):
    lses = []
    for part in parts:
        tail = part[HD:, :].astype(F32)
        lses.append(tail[0:1] + tail[1:2] + tail[2:3])
    top = functools.reduce(jnp.maximum, lses)
    ws = [jnp.exp2(lse - top) for lse in lses]
    total = sum(ws)
    inv = 1.0 / total
    acc = sum(part[:HD, :].astype(F32) * (w * inv) for part, w in zip(parts, ws))
    return acc.astype(BF), top + jnp.log2(total)


def join_kernel(a_ref, b_ref, out_ref):
    out_ref[:144, :] = a_ref[...]
    out_ref[144:, :] = b_ref[...]


def share_kernel(own_ref, side_ref, send_ref):
    for core in range(NC):

        @pl.when(lax.axis_index("c") == core)
        def _():
            cols = slice((1 - core) * BLK, (2 - core) * BLK)
            acc, lse = merged([own_ref[:, cols], side_ref[:144, cols]])
            send_ref[:HD, :] = acc
            send_ref[HD:144, :] = packed_tail(lse)
            send_ref[144:, :] = side_ref[144:, cols]


def project_kernel(own_ref, side_ref, got_ref, w_ref, *refs):
    out_refs, lhs_ref = refs[:4], refs[4]
    for core in range(NC):

        @pl.when(lax.axis_index("c") == core)
        def _():
            cols = slice(core * BLK, (core + 1) * BLK)
            mine = [own_ref[:, cols], side_ref[:144, cols], got_ref[144:]]
            mate = [side_ref[144:, cols], got_ref[:144]]
            lhs_ref[:, core * HD : (core + 1) * HD] = merged(mine)[0].T
            lhs_ref[:, (1 - core) * HD : (2 - core) * HD] = merged(mate)[0].T

    lhs = lhs_ref[...]
    for start in range(0, w_ref.shape[1], 512):
        cols = slice(start, start + 512)
        out = jnp.dot(lhs, w_ref[:, cols], preferred_element_type=F32).astype(BF)
        for p in range(NY):
            out_refs[p][:, cols] = out[p * 32 : (p + 1) * 32]


def pass_kernel(one_ref, three_ref, a_ref, b_ref, by_one_ref, by_three_ref):
    half = a_ref.shape[1]
    by_one_ref[...] = (one_ref[:, half:].astype(F32) + b_ref[...].astype(F32)).astype(BF)
    by_three_ref[...] = (three_ref[:, :half].astype(F32) + a_ref[...].astype(F32)).astype(BF)


def sum_kernel(own_ref, a_ref, b_ref, c_ref, d_ref, out_ref, total_ref, sem):
    half = a_ref.shape[1]
    step = half // 2
    copies = []
    for i, (one, two) in enumerate(((c_ref, d_ref), (a_ref, b_ref))):
        base = half * (1 - i)
        for start in range(0, half, step):
            cols = slice(start, start + step)
            spot = slice(base + start, base + start + step)
            total = own_ref[:, spot].astype(F32) + one[:, cols].astype(F32)
            total_ref[:, spot] = (total + two[:, cols].astype(F32)).astype(BF)
            there = out_ref.at[:, pl.ds(base + start, step)]
            here = total_ref.at[:, pl.ds(base + start, step)]
            copies.append(pltpu.make_async_copy(here, there, sem.at[len(copies)]))
            copies[-1].start()
    for copy in copies:
        copy.wait()


def shape(*dims, dtype=BF):
    return jax.ShapeDtypeStruct(dims, dtype)


def attend(qs, kvs, met=None):
    count, merging = len(qs), met is not None
    return pl.pallas_call(
        functools.partial(attend_kernel, count, merging),
        out_shape=tuple(shape(144, 256) for _ in range(count)),
        in_specs=[VMEM] * (count + 8 + merging),
        out_specs=(VMEM,) * count,
        scratch_shapes=[
            pltpu.VMEM((HD, 2048), BF),
            pltpu.VMEM((2, 2048, 256), F32),
            pltpu.VMEM((2, 2048, 256), BF),
            pltpu.VMEM((HD, 256 * count), F32),
        ],
        compiler_params=PARAMS,
        cost_estimate=pl.CostEstimate(
            flops=2 * 2 * 256 * count * 2048 * HD * 8,
            bytes_accessed=2**21,
            transcendentals=2**19 * count,
        ),
    )(*qs, *kvs, *([met] if merging else []))


def body(queries, keys, values, block_mask, out_weight):
    *pieces, marks = pl.pallas_call(
        prep_kernel,
        out_shape=tuple(shape(32, 768) for _ in range(4)) + (shape(16, HD),),
        in_specs=[pl.BlockSpec(memory_space=pl.ANY)] * 4,
        out_specs=(VMEM,) * 5,
        scratch_shapes=[
            pltpu.VMEM((3, 32, 1024), BF),
            pltpu.VMEM(block_mask.shape, jnp.int32),
            pltpu.SemaphoreType.DMA((4,)),
        ],
        compiler_params=PARAMS,
    )(*(pltpu.with_memory_space_constraint(t, pltpu.HBM) for t in (queries, keys, values, block_mask)))
    met = {m: swapped(pieces[m], "y", m) for m in (2, 3, 1)}
    mine, send = pl.pallas_call(
        pack_kernel,
        out_shape=(shape(144, 512), shape(144, 512)),
        in_specs=[VMEM] * 5,
        out_specs=(VMEM, VMEM),
        compiler_params=PARAMS,
    )(marks, pieces[0], met[1], met[2], met[3])
    got = moved(send, "c", 1)
    q, kv = pl.pallas_call(
        mid_kernel,
        out_shape=(shape(544, HD), shape(256, 256)),
        in_specs=[VMEM] * 2,
        out_specs=(VMEM, VMEM),
        compiler_params=PARAMS,
    )(mine, got)

    pair = swapped(kv, "zl", 1)
    near = [swapped(kv, "x", m) for m in (1, 3, 2)]
    far = [swapped(pair, "x", m) for m in (1, 3, 2)]
    kvs = [kv, near[0], near[2], near[1], pair, far[0], far[2], far[1]]
    first = swapped_by_core(q, "zh", (1, 3))
    across = swapped_by_core(first[:272], "zh", (3, 1))
    second = moved(first[272:], "c", 1)
    qs = [q, first, across, second]

    across, give = attend((across, first), kvs)
    across = swapped(across, "zh", 2)
    took = moved(give, "c", 1)
    (keep,) = attend((second,), kvs)
    joined = pl.pallas_call(
        join_kernel,
        out_shape=shape(288, 256),
        in_specs=[VMEM] * 2,
        out_specs=VMEM,
        compiler_params=PARAMS,
    )(keep, took)
    side = swapped_by_core(joined, "zh", (3, 1))
    (own,) = attend((q,), kvs, across)
    send = pl.pallas_call(
        share_kernel,
        out_shape=shape(288, BLK),
        in_specs=[VMEM] * 2,
        out_specs=VMEM,
        compiler_params=PARAMS,
    )(own, side)
    got = moved(send, "c", 1)

    width = out_weight.shape[1]
    pieces = pl.pallas_call(
        project_kernel,
        out_shape=tuple(shape(32, width) for _ in range(4)),
        in_specs=[VMEM] * 4,
        out_specs=(VMEM,) * 4,
        scratch_shapes=[pltpu.VMEM((BLK, 2 * HD), BF)],
        compiler_params=PARAMS,
        cost_estimate=pl.CostEstimate(
            flops=2 * 128 * 256 * width, bytes_accessed=2**22, transcendentals=0
        ),
    )(own, side, got, out_weight)
    own, one, two, three = pieces
    half = width // 2
    b = swapped(two[:, half:], "y", 3)
    a = swapped(two[:, :half], "y", 1)
    right_three = swapped(three[:, half:], "y", 3)
    left_one = swapped(one[:, :half], "y", 1)
    by_one, by_three = pl.pallas_call(
        pass_kernel,
        out_shape=(shape(32, half), shape(32, half)),
        in_specs=[VMEM] * 4,
        out_specs=(VMEM, VMEM),
        compiler_params=PARAMS,
    )(one, three, a, b)
    left_three = swapped(by_three, "y", 3)
    right_one = swapped(by_one, "y", 1)
    return pl.pallas_call(
        sum_kernel,
        out_shape=shape(32, width),
        in_specs=[VMEM] * 5,
        out_specs=pl.BlockSpec(memory_space=pl.ANY),
        scratch_shapes=[pltpu.VMEM((32, width), BF), pltpu.SemaphoreType.DMA((4,))],
        compiler_params=PARAMS,
    )(own, left_one, left_three, right_one, right_three)


def solution(mesh):
    grid = Mesh(mesh.devices.reshape(SIZES), AXES)
    rows = P(AXES, None)
    in_specs = (rows, rows, rows, P("y", AXES[:4], None), P("y", None))
    return jax.shard_map(body, mesh=grid, in_specs=in_specs, out_specs=rows, check_vma=False)
```

time: 222 us -> 69.8 us (0.31)
  waiting for transfers between devices: 152 us -> 29.3 us
  starting transfers between devices: 3.37 us -> 32.7 us
  local copies, waits for them, and re-layouts: 19.2 us -> 0.06 us
  blocking collectives: 18.6 us -> 0 us
  between operations: 13.2 us -> 0.33 us
  matrix products: 12 us -> 0 us
  Pallas kernels: 0 us -> 7.06 us
  other arithmetic: 2.62 us -> 0 us
    all_gather x2 -> x0, waiting for transfers between devices: 123 us -> none  [the longest x1 63.6 us: body(): v_piece = lax.all_gather(local_v, 'seq', axis=0, tiled=True)]
    ppermute x0 -> x24, starting transfers between devices: none -> 32.7 us  [the longest x17 24.7 us: swapped(): return lax.ppermute(value, axis, [(i, i ^ mask) for i in range(size)])]
    ppermute x0 -> x24, waiting for transfers between devices: none -> 29.3 us  [the longest x17 20.4 us: swapped(): return lax.ppermute(value, axis, [(i, i ^ mask) for i in range(size)])]
    reduce_scatter x1 -> x0, waiting for transfers between devices: 25.3 us -> none  [body(): lax.psum_scatter(jnp.dot(attn_rows, out_weight, preferred_element_type=jn...]
    all_to_all x2 -> x0, blocking collectives: 18.6 us -> none  [the longest x1 9.98 us: body(): lax.all_to_all(keys, 'head', split_axis=1, concat_axis=0, tiled=True)]
    all_gather x2 -> x0, local copies, waits for them, and re-layouts: 12.7 us -> none  [the longest x1 6.36 us: body(): k_piece = lax.all_gather(local_k, 'seq', axis=0, tiled=True)]
    dot_general x4 -> x0, matrix products: 12 us -> none  [the longest x1 5.97 us: body(): jnp.einsum('hqk,khd->qhd', weights.astype(jnp.bfloat16), v_three, preferr...]
    pallas_call x0 -> x11, Pallas kernels: none -> 7.06 us  [the longest x3 4.49 us: attend(): pl.pallas_call(functools.partial(attend_kernel, count, merging), out_shap...]
  transfers between devices with their start and end apart: 4 -> 24, of which waited for: 4 -> 14; matrix products, arithmetic and copies ran while one was open for 7% -> 0% of each run, Pallas kernels for 0% -> 7%
where the time goes in v4:
time: 69.8 us; the launch traced here: 69.5 us
  starting transfers between devices  32.7 us (47%)
  waiting for transfers between devices  29.3 us (42%)
  Pallas kernels  7.06 us (10%)
    ppermute x17, starting transfers between devices, swapped(): return lax.ppermute(value, axis, [(i, i ^ mask) for i in range(size)])  24.7 us
    ppermute x17, waiting for transfers between devices, swapped(): return lax.ppermute(value, axis, [(i, i ^ mask) for i in range(size)])  20.4 us
    ppermute x3, starting transfers between devices, swapped_by_core(): return lax.ppermute(value, (axis, 'c'), pairs)  7.15 us
    ppermute x3, waiting for transfers between devices, swapped_by_core(): return lax.ppermute(value, (axis, 'c'), pairs)  6.35 us
    pallas_call x3, Pallas kernels, attend(): pl.pallas_call(functools.partial(attend_kernel, count, merging), out_shap...  4.49 us
    ppermute x4, waiting for transfers between devices, moved(): lax.ppermute(value, axis, [(i, (i + by) % size) for i in range(size)])  2.62 us
  transfers between devices with their start and end apart: 24, of which 14 were waited for; matrix products, arithmetic and copies ran while one was open for 0% of the time, Pallas kernels for 7%

profile of v4, /device:TPU:32, one launch (start us, length us, event | category | flops | bytes accessed | tf_op | source)
XLA Modules:
  0.0 69.5 jit_solution(6818047032749220449)
XLA Ops:
  0.0 1.0 %shard_map.55 = (bf16[32,768]{1,0:T(8,128)(2,1)S(1)}, bf16[32,768]{1,0:T(8,128)(2,1)S(1)}, bf16[32,768]{1,0:T(8,128)(2,1)S(1)}, bf16[32,768]{1,0:T(8,128)(2,1)S(1)}, bf16[16,128]{1,0:T(8,128)(2,1)S(1)}) custom-call(bf16[32,1024]{1,0:T(8,128)(2,1)} %q_ref.1, bf16[32,1024]{1,0:T(8,128)(2,1)} %k_ref.1, bf16[32,1024]{1,0:T(8,128)(2,1)} %v_ref.1, ...), custom_call_target="tpu_custom_call" | custom-call | tf_op jit(solution)/shard_map/pallas_call | solution.py:270
  1.0 1.7 %collective-permute-start = (bf16[32,768]{1,0:T(8,128)(2,1)S(1)}, bf16[32,768]{1,0:T(8,128)(2,1)S(1)}, u32[]{:S(2)}, u32[]{:S(2)}) collective-permute-start(bf16[32,768]{1,0:T(8,128)(2,1)S(1)} %get-tuple-element.24), channel_id=1, source_target_pairs={{0,1},{1,0},{2,3},{3,2},{4,5},{5,4},{6,7},{7,6},{8,9},{9,8},{10,11... | collective-permute-start | bytes 147464 | tf_op jit(solution)/shard_map/ppermute | solution.py:32
  2.6 2.9 %collective-permute-start.1 = (bf16[32,768]{1,0:T(8,128)(2,1)S(1)}, bf16[32,768]{1,0:T(8,128)(2,1)S(1)}, u32[]{:S(2)}, u32[]{:S(2)}) collective-permute-start(bf16[32,768]{1,0:T(8,128)(2,1)S(1)} %get-tuple-element.25), channel_id=1, source_target_pairs={{0,2},{1,3},{2,0},{3,1},{4,6},{5,7},{6,4},{7,5},{8,10},{9,11},{10,... | collective-permute-start | bytes 147464 | tf_op jit(solution)/shard_map/ppermute | solution.py:32
  5.8 2.5 %collective-permute-done.1.refs_2_ = bf16[32,768]{1,0:T(8,128)(2,1)S(1)} collective-permute-done((bf16[32,768]{1,0:T(8,128)(2,1)S(1)}, bf16[32,768]{1,0:T(8,128)(2,1)S(1)}, u32[]{:S(2)}, u32[]{:S(2)}) %collective-permute-start.1) | collective-permute-done | bytes 49184 | tf_op jit(solution)/shard_map/ppermute | solution.py:32
  8.2 2.6 %collective-permute-done.2.refs_3_ = bf16[32,768]{1,0:T(8,128)(2,1)S(1)} collective-permute-done((bf16[32,768]{1,0:T(8,128)(2,1)S(1)}, bf16[32,768]{1,0:T(8,128)(2,1)S(1)}, u32[]{:S(2)}, u32[]{:S(2)}) %collective-permute-start.2) | collective-permute-done | bytes 49184 | tf_op jit(solution)/shard_map/ppermute | solution.py:32
  11.0 1.4 %collective-permute-done.3.got_ref = bf16[144,512]{1,0:T(8,128)(2,1)S(1)} collective-permute-done((bf16[144,512]{1,0:T(8,128)(2,1)S(1)}, bf16[144,512]{1,0:T(8,128)(2,1)S(1)}, u32[]{:S(2)}, u32[]{:S(2)}) %collective-permute-start.3) | collective-permute-done | bytes 147488 | tf_op jit(solution)/shard_map/ppermute | solution.py:27
  12.4 3.4 %collective-permute-start.11 = (bf16[544,128]{1,0:T(8,128)(2,1)S(1)}, bf16[544,128]{1,0:T(8,128)(2,1)S(1)}, u32[]{:S(2)}, u32[]{:S(2)}) collective-permute-start(bf16[544,128]{1,0:T(8,128)(2,1)S(1)} %get-tuple-element.29.refs_0_), channel_id=1, source_target_pairs={{0,16},{4,52},{16,0},{20,36},{32,48},{36,20},{48,32},{52,4},{1,17}... | collective-permute-start | bytes 417800 | tf_op jit(solution)/shard_map/ppermute | solution.py:38
  15.8 1.5 %collective-permute-start.4 = (bf16[256,256]{1,0:T(8,128)(2,1)S(1)}, bf16[256,256]{1,0:T(8,128)(2,1)S(1)}, u32[]{:S(2)}, u32[]{:S(2)}) collective-permute-start(bf16[256,256]{1,0:T(8,128)(2,1)S(1)} %get-tuple-element.30.refs_2_.refs_1_), channel_id=1, source_target_pairs={{0,64},{64,0},{128,192},{192,128},{1,65},{65,1},{129,193},{193,129... | collective-permute-start | bytes 393224 | tf_op jit(solution)/shard_map/ppermute | solution.py:32
  17.3 2.7 %collective-permute-start.5 = (bf16[256,256]{1,0:T(8,128)(2,1)S(1)}, bf16[256,256]{1,0:T(8,128)(2,1)S(1)}, u32[]{:S(2)}, u32[]{:S(2)}) collective-permute-start(bf16[256,256]{1,0:T(8,128)(2,1)S(1)} %get-tuple-element.30.refs_2_.refs_1_), channel_id=1, source_target_pairs={{0,128},{64,192},{128,0},{192,64},{1,129},{65,193},{129,1},{193,65... | collective-permute-start | bytes 393224 | tf_op jit(solution)/shard_map/ppermute | solution.py:32
  20.5 1.7 %collective-permute-done.7.refs_6_.refs_5_ = bf16[256,256]{1,0:T(8,128)(2,1)S(1)} collective-permute-done((bf16[256,256]{1,0:T(8,128)(2,1)S(1)}, bf16[256,256]{1,0:T(8,128)(2,1)S(1)}, u32[]{:S(2)}, u32[]{:S(2)}) %collective-permute-start.7) | collective-permute-done | bytes 131104 | tf_op jit(solution)/shard_map/ppermute | solution.py:32
  22.3 2.8 %collective-permute-start.10 = (bf16[256,256]{1,0:T(8,128)(2,1)S(1)}, bf16[256,256]{1,0:T(8,128)(2,1)S(1)}, u32[]{:S(2)}, u32[]{:S(2)}) collective-permute-start(bf16[256,256]{1,0:T(8,128)(2,1)S(1)} %collective-permute-done.7.refs_6_.refs_5_), channel_id=1, source_target_pairs={{0,192},{64,128},{128,64},{192,0},{1,193},{65,129},{129,65},{193,1... | collective-permute-start | bytes 393224 | tf_op jit(solution)/shard_map/ppermute | solution.py:32
  25.2 1.7 %collective-permute-start.9 = (bf16[256,256]{1,0:T(8,128)(2,1)S(1)}, bf16[256,256]{1,0:T(8,128)(2,1)S(1)}, u32[]{:S(2)}, u32[]{:S(2)}) collective-permute-start(bf16[256,256]{1,0:T(8,128)(2,1)S(1)} %collective-permute-done.7.refs_6_.refs_5_), channel_id=1, source_target_pairs={{0,128},{64,192},{128,0},{192,64},{1,129},{65,193},{129,1},{193,65... | collective-permute-start | bytes 393224 | tf_op jit(solution)/shard_map/ppermute | solution.py:32
  27.0 3.5 %collective-permute-start.12 = (bf16[272,128]{1,0:T(8,128)(2,1)S(1)}, bf16[272,128]{1,0:T(8,128)(2,1)S(1)}, u32[]{:S(2)}, u32[]{:S(2)}) collective-permute-start(bf16[272,128]{1,0:T(8,128)(2,1)S(1)} %get-tuple-element.42), channel_id=1, source_target_pairs={{0,48},{4,20},{16,32},{20,4},{32,16},{36,52},{48,0},{52,36},{1,49}... | collective-permute-start | bytes 208904 | tf_op jit(solution)/shard_map/ppermute | solution.py:38
  30.5 3.0 %collective-permute-done.12.refs_0_ = bf16[272,128]{1,0:T(8,128)(2,1)S(1)} collective-permute-done((bf16[272,128]{1,0:T(8,128)(2,1)S(1)}, bf16[272,128]{1,0:T(8,128)(2,1)S(1)}, u32[]{:S(2)}, u32[]{:S(2)}) %collective-permute-start.12) | collective-permute-done | bytes 69664 | tf_op jit(solution)/shard_map/ppermute | solution.py:38
  33.5 0.8 %collective-permute-done.10.refs_9_.refs_8_ = bf16[256,256]{1,0:T(8,128)(2,1)S(1)} collective-permute-done((bf16[256,256]{1,0:T(8,128)(2,1)S(1)}, bf16[256,256]{1,0:T(8,128)(2,1)S(1)}, u32[]{:S(2)}, u32[]{:S(2)}) %collective-permute-start.10) | collective-permute-done | bytes 131104 | tf_op jit(solution)/shard_map/ppermute | solution.py:32
  34.3 1.8 %shard_map.58 = (bf16[144,256]{1,0:T(8,128)(2,1)S(1)}, bf16[144,256]{1,0:T(8,128)(2,1)S(1)}) custom-call(bf16[272,128]{1,0:T(8,128)(2,1)S(1)} %collective-permute-done.12.refs_0_, bf16[544,128]{1,0:T(8,128)(2,1)S(1)} %collective-permute-done.11.refs_1_, bf16[256,256]{1,0:T(8,128)(2,1)S(1)} %get-tuple-element.30.refs_2_.refs_1_, ...), custom_call_target="tpu_custom_call" | custom-call | flops 4294967296 | bytes 2097152 | tf_op jit(solution)/shard_map/pallas_call | solution.py:249
  36.1 0.6 collective-permute-start.15
  36.7 4.6 %collective-permute-start.13 = (bf16[144,256]{1,0:T(8,128)(2,1)S(1)}, bf16[144,256]{1,0:T(8,128)(2,1)S(1)}, u32[]{:S(2)}, u32[]{:S(2)}) collective-permute-start(bf16[144,256]{1,0:T(8,128)(2,1)S(1)} %get-tuple-element.31), channel_id=1, source_target_pairs={{0,32},{16,48},{32,0},{48,16},{1,33},{17,49},{33,1},{49,17},{2,34}... | collective-permute-start | bytes 221192 | tf_op jit(solution)/shard_map/ppermute | solution.py:32
  41.3 1.3 %shard_map.60.a_ref = bf16[144,256]{1,0:T(8,128)(2,1)S(1)} custom-call(bf16[272,128]{1,0:T(8,128)(2,1)S(1)} %collective-permute-done.14.refs_0_, bf16[256,256]{1,0:T(8,128)(2,1)S(1)} %get-tuple-element.30.refs_2_.refs_1_, bf16[256,256]{1,0:T(8,128)(2,1)S(1)} %collective-permute-done.4.refs_3_.refs_2_, ...), custom_call_target="tpu_custom_call" | custom-call | flops 2147483648 | bytes 2097152 | tf_op jit(solution)/shard_map/pallas_call | solution.py:249
  43.0 3.6 %collective-permute-done.13.refs_9_ = bf16[144,256]{1,0:T(8,128)(2,1)S(1)} collective-permute-done((bf16[144,256]{1,0:T(8,128)(2,1)S(1)}, bf16[144,256]{1,0:T(8,128)(2,1)S(1)}, u32[]{:S(2)}, u32[]{:S(2)}) %collective-permute-start.13) | collective-permute-done | bytes 73760 | tf_op jit(solution)/shard_map/ppermute | solution.py:32
  46.6 1.3 %shard_map.59.own_ref = bf16[144,256]{1,0:T(8,128)(2,1)S(1)} custom-call(bf16[544,128]{1,0:T(8,128)(2,1)S(1)} %get-tuple-element.29.refs_0_, bf16[256,256]{1,0:T(8,128)(2,1)S(1)} %get-tuple-element.30.refs_2_.refs_1_, bf16[256,256]{1,0:T(8,128)(2,1)S(1)} %collective-permute-done.4.refs_3_.refs_2_, ...), custom_call_target="tpu_custom_call" | custom-call | flops 2147483648 | bytes 2097152 | tf_op jit(solution)/shard_map/pallas_call | solution.py:249
  47.9 3.4 %collective-permute-done.16.side_ref = bf16[288,256]{1,0:T(8,128)(2,1)S(1)} collective-permute-done((bf16[288,256]{1,0:T(8,128)(2,1)S(1)}, bf16[288,256]{1,0:T(8,128)(2,1)S(1)}, u32[]{:S(2)}, u32[]{:S(2)}) %collective-permute-start.16) | collective-permute-done | bytes 147488 | tf_op jit(solution)/shard_map/ppermute | solution.py:38
  51.5 1.3 %collective-permute-done.17.got_ref = bf16[288,128]{1,0:T(8,128)(2,1)S(1)} collective-permute-done((bf16[288,128]{1,0:T(8,128)(2,1)S(1)}, bf16[288,128]{1,0:T(8,128)(2,1)S(1)}, u32[]{:S(2)}, u32[]{:S(2)}) %collective-permute-start.17) | collective-permute-done | bytes 73760 | tf_op jit(solution)/shard_map/ppermute | solution.py:27
  53.5 0.9 %collective-permute-start.20 = (bf16[32,2560]{1,0:T(8,128)(2,1)S(1)}, bf16[32,2560]{1,0:T(8,128)(2,1)S(1)}, u32[]{:S(2)}, u32[]{:S(2)}) collective-permute-start(bf16[32,2560]{1,0:T(8,128)(2,1)S(1)} %get-tuple-element.39), channel_id=1, source_target_pairs={{0,3},{1,2},{2,1},{3,0},{4,7},{5,6},{6,5},{7,4},{8,11},{9,10},{10,... | collective-permute-start | bytes 491528 | tf_op jit(solution)/shard_map/ppermute | solution.py:32
  54.4 1.2 %collective-permute-start.18 = (bf16[32,2560]{1,0:T(8,128)(2,1)S(1)}, bf16[32,2560]{1,0:T(8,128)(2,1)S(1)}, u32[]{:S(2)}, u32[]{:S(2)}) collective-permute-start(bf16[32,2560]{1,0:T(8,128)(2,1)S(1)} %slice.20), channel_id=1, source_target_pairs={{0,1},{1,0},{2,3},{3,2},{4,5},{5,4},{6,7},{7,6},{8,9},{9,8},{10,11... | collective-permute-start | bytes 491528 | tf_op jit(solution)/shard_map/ppermute | solution.py:32
  55.6 2.7 %collective-permute-start.23 = (bf16[32,2560]{1,0:T(8,128)(2,1)S(1)}, bf16[32,2560]{1,0:T(8,128)(2,1)S(1)}, u32[]{:S(2)}, u32[]{:S(2)}) collective-permute-start(bf16[32,2560]{1,0:T(8,128)(2,1)S(1)} %slice.23), channel_id=1, source_target_pairs={{0,3},{1,2},{2,1},{3,0},{4,7},{5,6},{6,5},{7,4},{8,11},{9,10},{10,... | collective-permute-start | bytes 491528 | tf_op jit(solution)/shard_map/ppermute | solution.py:32
  58.3 2.2 %collective-permute-done.19.a_ref = bf16[32,2560]{1,0:T(8,128)(2,1)S(1)} collective-permute-done((bf16[32,2560]{1,0:T(8,128)(2,1)S(1)}, bf16[32,2560]{1,0:T(8,128)(2,1)S(1)}, u32[]{:S(2)}, u32[]{:S(2)}) %collective-permute-start.19) | collective-permute-done | bytes 163872 | tf_op jit(solution)/shard_map/ppermute | solution.py:32
  60.5 1.3 %collective-permute-done.20.b_ref = bf16[32,2560]{1,0:T(8,128)(2,1)S(1)} collective-permute-done((bf16[32,2560]{1,0:T(8,128)(2,1)S(1)}, bf16[32,2560]{1,0:T(8,128)(2,1)S(1)}, u32[]{:S(2)}, u32[]{:S(2)}) %collective-permute-start.20) | collective-permute-done | bytes 163872 | tf_op jit(solution)/shard_map/ppermute | solution.py:32
  62.0 0.8 %collective-permute-start.22 = (bf16[32,2560]{1,0:T(8,128)(2,1)S(1)}, bf16[32,2560]{1,0:T(8,128)(2,1)S(1)}, u32[]{:S(2)}, u32[]{:S(2)}) collective-permute-start(bf16[32,2560]{1,0:T(8,128)(2,1)S(1)} %get-tuple-element.38), channel_id=1, source_target_pairs={{0,1},{1,0},{2,3},{3,2},{4,5},{5,4},{6,7},{7,6},{8,9},{9,8},{10,11... | collective-permute-start | bytes 491528 | tf_op jit(solution)/shard_map/ppermute | solution.py:32
  63.2 1.5 %collective-permute-done.23.d_ref = bf16[32,2560]{1,0:T(8,128)(2,1)S(1)} collective-permute-done((bf16[32,2560]{1,0:T(8,128)(2,1)S(1)}, bf16[32,2560]{1,0:T(8,128)(2,1)S(1)}, u32[]{:S(2)}, u32[]{:S(2)}) %collective-permute-start.23) | collective-permute-done | bytes 163872 | tf_op jit(solution)/shard_map/ppermute | solution.py:32
  64.7 3.8 %collective-permute-done.21.b_ref = bf16[32,2560]{1,0:T(8,128)(2,1)S(1)} collective-permute-done((bf16[32,2560]{1,0:T(8,128)(2,1)S(1)}, bf16[32,2560]{1,0:T(8,128)(2,1)S(1)}, u32[]{:S(2)}, u32[]{:S(2)}) %collective-permute-start.21) | collective-permute-done | bytes 163872 | tf_op jit(solution)/shard_map/ppermute | solution.py:32
  68.5 0.8 %shard_map.65 = bf16[32,5120]{1,0:T(8,128)(2,1)} custom-call(bf16[32,5120]{1,0:T(8,128)(2,1)S(1)} %get-tuple-element.33.own_ref, bf16[32,2560]{1,0:T(8,128)(2,1)S(1)} %collective-permute-done.18.a_ref, bf16[32,2560]{1,0:T(8,128)(2,1)S(1)} %collective-permute-done.21.b_ref, bf16[32,2560]{1,0:T(8,128)(2,1)S(1)} %collective-permute-done.22.c_ref, ...), custom_call_target="tpu_custom_call" | custom-call | tf_op jit(solution)/shard_map/pallas_call | solution.py:357
  (33 shorter events, 3.0 us)
Async XLA Ops:
  1.0 4.8 %collective-permute-start = (bf16[32,768]{1,0:T(8,128)(2,1)S(1)}, bf16[32,768]{1,0:T(8,128)(2,1)S(1)}, u32[]{:S(2)}, u32[]{:S(2)}) collective-permute-start(bf16[32,768]{1,0:T(8,128)(2,1)S(1)} %get-tuple-element.24), channel_id=1, source_target_pairs={{0,1},{1,0},{2,3},{3,2},{4,5},{5,4},{6,7},{7,6},{8,9},{9,8},{10,11... | collective-permute-start | bytes 147464 | tf_op jit(solution)/shard_map/ppermute | solution.py:32
  2.6 5.6 %collective-permute-start.1 = (bf16[32,768]{1,0:T(8,128)(2,1)S(1)}, bf16[32,768]{1,0:T(8,128)(2,1)S(1)}, u32[]{:S(2)}, u32[]{:S(2)}) collective-permute-start(bf16[32,768]{1,0:T(8,128)(2,1)S(1)} %get-tuple-element.25), channel_id=1, source_target_pairs={{0,2},{1,3},{2,0},{3,1},{4,6},{5,7},{6,4},{7,5},{8,10},{9,11},{10,... | collective-permute-start | bytes 147464 | tf_op jit(solution)/shard_map/ppermute | solution.py:32
  5.5 5.3 %collective-permute-start.2 = (bf16[32,768]{1,0:T(8,128)(2,1)S(1)}, bf16[32,768]{1,0:T(8,128)(2,1)S(1)}, u32[]{:S(2)}, u32[]{:S(2)}) collective-permute-start(bf16[32,768]{1,0:T(8,128)(2,1)S(1)} %get-tuple-element.26), channel_id=1, source_target_pairs={{0,3},{1,2},{2,1},{3,0},{4,7},{5,6},{6,5},{7,4},{8,11},{9,10},{10,... | collective-permute-start | bytes 147464 | tf_op jit(solution)/shard_map/ppermute | solution.py:32
  10.9 1.5 %collective-permute-start.3 = (bf16[144,512]{1,0:T(8,128)(2,1)S(1)}, bf16[144,512]{1,0:T(8,128)(2,1)S(1)}, u32[]{:S(2)}, u32[]{:S(2)}) collective-permute-start(bf16[144,512]{1,0:T(8,128)(2,1)S(1)} %get-tuple-element.28), channel_id=1, source_target_pairs={{0,4},{4,0},{1,5},{5,1},{2,6},{6,2},{3,7},{7,3},{8,12},{12,8},{9,1... | collective-permute-start | bytes 442376 | tf_op jit(solution)/shard_map/ppermute | solution.py:27
  12.4 12.9 %collective-permute-start.11 = (bf16[544,128]{1,0:T(8,128)(2,1)S(1)}, bf16[544,128]{1,0:T(8,128)(2,1)S(1)}, u32[]{:S(2)}, u32[]{:S(2)}) collective-permute-start(bf16[544,128]{1,0:T(8,128)(2,1)S(1)} %get-tuple-element.29.refs_0_), channel_id=1, source_target_pairs={{0,16},{4,52},{16,0},{20,36},{32,48},{36,20},{48,32},{52,4},{1,17}... | collective-permute-start | bytes 417800 | tf_op jit(solution)/shard_map/ppermute | solution.py:38
  15.7 6.5 %collective-permute-start.7 = (bf16[256,256]{1,0:T(8,128)(2,1)S(1)}, bf16[256,256]{1,0:T(8,128)(2,1)S(1)}, u32[]{:S(2)}, u32[]{:S(2)}) collective-permute-start(bf16[256,256]{1,0:T(8,128)(2,1)S(1)} %get-tuple-element.30.refs_2_.refs_1_), channel_id=1, source_target_pairs={{0,8},{8,0},{1,9},{9,1},{2,10},{10,2},{3,11},{11,3},{4,12},{12,4},... | collective-permute-start | bytes 393224 | tf_op jit(solution)/shard_map/ppermute | solution.py:32
  15.8 9.2 %collective-permute-start.4 = (bf16[256,256]{1,0:T(8,128)(2,1)S(1)}, bf16[256,256]{1,0:T(8,128)(2,1)S(1)}, u32[]{:S(2)}, u32[]{:S(2)}) collective-permute-start(bf16[256,256]{1,0:T(8,128)(2,1)S(1)} %get-tuple-element.30.refs_2_.refs_1_), channel_id=1, source_target_pairs={{0,64},{64,0},{128,192},{192,128},{1,65},{65,1},{129,193},{193,129... | collective-permute-start | bytes 393224 | tf_op jit(solution)/shard_map/ppermute | solution.py:32
  17.3 9.7 %collective-permute-start.5 = (bf16[256,256]{1,0:T(8,128)(2,1)S(1)}, bf16[256,256]{1,0:T(8,128)(2,1)S(1)}, u32[]{:S(2)}, u32[]{:S(2)}) collective-permute-start(bf16[256,256]{1,0:T(8,128)(2,1)S(1)} %get-tuple-element.30.refs_2_.refs_1_), channel_id=1, source_target_pairs={{0,128},{64,192},{128,0},{192,64},{1,129},{65,193},{129,1},{193,65... | collective-permute-start | bytes 393224 | tf_op jit(solution)/shard_map/ppermute | solution.py:32
  20.0 10.5 %collective-permute-start.6 = (bf16[256,256]{1,0:T(8,128)(2,1)S(1)}, bf16[256,256]{1,0:T(8,128)(2,1)S(1)}, u32[]{:S(2)}, u32[]{:S(2)}) collective-permute-start(bf16[256,256]{1,0:T(8,128)(2,1)S(1)} %get-tuple-element.30.refs_2_.refs_1_), channel_id=1, source_target_pairs={{0,192},{64,128},{128,64},{192,0},{1,193},{65,129},{129,65},{193,1... | collective-permute-start | bytes 393224 | tf_op jit(solution)/shard_map/ppermute | solution.py:32
  22.3 12.0 %collective-permute-start.10 = (bf16[256,256]{1,0:T(8,128)(2,1)S(1)}, bf16[256,256]{1,0:T(8,128)(2,1)S(1)}, u32[]{:S(2)}, u32[]{:S(2)}) collective-permute-start(bf16[256,256]{1,0:T(8,128)(2,1)S(1)} %collective-permute-done.7.refs_6_.refs_5_), channel_id=1, source_target_pairs={{0,192},{64,128},{128,64},{192,0},{1,193},{65,129},{129,65},{193,1... | collective-permute-start | bytes 393224 | tf_op jit(solution)/shard_map/ppermute | solution.py:32
  25.0 9.2 %collective-permute-start.8 = (bf16[256,256]{1,0:T(8,128)(2,1)S(1)}, bf16[256,256]{1,0:T(8,128)(2,1)S(1)}, u32[]{:S(2)}, u32[]{:S(2)}) collective-permute-start(bf16[256,256]{1,0:T(8,128)(2,1)S(1)} %collective-permute-done.7.refs_6_.refs_5_), channel_id=1, source_target_pairs={{0,64},{64,0},{128,192},{192,128},{1,65},{65,1},{129,193},{193,129... | collective-permute-start | bytes 393224 | tf_op jit(solution)/shard_map/ppermute | solution.py:32
  25.2 9.0 %collective-permute-start.9 = (bf16[256,256]{1,0:T(8,128)(2,1)S(1)}, bf16[256,256]{1,0:T(8,128)(2,1)S(1)}, u32[]{:S(2)}, u32[]{:S(2)}) collective-permute-start(bf16[256,256]{1,0:T(8,128)(2,1)S(1)} %collective-permute-done.7.refs_6_.refs_5_), channel_id=1, source_target_pairs={{0,128},{64,192},{128,0},{192,64},{1,129},{65,193},{129,1},{193,65... | collective-permute-start | bytes 393224 | tf_op jit(solution)/shard_map/ppermute | solution.py:32
  27.0 6.5 %collective-permute-start.12 = (bf16[272,128]{1,0:T(8,128)(2,1)S(1)}, bf16[272,128]{1,0:T(8,128)(2,1)S(1)}, u32[]{:S(2)}, u32[]{:S(2)}) collective-permute-start(bf16[272,128]{1,0:T(8,128)(2,1)S(1)} %get-tuple-element.42), channel_id=1, source_target_pairs={{0,48},{4,20},{16,32},{20,4},{32,16},{36,52},{48,0},{52,36},{1,49}... | collective-permute-start | bytes 208904 | tf_op jit(solution)/shard_map/ppermute | solution.py:38
  30.5 10.8 %collective-permute-start.14 = (bf16[272,128]{1,0:T(8,128)(2,1)S(1)}, bf16[272,128]{1,0:T(8,128)(2,1)S(1)}, u32[]{:S(2)}, u32[]{:S(2)}) collective-permute-start(bf16[272,128]{1,0:T(8,128)(2,1)S(1)} %get-tuple-element.41), channel_id=1, source_target_pairs={{0,4},{4,0},{1,5},{5,1},{2,6},{6,2},{3,7},{7,3},{8,12},{12,8},{9,1... | collective-permute-start | bytes 208904 | tf_op jit(solution)/shard_map/ppermute | solution.py:27
  36.1 6.6 %collective-permute-start.15 = (bf16[144,256]{1,0:T(8,128)(2,1)S(1)}, bf16[144,256]{1,0:T(8,128)(2,1)S(1)}, u32[]{:S(2)}, u32[]{:S(2)}) collective-permute-start(bf16[144,256]{1,0:T(8,128)(2,1)S(1)} %get-tuple-element.32), channel_id=1, source_target_pairs={{0,4},{4,0},{1,5},{5,1},{2,6},{6,2},{3,7},{7,3},{8,12},{12,8},{9,1... | collective-permute-start | bytes 221192 | tf_op jit(solution)/shard_map/ppermute | solution.py:27
  36.7 9.9 %collective-permute-start.13 = (bf16[144,256]{1,0:T(8,128)(2,1)S(1)}, bf16[144,256]{1,0:T(8,128)(2,1)S(1)}, u32[]{:S(2)}, u32[]{:S(2)}) collective-permute-start(bf16[144,256]{1,0:T(8,128)(2,1)S(1)} %get-tuple-element.31), channel_id=1, source_target_pairs={{0,32},{16,48},{32,0},{48,16},{1,33},{17,49},{33,1},{49,17},{2,34}... | collective-permute-start | bytes 221192 | tf_op jit(solution)/shard_map/ppermute | solution.py:32
  42.7 10.0 %copy-start = (bf16[256,5120]{1,0:T(8,128)(2,1)S(1)}, bf16[256,5120]{1,0:T(8,128)(2,1)}, u32[]{:S(2)}) copy-start(bf16[256,5120]{1,0:T(8,128)(2,1)} %w_ref.1) | copy-start | bytes 7864324
  42.7 8.6 %collective-permute-start.16 = (bf16[288,256]{1,0:T(8,128)(2,1)S(1)}, bf16[288,256]{1,0:T(8,128)(2,1)S(1)}, u32[]{:S(2)}, u32[]{:S(2)}) collective-permute-start(bf16[288,256]{1,0:T(8,128)(2,1)S(1)} %shard_map.61), channel_id=1, source_target_pairs={{0,48},{4,20},{16,32},{20,4},{32,16},{36,52},{48,0},{52,36},{1,49}... | collective-permute-start | bytes 442376 | tf_op jit(solution)/shard_map/ppermute | solution.py:38
  51.4 1.4 %collective-permute-start.17 = (bf16[288,128]{1,0:T(8,128)(2,1)S(1)}, bf16[288,128]{1,0:T(8,128)(2,1)S(1)}, u32[]{:S(2)}, u32[]{:S(2)}) collective-permute-start(bf16[288,128]{1,0:T(8,128)(2,1)S(1)} %shard_map.62), channel_id=1, source_target_pairs={{0,4},{4,0},{1,5},{5,1},{2,6},{6,2},{3,7},{7,3},{8,12},{12,8},{9,1... | collective-permute-start | bytes 221192 | tf_op jit(solution)/shard_map/ppermute | solution.py:27
  53.4 7.1 %collective-permute-start.19 = (bf16[32,2560]{1,0:T(8,128)(2,1)S(1)}, bf16[32,2560]{1,0:T(8,128)(2,1)S(1)}, u32[]{:S(2)}, u32[]{:S(2)}) collective-permute-start(bf16[32,2560]{1,0:T(8,128)(2,1)S(1)} %get-tuple-element.40), channel_id=1, source_target_pairs={{0,1},{1,0},{2,3},{3,2},{4,5},{5,4},{6,7},{7,6},{8,9},{9,8},{10,11... | collective-permute-start | bytes 491528 | tf_op jit(solution)/shard_map/ppermute | solution.py:32
  53.5 8.3 %collective-permute-start.20 = (bf16[32,2560]{1,0:T(8,128)(2,1)S(1)}, bf16[32,2560]{1,0:T(8,128)(2,1)S(1)}, u32[]{:S(2)}, u32[]{:S(2)}) collective-permute-start(bf16[32,2560]{1,0:T(8,128)(2,1)S(1)} %get-tuple-element.39), channel_id=1, source_target_pairs={{0,3},{1,2},{2,1},{3,0},{4,7},{5,6},{6,5},{7,4},{8,11},{9,10},{10,... | collective-permute-start | bytes 491528 | tf_op jit(solution)/shard_map/ppermute | solution.py:32
  54.4 8.8 %collective-permute-start.18 = (bf16[32,2560]{1,0:T(8,128)(2,1)S(1)}, bf16[32,2560]{1,0:T(8,128)(2,1)S(1)}, u32[]{:S(2)}, u32[]{:S(2)}) collective-permute-start(bf16[32,2560]{1,0:T(8,128)(2,1)S(1)} %slice.20), channel_id=1, source_target_pairs={{0,1},{1,0},{2,3},{3,2},{4,5},{5,4},{6,7},{7,6},{8,9},{9,8},{10,11... | collective-permute-start | bytes 491528 | tf_op jit(solution)/shard_map/ppermute | solution.py:32
  55.6 9.1 %collective-permute-start.23 = (bf16[32,2560]{1,0:T(8,128)(2,1)S(1)}, bf16[32,2560]{1,0:T(8,128)(2,1)S(1)}, u32[]{:S(2)}, u32[]{:S(2)}) collective-permute-start(bf16[32,2560]{1,0:T(8,128)(2,1)S(1)} %slice.23), channel_id=1, source_target_pairs={{0,3},{1,2},{2,1},{3,0},{4,7},{5,6},{6,5},{7,4},{8,11},{9,10},{10,... | collective-permute-start | bytes 491528 | tf_op jit(solution)/shard_map/ppermute | solution.py:32
  61.9 6.6 %collective-permute-start.21 = (bf16[32,2560]{1,0:T(8,128)(2,1)S(1)}, bf16[32,2560]{1,0:T(8,128)(2,1)S(1)}, u32[]{:S(2)}, u32[]{:S(2)}) collective-permute-start(bf16[32,2560]{1,0:T(8,128)(2,1)S(1)} %get-tuple-element.37), channel_id=1, source_target_pairs={{0,3},{1,2},{2,1},{3,0},{4,7},{5,6},{6,5},{7,4},{8,11},{9,10},{10,... | collective-permute-start | bytes 491528 | tf_op jit(solution)/shard_map/ppermute | solution.py:32
  62.0 6.5 %collective-permute-start.22 = (bf16[32,2560]{1,0:T(8,128)(2,1)S(1)}, bf16[32,2560]{1,0:T(8,128)(2,1)S(1)}, u32[]{:S(2)}, u32[]{:S(2)}) collective-permute-start(bf16[32,2560]{1,0:T(8,128)(2,1)S(1)} %get-tuple-element.38), channel_id=1, source_target_pairs={{0,1},{1,0},{2,3},{3,2},{4,5},{5,4},{6,7},{7,6},{8,9},{9,8},{10,11... | collective-permute-start | bytes 491528 | tf_op jit(solution)/shard_map/ppermute | solution.py:32

commit v5 on v4

--- a/solution.py
+++ b/solution.py
@@ -94,14 +94,17 @@
                 q_ref[256 + 272 * mate : 272 + 272 * mate, :] = jnp.where(low, *both).astype(BF)
 
 
-def attend_kernel(count, merging, *refs):
-    q_refs, kv_refs = refs[:count], refs[count : count + 8]
-    met_ref = refs[count + 8] if merging else None
-    refs = refs[count + 8 + merging :]
-    out_refs, (vt_ref, s_ref, p_ref, open_ref) = refs[:count], refs[count:]
+def attend_kernel(count, chunks, early, merging, *refs):
+    refs = list(refs)
+    q_refs = [refs.pop(0) for _ in range(count)]
+    kv_refs = [refs.pop(0) for _ in chunks]
+    before = [] if early else [(refs.pop(0), refs.pop(0)) for _ in range(count)]
+    met_ref = refs.pop(0) if merging else None
+    out_refs = [refs.pop(0) for _ in range(count * (1 + early))]
+    vt_ref, s_ref, p_ref, open_ref = refs
     x, zh, zl = (lax.axis_index(a) for a in ("x", "zh", "zl"))
-    for i in range(8):
-        vt_ref[:, i * 256 : (i + 1) * 256] = kv_refs[i][:, HD:].T
+    for i, ref in enumerate(kv_refs):
+        vt_ref[:, i * 256 : (i + 1) * 256] = ref[:, HD:].T
     masks = [ref[256:272, :] for ref in q_refs]
     masks = jnp.concatenate(masks, axis=0) if count > 1 else masks[0]
     row = lax.broadcasted_iota(jnp.int32, (16 * count, 256 * count), 0)
@@ -115,8 +118,8 @@
         q = q_refs[j][:256, :]
         opens = []
         top = jnp.full((1, 256), NEG, F32)
-        for i in range(8):
-            source = (x ^ (i % 4)) * 16 + zh * 4 + (zl ^ (i // 4)) * 2
+        for i, chunk in enumerate(chunks):
+            source = (x ^ (chunk % 4)) * 16 + zh * 4 + (zl ^ (chunk // 4)) * 2
             s = lax.dot_general(
                 kv_refs[i][:, :HD], q, (((1,), (1,)), ((), ())), preferred_element_type=F32
             )
@@ -134,7 +137,7 @@
         if j < count - 1:
             following = score(j + 1)
         sums = jnp.zeros((8, 256), F32)
-        for b in range(16):
+        for b in range(2 * len(chunks)):
             less = jnp.where(opens[b], top, BIG)
             rows = slice(b * BLK, (b + 1) * BLK)
             w = jnp.exp2(s_ref[j % 2, rows, :] * SCALE2 - less)
@@ -142,6 +145,17 @@
             p_ref[j % 2, rows, :] = w.astype(BF)
         total = jnp.sum(sums, axis=0, keepdims=True)
         acc = jnp.dot(vt_ref[...], p_ref[j % 2], preferred_element_type=F32)
+        if early:
+            row = lax.broadcasted_iota(jnp.int32, (8, 256), 0)
+            out_refs[2 * j][...] = acc
+            out_refs[2 * j + 1][...] = jnp.where(row == 0, top, total)
+            continue
+        acc_ref, stat_ref = before[j]
+        top0, total0 = stat_ref[0:1, :], stat_ref[1:2, :]
+        both = jnp.maximum(top, top0)
+        keep, keep0 = jnp.exp2(top - both), jnp.exp2(top0 - both)
+        acc = acc * keep + acc_ref[...] * keep0
+        top, total = both, total * keep + total0 * keep0
         some = total > 0.0
         safe = jnp.where(some, total, 1.0)
         acc = acc / safe
@@ -244,26 +258,37 @@
     return jax.ShapeDtypeStruct(dims, dtype)
 
 
-def attend(qs, kvs, met=None):
-    count, merging = len(qs), met is not None
+EARLY, LATE = (4, 0, 2, 1, 3), (5, 7, 6)
+
+
+def attend(qs, kvs, before=None, met=None):
+    count, early, merging = len(qs), before is None, met is not None
+    chunks = EARLY if early else LATE
+    keys = 256 * len(chunks)
+    outs = (shape(144, 256),)
+    if early:
+        outs = (shape(HD, 256, dtype=F32), shape(8, 256, dtype=F32))
+    operands = [*qs, *(kvs[i] for i in chunks)]
+    operands += [] if early else [part for pair in before for part in pair]
+    operands += [met] if merging else []
     return pl.pallas_call(
-        functools.partial(attend_kernel, count, merging),
-        out_shape=tuple(shape(144, 256) for _ in range(count)),
-        in_specs=[VMEM] * (count + 8 + merging),
-        out_specs=(VMEM,) * count,
+        functools.partial(attend_kernel, count, chunks, early, merging),
+        out_shape=outs * count,
+        in_specs=[VMEM] * len(operands),
+        out_specs=(VMEM,) * (len(outs) * count),
         scratch_shapes=[
-            pltpu.VMEM((HD, 2048), BF),
-            pltpu.VMEM((2, 2048, 256), F32),
-            pltpu.VMEM((2, 2048, 256), BF),
+            pltpu.VMEM((HD, keys), BF),
+            pltpu.VMEM((2, keys, 256), F32),
+            pltpu.VMEM((2, keys, 256), BF),
             pltpu.VMEM((HD, 256 * count), F32),
         ],
         compiler_params=PARAMS,
         cost_estimate=pl.CostEstimate(
-            flops=2 * 2 * 256 * count * 2048 * HD * 8,
+            flops=2 * 2 * 256 * count * keys * HD * 8,
             bytes_accessed=2**21,
-            transcendentals=2**19 * count,
+            transcendentals=256 * count * keys,
         ),
-    )(*qs, *kvs, *([met] if merging else []))
+    )(*operands)
 
 
 def body(queries, keys, values, block_mask, out_weight):
@@ -297,18 +322,20 @@
     )(mine, got)
 
     pair = swapped(kv, "zl", 1)
-    near = [swapped(kv, "x", m) for m in (1, 3, 2)]
-    far = [swapped(pair, "x", m) for m in (1, 3, 2)]
-    kvs = [kv, near[0], near[2], near[1], pair, far[0], far[2], far[1]]
+    near = {m: swapped(kv, "x", m) for m in (2, 1, 3)}
+    far = {m: swapped(pair, "x", m) for m in (1, 3)}
+    far[2] = swapped(near[2], "zl", 1)
+    kvs = [kv, near[1], near[2], near[3], pair, far[1], far[2], far[3]]
     first = swapped_by_core(q, "zh", (1, 3))
     across = swapped_by_core(first[:272], "zh", (3, 1))
     second = moved(first[272:], "c", 1)
-    qs = [q, first, across, second]
-
-    across, give = attend((across, first), kvs)
+
+    raw = attend((q, first, second, across), kvs)
+    raw = [raw[2 * i : 2 * i + 2] for i in (3, 1, 2, 0)]
+    across, give = attend((across, first), kvs, raw[:2])
     across = swapped(across, "zh", 2)
     took = moved(give, "c", 1)
-    (keep,) = attend((second,), kvs)
+    (keep,) = attend((second,), kvs, raw[2:3])
     joined = pl.pallas_call(
         join_kernel,
         out_shape=shape(288, 256),
@@ -317,7 +344,7 @@
         compiler_params=PARAMS,
     )(keep, took)
     side = swapped_by_core(joined, "zh", (3, 1))
-    (own,) = attend((q,), kvs, across)
+    (own,) = attend((q,), kvs, raw[3:], across)
     send = pl.pallas_call(
         share_kernel,
         out_shape=shape(288, BLK),

time: 69.8 us -> 67.1 us (0.961)
  waiting for transfers between devices: 29.3 us -> 24.2 us
  starting transfers between devices: 32.7 us -> 35.9 us
    ppermute x3, starting transfers between devices: 7.15 us -> 10.5 us  [swapped_by_core(): return lax.ppermute(value, (axis, 'c'), pairs)]
    ppermute x17, waiting for transfers between devices: 20.4 us -> 17.5 us  [swapped(): return lax.ppermute(value, axis, [(i, i ^ mask) for i in range(size)])]
    ppermute x3, waiting for transfers between devices: 6.35 us -> 4.12 us  [swapped_by_core(): return lax.ppermute(value, (axis, 'c'), pairs)]
    ppermute x17, starting transfers between devices: 24.7 us -> 23 us  [swapped(): return lax.ppermute(value, axis, [(i, i ^ mask) for i in range(size)])]
    ppermute x4, starting transfers between devices: 0.84 us -> 2.41 us  [moved(): lax.ppermute(value, axis, [(i, (i + by) % size) for i in range(size)])]
    pallas_call x3 -> x4, Pallas kernels: 4.49 us -> 3.93 us  [attend(): pl.pallas_call(functools.partial(attend_kernel, count, chunks, early, mer...]
  transfers between devices with their start and end apart: 24 -> 24, of which waited for: 14 -> 14; matrix products, arithmetic and copies ran while one was open for 0% -> 0% of each run, Pallas kernels for 7% -> 5%
where the time goes in v5:
time: 67.1 us; the launch traced here: 67 us
  starting transfers between devices  35.9 us (54%)
  waiting for transfers between devices  24.2 us (36%)
  Pallas kernels  6.49 us (10%)
    ppermute x17, starting transfers between devices, swapped(): return lax.ppermute(value, axis, [(i, i ^ mask) for i in range(size)])  23 us
    ppermute x17, waiting for transfers between devices, swapped(): return lax.ppermute(value, axis, [(i, i ^ mask) for i in range(size)])  17.5 us
    ppermute x3, starting transfers between devices, swapped_by_core(): return lax.ppermute(value, (axis, 'c'), pairs)  10.5 us
    ppermute x3, waiting for transfers between devices, swapped_by_core(): return lax.ppermute(value, (axis, 'c'), pairs)  4.12 us
    pallas_call x4, Pallas kernels, attend(): pl.pallas_call(functools.partial(attend_kernel, count, chunks, early, mer...  3.93 us
    ppermute x4, waiting for transfers between devices, moved(): lax.ppermute(value, axis, [(i, (i + by) % size) for i in range(size)])  2.62 us
    ppermute x4, starting transfers between devices, moved(): lax.ppermute(value, axis, [(i, (i + by) % size) for i in range(size)])  2.41 us
  transfers between devices with their start and end apart: 24, of which 14 were waited for; matrix products, arithmetic and copies ran while one was open for 0% of the time, Pallas kernels for 5%

profile of v5, /device:TPU:32, one launch (start us, length us, event | category | flops | bytes accessed | tf_op | source)
XLA Modules:
  0.0 67.0 jit_solution(11711668681668187690)
XLA Ops:
  0.0 1.0 %shard_map.55 = (bf16[32,768]{1,0:T(8,128)(2,1)S(1)}, bf16[32,768]{1,0:T(8,128)(2,1)S(1)}, bf16[32,768]{1,0:T(8,128)(2,1)S(1)}, bf16[32,768]{1,0:T(8,128)(2,1)S(1)}, bf16[16,128]{1,0:T(8,128)(2,1)S(1)}) custom-call(bf16[32,1024]{1,0:T(8,128)(2,1)} %q_ref.1, bf16[32,1024]{1,0:T(8,128)(2,1)} %k_ref.1, bf16[32,1024]{1,0:T(8,128)(2,1)} %v_ref.1, ...), custom_call_target="tpu_custom_call" | custom-call | tf_op jit(solution)/shard_map/pallas_call | solution.py:295
  1.0 1.7 %collective-permute-start = (bf16[32,768]{1,0:T(8,128)(2,1)S(1)}, bf16[32,768]{1,0:T(8,128)(2,1)S(1)}, u32[]{:S(2)}, u32[]{:S(2)}) collective-permute-start(bf16[32,768]{1,0:T(8,128)(2,1)S(1)} %get-tuple-element.32), channel_id=1, source_target_pairs={{0,1},{1,0},{2,3},{3,2},{4,5},{5,4},{6,7},{7,6},{8,9},{9,8},{10,11... | collective-permute-start | bytes 147464 | tf_op jit(solution)/shard_map/ppermute | solution.py:32
  2.6 2.9 %collective-permute-start.1 = (bf16[32,768]{1,0:T(8,128)(2,1)S(1)}, bf16[32,768]{1,0:T(8,128)(2,1)S(1)}, u32[]{:S(2)}, u32[]{:S(2)}) collective-permute-start(bf16[32,768]{1,0:T(8,128)(2,1)S(1)} %get-tuple-element.33), channel_id=1, source_target_pairs={{0,2},{1,3},{2,0},{3,1},{4,6},{5,7},{6,4},{7,5},{8,10},{9,11},{10,... | collective-permute-start | bytes 147464 | tf_op jit(solution)/shard_map/ppermute | solution.py:32
  5.8 2.5 %collective-permute-done.1.refs_2_ = bf16[32,768]{1,0:T(8,128)(2,1)S(1)} collective-permute-done((bf16[32,768]{1,0:T(8,128)(2,1)S(1)}, bf16[32,768]{1,0:T(8,128)(2,1)S(1)}, u32[]{:S(2)}, u32[]{:S(2)}) %collective-permute-start.1) | collective-permute-done | bytes 49184 | tf_op jit(solution)/shard_map/ppermute | solution.py:32
  8.2 2.6 %collective-permute-done.2.refs_3_ = bf16[32,768]{1,0:T(8,128)(2,1)S(1)} collective-permute-done((bf16[32,768]{1,0:T(8,128)(2,1)S(1)}, bf16[32,768]{1,0:T(8,128)(2,1)S(1)}, u32[]{:S(2)}, u32[]{:S(2)}) %collective-permute-start.2) | collective-permute-done | bytes 49184 | tf_op jit(solution)/shard_map/ppermute | solution.py:32
  11.0 1.4 %collective-permute-done.3.got_ref = bf16[144,512]{1,0:T(8,128)(2,1)S(1)} collective-permute-done((bf16[144,512]{1,0:T(8,128)(2,1)S(1)}, bf16[144,512]{1,0:T(8,128)(2,1)S(1)}, u32[]{:S(2)}, u32[]{:S(2)}) %collective-permute-start.3) | collective-permute-done | bytes 147488 | tf_op jit(solution)/shard_map/ppermute | solution.py:27
  12.4 3.4 %collective-permute-start.9 = (bf16[544,128]{1,0:T(8,128)(2,1)S(1)}, bf16[544,128]{1,0:T(8,128)(2,1)S(1)}, u32[]{:S(2)}, u32[]{:S(2)}) collective-permute-start(bf16[544,128]{1,0:T(8,128)(2,1)S(1)} %get-tuple-element.37.refs_0_), channel_id=1, source_target_pairs={{0,16},{4,52},{16,0},{20,36},{32,48},{36,20},{48,32},{52,4},{1,17}... | collective-permute-start | bytes 417800 | tf_op jit(solution)/shard_map/ppermute | solution.py:38
  15.8 3.0 %collective-permute-start.7 = (bf16[256,256]{1,0:T(8,128)(2,1)S(1)}, bf16[256,256]{1,0:T(8,128)(2,1)S(1)}, u32[]{:S(2)}, u32[]{:S(2)}) collective-permute-start(bf16[256,256]{1,0:T(8,128)(2,1)S(1)} %get-tuple-element.38.refs_5_), channel_id=1, source_target_pairs={{0,128},{64,192},{128,0},{192,64},{1,129},{65,193},{129,1},{193,65... | collective-permute-start | bytes 393224 | tf_op jit(solution)/shard_map/ppermute | solution.py:32
  20.0 2.1 %collective-permute-start.10 = (bf16[272,128]{1,0:T(8,128)(2,1)S(1)}, bf16[272,128]{1,0:T(8,128)(2,1)S(1)}, u32[]{:S(2)}, u32[]{:S(2)}) collective-permute-start(bf16[272,128]{1,0:T(8,128)(2,1)S(1)} %get-tuple-element.58), channel_id=1, source_target_pairs={{0,4},{4,0},{1,5},{5,1},{2,6},{6,2},{3,7},{7,3},{8,12},{12,8},{9,1... | collective-permute-start | bytes 208904 | tf_op jit(solution)/shard_map/ppermute | solution.py:27
  22.3 3.4 %collective-permute-start.11 = (bf16[272,128]{1,0:T(8,128)(2,1)S(1)}, bf16[272,128]{1,0:T(8,128)(2,1)S(1)}, u32[]{:S(2)}, u32[]{:S(2)}) collective-permute-start(bf16[272,128]{1,0:T(8,128)(2,1)S(1)} %get-tuple-element.57), channel_id=1, source_target_pairs={{0,48},{4,20},{16,32},{20,4},{32,16},{36,52},{48,0},{52,36},{1,49}... | collective-permute-start | bytes 208904 | tf_op jit(solution)/shard_map/ppermute | solution.py:38
  25.7 1.5 %collective-permute-start.5 = (bf16[256,256]{1,0:T(8,128)(2,1)S(1)}, bf16[256,256]{1,0:T(8,128)(2,1)S(1)}, u32[]{:S(2)}, u32[]{:S(2)}) collective-permute-start(bf16[256,256]{1,0:T(8,128)(2,1)S(1)} %collective-permute-done.4.refs_4_), channel_id=1, source_target_pairs={{0,64},{64,0},{128,192},{192,128},{1,65},{65,1},{129,193},{193,129... | collective-permute-start | bytes 393224 | tf_op jit(solution)/shard_map/ppermute | solution.py:32
  27.2 2.1 %collective-permute-start.6 = (bf16[256,256]{1,0:T(8,128)(2,1)S(1)}, bf16[256,256]{1,0:T(8,128)(2,1)S(1)}, u32[]{:S(2)}, u32[]{:S(2)}) collective-permute-start(bf16[256,256]{1,0:T(8,128)(2,1)S(1)} %collective-permute-done.4.refs_4_), channel_id=1, source_target_pairs={{0,192},{64,128},{128,64},{192,0},{1,193},{65,129},{129,65},{193,1... | collective-permute-start | bytes 393224 | tf_op jit(solution)/shard_map/ppermute | solution.py:32
  29.3 1.8 %collective-permute-start.8 = (bf16[256,256]{1,0:T(8,128)(2,1)S(1)}, bf16[256,256]{1,0:T(8,128)(2,1)S(1)}, u32[]{:S(2)}, u32[]{:S(2)}) collective-permute-start(bf16[256,256]{1,0:T(8,128)(2,1)S(1)} %collective-permute-done.7.refs_6_), channel_id=1, source_target_pairs={{0,8},{8,0},{1,9},{9,1},{2,10},{10,2},{3,11},{11,3},{4,12},{12,4},... | collective-permute-start | bytes 393224 | tf_op jit(solution)/shard_map/ppermute | solution.py:32
  31.1 1.8 %shard_map.58 = (f32[128,256]{1,0:T(8,128)S(1)}, f32[8,256]{1,0:T(8,128)S(1)}, f32[128,256]{1,0:T(8,128)S(1)}, f32[8,256]{1,0:T(8,128)S(1)}, f32[128,256]{1,0:T(...) custom-call(bf16[544,128]{1,0:T(8,128)(2,1)S(1)} %get-tuple-element.37.refs_0_, ...), custom_call_target="tpu_custom_call" | custom-call | flops 5368709120 | bytes 2097152 | tf_op jit(solution)/shard_map/pallas_call | solution.py:274
  33.4 0.9 %collective-permute-done.8.refs_4_.refs_3_ = bf16[256,256]{1,0:T(8,128)(2,1)S(1)} collective-permute-done((bf16[256,256]{1,0:T(8,128)(2,1)S(1)}, bf16[256,256]{1,0:T(8,128)(2,1)S(1)}, u32[]{:S(2)}, u32[]{:S(2)}) %collective-permute-start.8) | collective-permute-done | bytes 131104 | tf_op jit(solution)/shard_map/ppermute | solution.py:32
  34.3 0.9 %shard_map.59 = (bf16[144,256]{1,0:T(8,128)(2,1)S(1)}, bf16[144,256]{1,0:T(8,128)(2,1)S(1)}) custom-call(bf16[272,128]{1,0:T(8,128)(2,1)S(1)} %collective-permute-done.11.refs_3_.refs_0_, bf16[544,128]{1,0:T(8,128)(2,1)S(1)} %collective-permute-done.9.refs_1_, bf16[256,256]{1,0:T(8,128)(2,1)S(1)} %collective-permute-done.5.refs_2_.refs_1_, ...), custom_call_target="tpu_custom_call" | custom-call | flops 1610612736 | bytes 2097152 | tf_op jit(solution)/shard_map/pallas_call | solution.py:274
  35.3 2.7 %collective-permute-start.14 = (bf16[144,256]{1,0:T(8,128)(2,1)S(1)}, bf16[144,256]{1,0:T(8,128)(2,1)S(1)}, u32[]{:S(2)}, u32[]{:S(2)}) collective-permute-start(bf16[144,256]{1,0:T(8,128)(2,1)S(1)} %get-tuple-element.45), channel_id=1, source_target_pairs={{0,32},{16,48},{32,0},{48,16},{1,33},{17,49},{33,1},{49,17},{2,34}... | collective-permute-start | bytes 221192 | tf_op jit(solution)/shard_map/ppermute | solution.py:32
  38.6 3.7 %collective-permute-start.16 = (bf16[288,256]{1,0:T(8,128)(2,1)S(1)}, bf16[288,256]{1,0:T(8,128)(2,1)S(1)}, u32[]{:S(2)}, u32[]{:S(2)}) collective-permute-start(bf16[288,256]{1,0:T(8,128)(2,1)S(1)} %shard_map.62), channel_id=1, source_target_pairs={{0,48},{4,20},{16,32},{20,4},{32,16},{36,52},{48,0},{52,36},{1,49}... | collective-permute-start | bytes 442376 | tf_op jit(solution)/shard_map/ppermute | solution.py:38
  42.3 1.8 %collective-permute-done.14.refs_6_ = bf16[144,256]{1,0:T(8,128)(2,1)S(1)} collective-permute-done((bf16[144,256]{1,0:T(8,128)(2,1)S(1)}, bf16[144,256]{1,0:T(8,128)(2,1)S(1)}, u32[]{:S(2)}, u32[]{:S(2)}) %collective-permute-start.14) | collective-permute-done | bytes 73760 | tf_op jit(solution)/shard_map/ppermute | solution.py:32
  44.1 0.6 shard_map.60.own_ref
  44.7 4.1 %collective-permute-done.16.side_ref = bf16[288,256]{1,0:T(8,128)(2,1)S(1)} collective-permute-done((bf16[288,256]{1,0:T(8,128)(2,1)S(1)}, bf16[288,256]{1,0:T(8,128)(2,1)S(1)}, u32[]{:S(2)}, u32[]{:S(2)}) %collective-permute-start.16) | collective-permute-done | bytes 147488 | tf_op jit(solution)/shard_map/ppermute | solution.py:38
  49.0 1.3 %collective-permute-done.17.got_ref = bf16[288,128]{1,0:T(8,128)(2,1)S(1)} collective-permute-done((bf16[288,128]{1,0:T(8,128)(2,1)S(1)}, bf16[288,128]{1,0:T(8,128)(2,1)S(1)}, u32[]{:S(2)}, u32[]{:S(2)}) %collective-permute-start.17) | collective-permute-done | bytes 73760 | tf_op jit(solution)/shard_map/ppermute | solution.py:27
  50.2 0.6 shard_map.64
  51.0 0.8 %collective-permute-start.20 = (bf16[32,2560]{1,0:T(8,128)(2,1)S(1)}, bf16[32,2560]{1,0:T(8,128)(2,1)S(1)}, u32[]{:S(2)}, u32[]{:S(2)}) collective-permute-start(bf16[32,2560]{1,0:T(8,128)(2,1)S(1)} %get-tuple-element.55), channel_id=1, source_target_pairs={{0,3},{1,2},{2,1},{3,0},{4,7},{5,6},{6,5},{7,4},{8,11},{9,10},{10,... | collective-permute-start | bytes 491528 | tf_op jit(solution)/shard_map/ppermute | solution.py:32
  51.8 1.3 %collective-permute-start.18 = (bf16[32,2560]{1,0:T(8,128)(2,1)S(1)}, bf16[32,2560]{1,0:T(8,128)(2,1)S(1)}, u32[]{:S(2)}, u32[]{:S(2)}) collective-permute-start(bf16[32,2560]{1,0:T(8,128)(2,1)S(1)} %slice.20), channel_id=1, source_target_pairs={{0,1},{1,0},{2,3},{3,2},{4,5},{5,4},{6,7},{7,6},{8,9},{9,8},{10,11... | collective-permute-start | bytes 491528 | tf_op jit(solution)/shard_map/ppermute | solution.py:32
  53.1 2.7 %collective-permute-start.23 = (bf16[32,2560]{1,0:T(8,128)(2,1)S(1)}, bf16[32,2560]{1,0:T(8,128)(2,1)S(1)}, u32[]{:S(2)}, u32[]{:S(2)}) collective-permute-start(bf16[32,2560]{1,0:T(8,128)(2,1)S(1)} %slice.23), channel_id=1, source_target_pairs={{0,3},{1,2},{2,1},{3,0},{4,7},{5,6},{6,5},{7,4},{8,11},{9,10},{10,... | collective-permute-start | bytes 491528 | tf_op jit(solution)/shard_map/ppermute | solution.py:32
  55.9 2.2 %collective-permute-done.19.a_ref = bf16[32,2560]{1,0:T(8,128)(2,1)S(1)} collective-permute-done((bf16[32,2560]{1,0:T(8,128)(2,1)S(1)}, bf16[32,2560]{1,0:T(8,128)(2,1)S(1)}, u32[]{:S(2)}, u32[]{:S(2)}) %collective-permute-start.19) | collective-permute-done | bytes 163872 | tf_op jit(solution)/shard_map/ppermute | solution.py:32
  58.0 1.3 %collective-permute-done.20.b_ref = bf16[32,2560]{1,0:T(8,128)(2,1)S(1)} collective-permute-done((bf16[32,2560]{1,0:T(8,128)(2,1)S(1)}, bf16[32,2560]{1,0:T(8,128)(2,1)S(1)}, u32[]{:S(2)}, u32[]{:S(2)}) %collective-permute-start.20) | collective-permute-done | bytes 163872 | tf_op jit(solution)/shard_map/ppermute | solution.py:32
  59.5 0.9 %collective-permute-start.22 = (bf16[32,2560]{1,0:T(8,128)(2,1)S(1)}, bf16[32,2560]{1,0:T(8,128)(2,1)S(1)}, u32[]{:S(2)}, u32[]{:S(2)}) collective-permute-start(bf16[32,2560]{1,0:T(8,128)(2,1)S(1)} %get-tuple-element.54), channel_id=1, source_target_pairs={{0,1},{1,0},{2,3},{3,2},{4,5},{5,4},{6,7},{7,6},{8,9},{9,8},{10,11... | collective-permute-start | bytes 491528 | tf_op jit(solution)/shard_map/ppermute | solution.py:32
  60.8 1.5 %collective-permute-done.23.d_ref = bf16[32,2560]{1,0:T(8,128)(2,1)S(1)} collective-permute-done((bf16[32,2560]{1,0:T(8,128)(2,1)S(1)}, bf16[32,2560]{1,0:T(8,128)(2,1)S(1)}, u32[]{:S(2)}, u32[]{:S(2)}) %collective-permute-start.23) | collective-permute-done | bytes 163872 | tf_op jit(solution)/shard_map/ppermute | solution.py:32
  62.2 3.8 %collective-permute-done.21.b_ref = bf16[32,2560]{1,0:T(8,128)(2,1)S(1)} collective-permute-done((bf16[32,2560]{1,0:T(8,128)(2,1)S(1)}, bf16[32,2560]{1,0:T(8,128)(2,1)S(1)}, u32[]{:S(2)}, u32[]{:S(2)}) %collective-permute-start.21) | collective-permute-done | bytes 163872 | tf_op jit(solution)/shard_map/ppermute | solution.py:32
  66.0 0.8 %shard_map.66 = bf16[32,5120]{1,0:T(8,128)(2,1)} custom-call(bf16[32,5120]{1,0:T(8,128)(2,1)S(1)} %get-tuple-element.49.own_ref, bf16[32,2560]{1,0:T(8,128)(2,1)S(1)} %collective-permute-done.18.a_ref, bf16[32,2560]{1,0:T(8,128)(2,1)S(1)} %collective-permute-done.21.b_ref, bf16[32,2560]{1,0:T(8,128)(2,1)S(1)} %collective-permute-done.22.c_ref, ...), custom_call_target="tpu_custom_call" | custom-call | tf_op jit(solution)/shard_map/pallas_call | solution.py:384
  (34 shorter events, 3.8 us)
Async XLA Ops:
  1.0 4.8 %collective-permute-start = (bf16[32,768]{1,0:T(8,128)(2,1)S(1)}, bf16[32,768]{1,0:T(8,128)(2,1)S(1)}, u32[]{:S(2)}, u32[]{:S(2)}) collective-permute-start(bf16[32,768]{1,0:T(8,128)(2,1)S(1)} %get-tuple-element.32), channel_id=1, source_target_pairs={{0,1},{1,0},{2,3},{3,2},{4,5},{5,4},{6,7},{7,6},{8,9},{9,8},{10,11... | collective-permute-start | bytes 147464 | tf_op jit(solution)/shard_map/ppermute | solution.py:32
  2.6 5.6 %collective-permute-start.1 = (bf16[32,768]{1,0:T(8,128)(2,1)S(1)}, bf16[32,768]{1,0:T(8,128)(2,1)S(1)}, u32[]{:S(2)}, u32[]{:S(2)}) collective-permute-start(bf16[32,768]{1,0:T(8,128)(2,1)S(1)} %get-tuple-element.33), channel_id=1, source_target_pairs={{0,2},{1,3},{2,0},{3,1},{4,6},{5,7},{6,4},{7,5},{8,10},{9,11},{10,... | collective-permute-start | bytes 147464 | tf_op jit(solution)/shard_map/ppermute | solution.py:32
  5.5 5.3 %collective-permute-start.2 = (bf16[32,768]{1,0:T(8,128)(2,1)S(1)}, bf16[32,768]{1,0:T(8,128)(2,1)S(1)}, u32[]{:S(2)}, u32[]{:S(2)}) collective-permute-start(bf16[32,768]{1,0:T(8,128)(2,1)S(1)} %get-tuple-element.34), channel_id=1, source_target_pairs={{0,3},{1,2},{2,1},{3,0},{4,7},{5,6},{6,5},{7,4},{8,11},{9,10},{10,... | collective-permute-start | bytes 147464 | tf_op jit(solution)/shard_map/ppermute | solution.py:32
  10.9 1.5 %collective-permute-start.3 = (bf16[144,512]{1,0:T(8,128)(2,1)S(1)}, bf16[144,512]{1,0:T(8,128)(2,1)S(1)}, u32[]{:S(2)}, u32[]{:S(2)}) collective-permute-start(bf16[144,512]{1,0:T(8,128)(2,1)S(1)} %get-tuple-element.36), channel_id=1, source_target_pairs={{0,4},{4,0},{1,5},{5,1},{2,6},{6,2},{3,7},{7,3},{8,12},{12,8},{9,1... | collective-permute-start | bytes 442376 | tf_op jit(solution)/shard_map/ppermute | solution.py:27
  12.4 7.6 %collective-permute-start.9 = (bf16[544,128]{1,0:T(8,128)(2,1)S(1)}, bf16[544,128]{1,0:T(8,128)(2,1)S(1)}, u32[]{:S(2)}, u32[]{:S(2)}) collective-permute-start(bf16[544,128]{1,0:T(8,128)(2,1)S(1)} %get-tuple-element.37.refs_0_), channel_id=1, source_target_pairs={{0,16},{4,52},{16,0},{20,36},{32,48},{36,20},{48,32},{52,4},{1,17}... | collective-permute-start | bytes 417800 | tf_op jit(solution)/shard_map/ppermute | solution.py:38
  15.7 6.5 %collective-permute-start.4 = (bf16[256,256]{1,0:T(8,128)(2,1)S(1)}, bf16[256,256]{1,0:T(8,128)(2,1)S(1)}, u32[]{:S(2)}, u32[]{:S(2)}) collective-permute-start(bf16[256,256]{1,0:T(8,128)(2,1)S(1)} %get-tuple-element.38.refs_5_), channel_id=1, source_target_pairs={{0,8},{8,0},{1,9},{9,1},{2,10},{10,2},{3,11},{11,3},{4,12},{12,4},... | collective-permute-start | bytes 393224 | tf_op jit(solution)/shard_map/ppermute | solution.py:32
  15.8 9.9 %collective-permute-start.7 = (bf16[256,256]{1,0:T(8,128)(2,1)S(1)}, bf16[256,256]{1,0:T(8,128)(2,1)S(1)}, u32[]{:S(2)}, u32[]{:S(2)}) collective-permute-start(bf16[256,256]{1,0:T(8,128)(2,1)S(1)} %get-tuple-element.38.refs_5_), channel_id=1, source_target_pairs={{0,128},{64,192},{128,0},{192,64},{1,129},{65,193},{129,1},{193,65... | collective-permute-start | bytes 393224 | tf_op jit(solution)/shard_map/ppermute | solution.py:32
  18.9 8.3 %collective-permute-start.12 = (bf16[256,256]{1,0:T(8,128)(2,1)S(1)}, bf16[256,256]{1,0:T(8,128)(2,1)S(1)}, u32[]{:S(2)}, u32[]{:S(2)}) collective-permute-start(bf16[256,256]{1,0:T(8,128)(2,1)S(1)} %get-tuple-element.38.refs_5_), channel_id=1, source_target_pairs={{0,64},{64,0},{128,192},{192,128},{1,65},{65,1},{129,193},{193,129... | collective-permute-start | bytes 393224 | tf_op jit(solution)/shard_map/ppermute | solution.py:32
  19.4 9.8 %collective-permute-start.13 = (bf16[256,256]{1,0:T(8,128)(2,1)S(1)}, bf16[256,256]{1,0:T(8,128)(2,1)S(1)}, u32[]{:S(2)}, u32[]{:S(2)}) collective-permute-start(bf16[256,256]{1,0:T(8,128)(2,1)S(1)} %get-tuple-element.38.refs_5_), channel_id=1, source_target_pairs={{0,192},{64,128},{128,64},{192,0},{1,193},{65,129},{129,65},{193,1... | collective-permute-start | bytes 393224 | tf_op jit(solution)/shard_map/ppermute | solution.py:32
  20.0 11.1 %collective-permute-start.10 = (bf16[272,128]{1,0:T(8,128)(2,1)S(1)}, bf16[272,128]{1,0:T(8,128)(2,1)S(1)}, u32[]{:S(2)}, u32[]{:S(2)}) collective-permute-start(bf16[272,128]{1,0:T(8,128)(2,1)S(1)} %get-tuple-element.58), channel_id=1, source_target_pairs={{0,4},{4,0},{1,5},{5,1},{2,6},{6,2},{3,7},{7,3},{8,12},{12,8},{9,1... | collective-permute-start | bytes 208904 | tf_op jit(solution)/shard_map/ppermute | solution.py:27
  22.3 8.8 %collective-permute-start.11 = (bf16[272,128]{1,0:T(8,128)(2,1)S(1)}, bf16[272,128]{1,0:T(8,128)(2,1)S(1)}, u32[]{:S(2)}, u32[]{:S(2)}) collective-permute-start(bf16[272,128]{1,0:T(8,128)(2,1)S(1)} %get-tuple-element.57), channel_id=1, source_target_pairs={{0,48},{4,20},{16,32},{20,4},{32,16},{36,52},{48,0},{52,36},{1,49}... | collective-permute-start | bytes 208904 | tf_op jit(solution)/shard_map/ppermute | solution.py:38
  25.7 7.2 %collective-permute-start.5 = (bf16[256,256]{1,0:T(8,128)(2,1)S(1)}, bf16[256,256]{1,0:T(8,128)(2,1)S(1)}, u32[]{:S(2)}, u32[]{:S(2)}) collective-permute-start(bf16[256,256]{1,0:T(8,128)(2,1)S(1)} %collective-permute-done.4.refs_4_), channel_id=1, source_target_pairs={{0,64},{64,0},{128,192},{192,128},{1,65},{65,1},{129,193},{193,129... | collective-permute-start | bytes 393224 | tf_op jit(solution)/shard_map/ppermute | solution.py:32
  27.2 6.2 %collective-permute-start.6 = (bf16[256,256]{1,0:T(8,128)(2,1)S(1)}, bf16[256,256]{1,0:T(8,128)(2,1)S(1)}, u32[]{:S(2)}, u32[]{:S(2)}) collective-permute-start(bf16[256,256]{1,0:T(8,128)(2,1)S(1)} %collective-permute-done.4.refs_4_), channel_id=1, source_target_pairs={{0,192},{64,128},{128,64},{192,0},{1,193},{65,129},{129,65},{193,1... | collective-permute-start | bytes 393224 | tf_op jit(solution)/shard_map/ppermute | solution.py:32
  29.3 5.0 %collective-permute-start.8 = (bf16[256,256]{1,0:T(8,128)(2,1)S(1)}, bf16[256,256]{1,0:T(8,128)(2,1)S(1)}, u32[]{:S(2)}, u32[]{:S(2)}) collective-permute-start(bf16[256,256]{1,0:T(8,128)(2,1)S(1)} %collective-permute-done.7.refs_6_), channel_id=1, source_target_pairs={{0,8},{8,0},{1,9},{9,1},{2,10},{10,2},{3,11},{11,3},{4,12},{12,4},... | collective-permute-start | bytes 393224 | tf_op jit(solution)/shard_map/ppermute | solution.py:32
  35.2 3.4 %collective-permute-start.15 = (bf16[144,256]{1,0:T(8,128)(2,1)S(1)}, bf16[144,256]{1,0:T(8,128)(2,1)S(1)}, u32[]{:S(2)}, u32[]{:S(2)}) collective-permute-start(bf16[144,256]{1,0:T(8,128)(2,1)S(1)} %get-tuple-element.48), channel_id=1, source_target_pairs={{0,4},{4,0},{1,5},{5,1},{2,6},{6,2},{3,7},{7,3},{8,12},{12,8},{9,1... | collective-permute-start | bytes 221192 | tf_op jit(solution)/shard_map/ppermute | solution.py:27
  35.3 8.8 %collective-permute-start.14 = (bf16[144,256]{1,0:T(8,128)(2,1)S(1)}, bf16[144,256]{1,0:T(8,128)(2,1)S(1)}, u32[]{:S(2)}, u32[]{:S(2)}) collective-permute-start(bf16[144,256]{1,0:T(8,128)(2,1)S(1)} %get-tuple-element.45), channel_id=1, source_target_pairs={{0,32},{16,48},{32,0},{48,16},{1,33},{17,49},{33,1},{49,17},{2,34}... | collective-permute-start | bytes 221192 | tf_op jit(solution)/shard_map/ppermute | solution.py:32
  37.9 12.3 %copy-start = (bf16[256,5120]{1,0:T(8,128)(2,1)S(1)}, bf16[256,5120]{1,0:T(8,128)(2,1)}, u32[]{:S(2)}) copy-start(bf16[256,5120]{1,0:T(8,128)(2,1)} %w_ref.1) | copy-start | bytes 7864324
  38.6 10.2 %collective-permute-start.16 = (bf16[288,256]{1,0:T(8,128)(2,1)S(1)}, bf16[288,256]{1,0:T(8,128)(2,1)S(1)}, u32[]{:S(2)}, u32[]{:S(2)}) collective-permute-start(bf16[288,256]{1,0:T(8,128)(2,1)S(1)} %shard_map.62), channel_id=1, source_target_pairs={{0,48},{4,20},{16,32},{20,4},{32,16},{36,52},{48,0},{52,36},{1,49}... | collective-permute-start | bytes 442376 | tf_op jit(solution)/shard_map/ppermute | solution.py:38
  48.9 1.4 %collective-permute-start.17 = (bf16[288,128]{1,0:T(8,128)(2,1)S(1)}, bf16[288,128]{1,0:T(8,128)(2,1)S(1)}, u32[]{:S(2)}, u32[]{:S(2)}) collective-permute-start(bf16[288,128]{1,0:T(8,128)(2,1)S(1)} %shard_map.63), channel_id=1, source_target_pairs={{0,4},{4,0},{1,5},{5,1},{2,6},{6,2},{3,7},{7,3},{8,12},{12,8},{9,1... | collective-permute-start | bytes 221192 | tf_op jit(solution)/shard_map/ppermute | solution.py:27
  50.9 7.1 %collective-permute-start.19 = (bf16[32,2560]{1,0:T(8,128)(2,1)S(1)}, bf16[32,2560]{1,0:T(8,128)(2,1)S(1)}, u32[]{:S(2)}, u32[]{:S(2)}) collective-permute-start(bf16[32,2560]{1,0:T(8,128)(2,1)S(1)} %get-tuple-element.56), channel_id=1, source_target_pairs={{0,1},{1,0},{2,3},{3,2},{4,5},{5,4},{6,7},{7,6},{8,9},{9,8},{10,11... | collective-permute-start | bytes 491528 | tf_op jit(solution)/shard_map/ppermute | solution.py:32
  51.0 8.3 %collective-permute-start.20 = (bf16[32,2560]{1,0:T(8,128)(2,1)S(1)}, bf16[32,2560]{1,0:T(8,128)(2,1)S(1)}, u32[]{:S(2)}, u32[]{:S(2)}) collective-permute-start(bf16[32,2560]{1,0:T(8,128)(2,1)S(1)} %get-tuple-element.55), channel_id=1, source_target_pairs={{0,3},{1,2},{2,1},{3,0},{4,7},{5,6},{6,5},{7,4},{8,11},{9,10},{10,... | collective-permute-start | bytes 491528 | tf_op jit(solution)/shard_map/ppermute | solution.py:32
  51.8 8.9 %collective-permute-start.18 = (bf16[32,2560]{1,0:T(8,128)(2,1)S(1)}, bf16[32,2560]{1,0:T(8,128)(2,1)S(1)}, u32[]{:S(2)}, u32[]{:S(2)}) collective-permute-start(bf16[32,2560]{1,0:T(8,128)(2,1)S(1)} %slice.20), channel_id=1, source_target_pairs={{0,1},{1,0},{2,3},{3,2},{4,5},{5,4},{6,7},{7,6},{8,9},{9,8},{10,11... | collective-permute-start | bytes 491528 | tf_op jit(solution)/shard_map/ppermute | solution.py:32
  53.1 9.1 %collective-permute-start.23 = (bf16[32,2560]{1,0:T(8,128)(2,1)S(1)}, bf16[32,2560]{1,0:T(8,128)(2,1)S(1)}, u32[]{:S(2)}, u32[]{:S(2)}) collective-permute-start(bf16[32,2560]{1,0:T(8,128)(2,1)S(1)} %slice.23), channel_id=1, source_target_pairs={{0,3},{1,2},{2,1},{3,0},{4,7},{5,6},{6,5},{7,4},{8,11},{9,10},{10,... | collective-permute-start | bytes 491528 | tf_op jit(solution)/shard_map/ppermute | solution.py:32
  59.4 6.6 %collective-permute-start.21 = (bf16[32,2560]{1,0:T(8,128)(2,1)S(1)}, bf16[32,2560]{1,0:T(8,128)(2,1)S(1)}, u32[]{:S(2)}, u32[]{:S(2)}) collective-permute-start(bf16[32,2560]{1,0:T(8,128)(2,1)S(1)} %get-tuple-element.53), channel_id=1, source_target_pairs={{0,3},{1,2},{2,1},{3,0},{4,7},{5,6},{6,5},{7,4},{8,11},{9,10},{10,... | collective-permute-start | bytes 491528 | tf_op jit(solution)/shard_map/ppermute | solution.py:32
  59.5 6.5 %collective-permute-start.22 = (bf16[32,2560]{1,0:T(8,128)(2,1)S(1)}, bf16[32,2560]{1,0:T(8,128)(2,1)S(1)}, u32[]{:S(2)}, u32[]{:S(2)}) collective-permute-start(bf16[32,2560]{1,0:T(8,128)(2,1)S(1)} %get-tuple-element.54), channel_id=1, source_target_pairs={{0,1},{1,0},{2,3},{3,2},{4,5},{5,4},{6,7},{7,6},{8,9},{9,8},{10,11... | collective-permute-start | bytes 491528 | tf_op jit(solution)/shard_map/ppermute | solution.py:32

commit v6 on v5

--- a/solution.py
+++ b/solution.py
@@ -65,7 +65,7 @@
 
 def pack_kernel(marks_ref, *refs):
     piece_refs, (mine_ref, send_ref) = refs[:4], refs[4:]
-    for mask, ref in enumerate(piece_refs):
+    for mask, ref in zip((0, 2, 3, 1), piece_refs):
         rows = slice(mask * 32, (mask + 1) * 32)
         mine_ref[rows, :] = ref[:, : 4 * HD]
         send_ref[rows, :HD] = ref[:, HD : 2 * HD]
@@ -311,7 +311,7 @@
         in_specs=[VMEM] * 5,
         out_specs=(VMEM, VMEM),
         compiler_params=PARAMS,
-    )(marks, pieces[0], met[1], met[2], met[3])
+    )(marks, pieces[0], met[2], met[3], met[1])
     got = moved(send, "c", 1)
     q, kv = pl.pallas_call(
         mid_kernel,
@@ -330,8 +330,8 @@
     across = swapped_by_core(first[:272], "zh", (3, 1))
     second = moved(first[272:], "c", 1)
 
-    raw = attend((q, first, second, across), kvs)
-    raw = [raw[2 * i : 2 * i + 2] for i in (3, 1, 2, 0)]
+    raw = attend((across, second, q, first), kvs)
+    raw = [raw[2 * i : 2 * i + 2] for i in (0, 3, 1, 2)]
     across, give = attend((across, first), kvs, raw[:2])
     across = swapped(across, "zh", 2)
     took = moved(give, "c", 1)

time: 67.1 us -> 66 us (0.984)
  starting transfers between devices: 35.9 us -> 35.1 us
    ppermute x4, starting transfers between devices: 2.41 us -> 0.28 us  [moved(): lax.ppermute(value, axis, [(i, (i + by) % size) for i in range(size)])]
    ppermute x3, waiting for transfers between devices: 4.12 us -> 2.37 us  [swapped_by_core(): return lax.ppermute(value, (axis, 'c'), pairs)]
    ppermute x17, waiting for transfers between devices: 17.5 us -> 18.9 us  [swapped(): return lax.ppermute(value, axis, [(i, i ^ mask) for i in range(size)])]
    ppermute x17, starting transfers between devices: 23 us -> 24.2 us  [swapped(): return lax.ppermute(value, axis, [(i, i ^ mask) for i in range(size)])]
  transfers between devices with their start and end apart: 24 -> 24, of which waited for: 14 -> 13; matrix products, arithmetic and copies ran while one was open for 0% -> 0% of each run, Pallas kernels for 5% -> 5%
where the time goes in v6:
time: 66 us; the launch traced here: 65.9 us
  starting transfers between devices  35.1 us (53%)
  waiting for transfers between devices  23.9 us (36%)
  Pallas kernels  6.45 us (10%)
    ppermute x17, starting transfers between devices, swapped(): return lax.ppermute(value, axis, [(i, i ^ mask) for i in range(size)])  24.2 us
    ppermute x17, waiting for transfers between devices, swapped(): return lax.ppermute(value, axis, [(i, i ^ mask) for i in range(size)])  18.9 us
    ppermute x3, starting transfers between devices, swapped_by_core(): return lax.ppermute(value, (axis, 'c'), pairs)  10.6 us
    pallas_call x4, Pallas kernels, attend(): pl.pallas_call(functools.partial(attend_kernel, count, chunks, early, mer...  3.88 us
    ppermute x4, waiting for transfers between devices, moved(): lax.ppermute(value, axis, [(i, (i + by) % size) for i in range(size)])  2.62 us
    ppermute x3, waiting for transfers between devices, swapped_by_core(): return lax.ppermute(value, (axis, 'c'), pairs)  2.37 us
  transfers between devices with their start and end apart: 24, of which 13 were waited for; matrix products, arithmetic and copies ran while one was open for 0% of the time, Pallas kernels for 5%

profile of v6, /device:TPU:32, one launch (start us, length us, event | category | flops | bytes accessed | tf_op | source)
XLA Modules:
  0.0 65.9 jit_solution(13045829468789853749)
XLA Ops:
  0.0 1.0 %shard_map.55 = (bf16[32,768]{1,0:T(8,128)(2,1)S(1)}, bf16[32,768]{1,0:T(8,128)(2,1)S(1)}, bf16[32,768]{1,0:T(8,128)(2,1)S(1)}, bf16[32,768]{1,0:T(8,128)(2,1)S(1)}, bf16[16,128]{1,0:T(8,128)(2,1)S(1)}) custom-call(bf16[32,1024]{1,0:T(8,128)(2,1)} %q_ref.1, bf16[32,1024]{1,0:T(8,128)(2,1)} %k_ref.1, bf16[32,1024]{1,0:T(8,128)(2,1)} %v_ref.1, ...), custom_call_target="tpu_custom_call" | custom-call | tf_op jit(solution)/shard_map/pallas_call | solution.py:295
  1.0 3.3 %collective-permute-start = (bf16[32,768]{1,0:T(8,128)(2,1)S(1)}, bf16[32,768]{1,0:T(8,128)(2,1)S(1)}, u32[]{:S(2)}, u32[]{:S(2)}) collective-permute-start(bf16[32,768]{1,0:T(8,128)(2,1)S(1)} %get-tuple-element.32), channel_id=1, source_target_pairs={{0,2},{1,3},{2,0},{3,1},{4,6},{5,7},{6,4},{7,5},{8,10},{9,11},{10,... | collective-permute-start | bytes 147464 | tf_op jit(solution)/shard_map/ppermute | solution.py:32
  4.2 1.1 %collective-permute-start.1 = (bf16[32,768]{1,0:T(8,128)(2,1)S(1)}, bf16[32,768]{1,0:T(8,128)(2,1)S(1)}, u32[]{:S(2)}, u32[]{:S(2)}) collective-permute-start(bf16[32,768]{1,0:T(8,128)(2,1)S(1)} %get-tuple-element.33), channel_id=1, source_target_pairs={{0,3},{1,2},{2,1},{3,0},{4,7},{5,6},{6,5},{7,4},{8,11},{9,10},{10,... | collective-permute-start | bytes 147464 | tf_op jit(solution)/shard_map/ppermute | solution.py:32
  5.3 1.3 %collective-permute-done.refs_1_ = bf16[32,768]{1,0:T(8,128)(2,1)S(1)} collective-permute-done((bf16[32,768]{1,0:T(8,128)(2,1)S(1)}, bf16[32,768]{1,0:T(8,128)(2,1)S(1)}, u32[]{:S(2)}, u32[]{:S(2)}) %collective-permute-start) | collective-permute-done | bytes 49184 | tf_op jit(solution)/shard_map/ppermute | solution.py:32
  6.6 2.9 %collective-permute-done.1.refs_2_ = bf16[32,768]{1,0:T(8,128)(2,1)S(1)} collective-permute-done((bf16[32,768]{1,0:T(8,128)(2,1)S(1)}, bf16[32,768]{1,0:T(8,128)(2,1)S(1)}, u32[]{:S(2)}, u32[]{:S(2)}) %collective-permute-start.1) | collective-permute-done | bytes 49184 | tf_op jit(solution)/shard_map/ppermute | solution.py:32
  9.7 1.4 %collective-permute-done.3.got_ref = bf16[144,512]{1,0:T(8,128)(2,1)S(1)} collective-permute-done((bf16[144,512]{1,0:T(8,128)(2,1)S(1)}, bf16[144,512]{1,0:T(8,128)(2,1)S(1)}, u32[]{:S(2)}, u32[]{:S(2)}) %collective-permute-start.3) | collective-permute-done | bytes 147488 | tf_op jit(solution)/shard_map/ppermute | solution.py:27
  11.1 3.4 %collective-permute-start.9 = (bf16[544,128]{1,0:T(8,128)(2,1)S(1)}, bf16[544,128]{1,0:T(8,128)(2,1)S(1)}, u32[]{:S(2)}, u32[]{:S(2)}) collective-permute-start(bf16[544,128]{1,0:T(8,128)(2,1)S(1)} %get-tuple-element.37.refs_2_.refs_0_), channel_id=1, source_target_pairs={{0,16},{4,52},{16,0},{20,36},{32,48},{36,20},{48,32},{52,4},{1,17}... | collective-permute-start | bytes 417800 | tf_op jit(solution)/shard_map/ppermute | solution.py:38
  14.5 3.0 %collective-permute-start.7 = (bf16[256,256]{1,0:T(8,128)(2,1)S(1)}, bf16[256,256]{1,0:T(8,128)(2,1)S(1)}, u32[]{:S(2)}, u32[]{:S(2)}) collective-permute-start(bf16[256,256]{1,0:T(8,128)(2,1)S(1)} %get-tuple-element.38.refs_5_), channel_id=1, source_target_pairs={{0,128},{64,192},{128,0},{192,64},{1,129},{65,193},{129,1},{193,65... | collective-permute-start | bytes 393224 | tf_op jit(solution)/shard_map/ppermute | solution.py:32
  18.7 4.7 %collective-permute-start.10 = (bf16[272,128]{1,0:T(8,128)(2,1)S(1)}, bf16[272,128]{1,0:T(8,128)(2,1)S(1)}, u32[]{:S(2)}, u32[]{:S(2)}) collective-permute-start(bf16[272,128]{1,0:T(8,128)(2,1)S(1)} %get-tuple-element.58), channel_id=1, source_target_pairs={{0,48},{4,20},{16,32},{20,4},{32,16},{36,52},{48,0},{52,36},{1,49}... | collective-permute-start | bytes 208904 | tf_op jit(solution)/shard_map/ppermute | solution.py:38
  23.5 1.6 %collective-permute-start.5 = (bf16[256,256]{1,0:T(8,128)(2,1)S(1)}, bf16[256,256]{1,0:T(8,128)(2,1)S(1)}, u32[]{:S(2)}, u32[]{:S(2)}) collective-permute-start(bf16[256,256]{1,0:T(8,128)(2,1)S(1)} %collective-permute-done.4.refs_4_), channel_id=1, source_target_pairs={{0,64},{64,0},{128,192},{192,128},{1,65},{65,1},{129,193},{193,129... | collective-permute-start | bytes 393224 | tf_op jit(solution)/shard_map/ppermute | solution.py:32
  25.0 2.1 %collective-permute-start.6 = (bf16[256,256]{1,0:T(8,128)(2,1)S(1)}, bf16[256,256]{1,0:T(8,128)(2,1)S(1)}, u32[]{:S(2)}, u32[]{:S(2)}) collective-permute-start(bf16[256,256]{1,0:T(8,128)(2,1)S(1)} %collective-permute-done.4.refs_4_), channel_id=1, source_target_pairs={{0,192},{64,128},{128,64},{192,0},{1,193},{65,129},{129,65},{193,1... | collective-permute-start | bytes 393224 | tf_op jit(solution)/shard_map/ppermute | solution.py:32
  27.1 2.1 %collective-permute-start.8 = (bf16[256,256]{1,0:T(8,128)(2,1)S(1)}, bf16[256,256]{1,0:T(8,128)(2,1)S(1)}, u32[]{:S(2)}, u32[]{:S(2)}) collective-permute-start(bf16[256,256]{1,0:T(8,128)(2,1)S(1)} %collective-permute-done.7.refs_6_), channel_id=1, source_target_pairs={{0,8},{8,0},{1,9},{9,1},{2,10},{10,2},{3,11},{11,3},{4,12},{12,4},... | collective-permute-start | bytes 393224 | tf_op jit(solution)/shard_map/ppermute | solution.py:32
  29.2 1.7 %shard_map.58 = (f32[128,256]{1,0:T(8,128)S(1)}, f32[8,256]{1,0:T(8,128)S(1)}, f32[128,256]{1,0:T(8,128)S(1)}, f32[8,256]{1,0:T(8,128)S(1)}, f32[128,256]{1,0:T(...) custom-call(bf16[272,128]{1,0:T(8,128)(2,1)S(1)} %collective-permute-done.10.refs_0_, ...), custom_call_target="tpu_custom_call" | custom-call | flops 5368709120 | bytes 2097152 | tf_op jit(solution)/shard_map/pallas_call | solution.py:274
  31.0 1.1 %collective-permute-done.6.refs_3_.refs_2_ = bf16[256,256]{1,0:T(8,128)(2,1)S(1)} collective-permute-done((bf16[256,256]{1,0:T(8,128)(2,1)S(1)}, bf16[256,256]{1,0:T(8,128)(2,1)S(1)}, u32[]{:S(2)}, u32[]{:S(2)}) %collective-permute-start.6) | collective-permute-done | bytes 131104 | tf_op jit(solution)/shard_map/ppermute | solution.py:32
  32.1 0.7 collective-permute-done.8.refs_4_.refs_3_
  32.7 0.9 %shard_map.59 = (bf16[144,256]{1,0:T(8,128)(2,1)S(1)}, bf16[144,256]{1,0:T(8,128)(2,1)S(1)}) custom-call(bf16[272,128]{1,0:T(8,128)(2,1)S(1)} %collective-permute-done.10.refs_0_, bf16[544,128]{1,0:T(8,128)(2,1)S(1)} %collective-permute-done.9.refs_3_.refs_1_, bf16[256,256]{1,0:T(8,128)(2,1)S(1)} %collective-permute-done.5.refs_2_.refs_1_, ...), custom_call_target="tpu_custom_call" | custom-call | flops 1610612736 | bytes 2097152 | tf_op jit(solution)/shard_map/pallas_call | solution.py:274
  33.8 2.7 %collective-permute-start.14 = (bf16[144,256]{1,0:T(8,128)(2,1)S(1)}, bf16[144,256]{1,0:T(8,128)(2,1)S(1)}, u32[]{:S(2)}, u32[]{:S(2)}) collective-permute-start(bf16[144,256]{1,0:T(8,128)(2,1)S(1)} %get-tuple-element.45), channel_id=1, source_target_pairs={{0,32},{16,48},{32,0},{48,16},{1,33},{17,49},{33,1},{49,17},{2,34}... | collective-permute-start | bytes 221192 | tf_op jit(solution)/shard_map/ppermute | solution.py:32
  37.1 2.5 %collective-permute-start.16 = (bf16[288,256]{1,0:T(8,128)(2,1)S(1)}, bf16[288,256]{1,0:T(8,128)(2,1)S(1)}, u32[]{:S(2)}, u32[]{:S(2)}) collective-permute-start(bf16[288,256]{1,0:T(8,128)(2,1)S(1)} %shard_map.62), channel_id=1, source_target_pairs={{0,48},{4,20},{16,32},{20,4},{32,16},{36,52},{48,0},{52,36},{1,49}... | collective-permute-start | bytes 442376 | tf_op jit(solution)/shard_map/ppermute | solution.py:38
  39.7 4.2 %collective-permute-done.14.refs_6_ = bf16[144,256]{1,0:T(8,128)(2,1)S(1)} collective-permute-done((bf16[144,256]{1,0:T(8,128)(2,1)S(1)}, bf16[144,256]{1,0:T(8,128)(2,1)S(1)}, u32[]{:S(2)}, u32[]{:S(2)}) %collective-permute-start.14) | collective-permute-done | bytes 73760 | tf_op jit(solution)/shard_map/ppermute | solution.py:32
  43.9 0.6 shard_map.60.own_ref
  44.5 2.4 %collective-permute-done.16.side_ref = bf16[288,256]{1,0:T(8,128)(2,1)S(1)} collective-permute-done((bf16[288,256]{1,0:T(8,128)(2,1)S(1)}, bf16[288,256]{1,0:T(8,128)(2,1)S(1)}, u32[]{:S(2)}, u32[]{:S(2)}) %collective-permute-start.16) | collective-permute-done | bytes 147488 | tf_op jit(solution)/shard_map/ppermute | solution.py:38
  47.1 1.3 %collective-permute-done.17.got_ref = bf16[288,128]{1,0:T(8,128)(2,1)S(1)} collective-permute-done((bf16[288,128]{1,0:T(8,128)(2,1)S(1)}, bf16[288,128]{1,0:T(8,128)(2,1)S(1)}, u32[]{:S(2)}, u32[]{:S(2)}) %collective-permute-start.17) | collective-permute-done | bytes 73760 | tf_op jit(solution)/shard_map/ppermute | solution.py:27
  48.3 0.6 shard_map.64
  49.1 2.1 %collective-permute-start.20 = (bf16[32,2560]{1,0:T(8,128)(2,1)S(1)}, bf16[32,2560]{1,0:T(8,128)(2,1)S(1)}, u32[]{:S(2)}, u32[]{:S(2)}) collective-permute-start(bf16[32,2560]{1,0:T(8,128)(2,1)S(1)} %get-tuple-element.55), channel_id=1, source_target_pairs={{0,3},{1,2},{2,1},{3,0},{4,7},{5,6},{6,5},{7,4},{8,11},{9,10},{10,... | collective-permute-start | bytes 491528 | tf_op jit(solution)/shard_map/ppermute | solution.py:32
  51.2 1.4 %collective-permute-start.18 = (bf16[32,2560]{1,0:T(8,128)(2,1)S(1)}, bf16[32,2560]{1,0:T(8,128)(2,1)S(1)}, u32[]{:S(2)}, u32[]{:S(2)}) collective-permute-start(bf16[32,2560]{1,0:T(8,128)(2,1)S(1)} %slice.20), channel_id=1, source_target_pairs={{0,1},{1,0},{2,3},{3,2},{4,5},{5,4},{6,7},{7,6},{8,9},{9,8},{10,11... | collective-permute-start | bytes 491528 | tf_op jit(solution)/shard_map/ppermute | solution.py:32
  52.6 1.3 %collective-permute-start.23 = (bf16[32,2560]{1,0:T(8,128)(2,1)S(1)}, bf16[32,2560]{1,0:T(8,128)(2,1)S(1)}, u32[]{:S(2)}, u32[]{:S(2)}) collective-permute-start(bf16[32,2560]{1,0:T(8,128)(2,1)S(1)} %slice.23), channel_id=1, source_target_pairs={{0,3},{1,2},{2,1},{3,0},{4,7},{5,6},{6,5},{7,4},{8,11},{9,10},{10,... | collective-permute-start | bytes 491528 | tf_op jit(solution)/shard_map/ppermute | solution.py:32
  53.9 2.2 %collective-permute-done.19.a_ref = bf16[32,2560]{1,0:T(8,128)(2,1)S(1)} collective-permute-done((bf16[32,2560]{1,0:T(8,128)(2,1)S(1)}, bf16[32,2560]{1,0:T(8,128)(2,1)S(1)}, u32[]{:S(2)}, u32[]{:S(2)}) %collective-permute-start.19) | collective-permute-done | bytes 163872 | tf_op jit(solution)/shard_map/ppermute | solution.py:32
  56.1 1.3 %collective-permute-done.20.b_ref = bf16[32,2560]{1,0:T(8,128)(2,1)S(1)} collective-permute-done((bf16[32,2560]{1,0:T(8,128)(2,1)S(1)}, bf16[32,2560]{1,0:T(8,128)(2,1)S(1)}, u32[]{:S(2)}, u32[]{:S(2)}) %collective-permute-start.20) | collective-permute-done | bytes 163872 | tf_op jit(solution)/shard_map/ppermute | solution.py:32
  57.5 2.1 %collective-permute-start.21 = (bf16[32,2560]{1,0:T(8,128)(2,1)S(1)}, bf16[32,2560]{1,0:T(8,128)(2,1)S(1)}, u32[]{:S(2)}, u32[]{:S(2)}) collective-permute-start(bf16[32,2560]{1,0:T(8,128)(2,1)S(1)} %get-tuple-element.53), channel_id=1, source_target_pairs={{0,3},{1,2},{2,1},{3,0},{4,7},{5,6},{6,5},{7,4},{8,11},{9,10},{10,... | collective-permute-start | bytes 491528 | tf_op jit(solution)/shard_map/ppermute | solution.py:32
  60.3 3.8 %collective-permute-done.21.b_ref = bf16[32,2560]{1,0:T(8,128)(2,1)S(1)} collective-permute-done((bf16[32,2560]{1,0:T(8,128)(2,1)S(1)}, bf16[32,2560]{1,0:T(8,128)(2,1)S(1)}, u32[]{:S(2)}, u32[]{:S(2)}) %collective-permute-start.21) | collective-permute-done | bytes 163872 | tf_op jit(solution)/shard_map/ppermute | solution.py:32
  64.1 0.8 %collective-permute-done.22.c_ref = bf16[32,2560]{1,0:T(8,128)(2,1)S(1)} collective-permute-done((bf16[32,2560]{1,0:T(8,128)(2,1)S(1)}, bf16[32,2560]{1,0:T(8,128)(2,1)S(1)}, u32[]{:S(2)}, u32[]{:S(2)}) %collective-permute-start.22) | collective-permute-done | bytes 163872 | tf_op jit(solution)/shard_map/ppermute | solution.py:32
  64.9 0.8 %shard_map.66 = bf16[32,5120]{1,0:T(8,128)(2,1)} custom-call(bf16[32,5120]{1,0:T(8,128)(2,1)S(1)} %get-tuple-element.49.own_ref, bf16[32,2560]{1,0:T(8,128)(2,1)S(1)} %collective-permute-done.18.a_ref, bf16[32,2560]{1,0:T(8,128)(2,1)S(1)} %collective-permute-done.21.b_ref, bf16[32,2560]{1,0:T(8,128)(2,1)S(1)} %collective-permute-done.22.c_ref, ...), custom_call_target="tpu_custom_call" | custom-call | tf_op jit(solution)/shard_map/pallas_call | solution.py:384
  (34 shorter events, 3.2 us)
Async XLA Ops:
  1.0 5.7 %collective-permute-start = (bf16[32,768]{1,0:T(8,128)(2,1)S(1)}, bf16[32,768]{1,0:T(8,128)(2,1)S(1)}, u32[]{:S(2)}, u32[]{:S(2)}) collective-permute-start(bf16[32,768]{1,0:T(8,128)(2,1)S(1)} %get-tuple-element.32), channel_id=1, source_target_pairs={{0,2},{1,3},{2,0},{3,1},{4,6},{5,7},{6,4},{7,5},{8,10},{9,11},{10,... | collective-permute-start | bytes 147464 | tf_op jit(solution)/shard_map/ppermute | solution.py:32
  4.2 5.3 %collective-permute-start.1 = (bf16[32,768]{1,0:T(8,128)(2,1)S(1)}, bf16[32,768]{1,0:T(8,128)(2,1)S(1)}, u32[]{:S(2)}, u32[]{:S(2)}) collective-permute-start(bf16[32,768]{1,0:T(8,128)(2,1)S(1)} %get-tuple-element.33), channel_id=1, source_target_pairs={{0,3},{1,2},{2,1},{3,0},{4,7},{5,6},{6,5},{7,4},{8,11},{9,10},{10,... | collective-permute-start | bytes 147464 | tf_op jit(solution)/shard_map/ppermute | solution.py:32
  5.3 4.2 %collective-permute-start.2 = (bf16[32,768]{1,0:T(8,128)(2,1)S(1)}, bf16[32,768]{1,0:T(8,128)(2,1)S(1)}, u32[]{:S(2)}, u32[]{:S(2)}) collective-permute-start(bf16[32,768]{1,0:T(8,128)(2,1)S(1)} %get-tuple-element.34), channel_id=1, source_target_pairs={{0,1},{1,0},{2,3},{3,2},{4,5},{5,4},{6,7},{7,6},{8,9},{9,8},{10,11... | collective-permute-start | bytes 147464 | tf_op jit(solution)/shard_map/ppermute | solution.py:32
  9.6 1.5 %collective-permute-start.3 = (bf16[144,512]{1,0:T(8,128)(2,1)S(1)}, bf16[144,512]{1,0:T(8,128)(2,1)S(1)}, u32[]{:S(2)}, u32[]{:S(2)}) collective-permute-start(bf16[144,512]{1,0:T(8,128)(2,1)S(1)} %get-tuple-element.36), channel_id=1, source_target_pairs={{0,4},{4,0},{1,5},{5,1},{2,6},{6,2},{3,7},{7,3},{8,12},{12,8},{9,1... | collective-permute-start | bytes 442376 | tf_op jit(solution)/shard_map/ppermute | solution.py:27
  11.1 7.6 %collective-permute-start.9 = (bf16[544,128]{1,0:T(8,128)(2,1)S(1)}, bf16[544,128]{1,0:T(8,128)(2,1)S(1)}, u32[]{:S(2)}, u32[]{:S(2)}) collective-permute-start(bf16[544,128]{1,0:T(8,128)(2,1)S(1)} %get-tuple-element.37.refs_2_.refs_0_), channel_id=1, source_target_pairs={{0,16},{4,52},{16,0},{20,36},{32,48},{36,20},{48,32},{52,4},{1,17}... | collective-permute-start | bytes 417800 | tf_op jit(solution)/shard_map/ppermute | solution.py:38
  14.4 9.0 %collective-permute-start.4 = (bf16[256,256]{1,0:T(8,128)(2,1)S(1)}, bf16[256,256]{1,0:T(8,128)(2,1)S(1)}, u32[]{:S(2)}, u32[]{:S(2)}) collective-permute-start(bf16[256,256]{1,0:T(8,128)(2,1)S(1)} %get-tuple-element.38.refs_5_), channel_id=1, source_target_pairs={{0,8},{8,0},{1,9},{9,1},{2,10},{10,2},{3,11},{11,3},{4,12},{12,4},... | collective-permute-start | bytes 393224 | tf_op jit(solution)/shard_map/ppermute | solution.py:32
  14.5 8.9 %collective-permute-start.7 = (bf16[256,256]{1,0:T(8,128)(2,1)S(1)}, bf16[256,256]{1,0:T(8,128)(2,1)S(1)}, u32[]{:S(2)}, u32[]{:S(2)}) collective-permute-start(bf16[256,256]{1,0:T(8,128)(2,1)S(1)} %get-tuple-element.38.refs_5_), channel_id=1, source_target_pairs={{0,128},{64,192},{128,0},{192,64},{1,129},{65,193},{129,1},{193,65... | collective-permute-start | bytes 393224 | tf_op jit(solution)/shard_map/ppermute | solution.py:32
  17.6 7.5 %collective-permute-start.12 = (bf16[256,256]{1,0:T(8,128)(2,1)S(1)}, bf16[256,256]{1,0:T(8,128)(2,1)S(1)}, u32[]{:S(2)}, u32[]{:S(2)}) collective-permute-start(bf16[256,256]{1,0:T(8,128)(2,1)S(1)} %get-tuple-element.38.refs_5_), channel_id=1, source_target_pairs={{0,64},{64,0},{128,192},{192,128},{1,65},{65,1},{129,193},{193,129... | collective-permute-start | bytes 393224 | tf_op jit(solution)/shard_map/ppermute | solution.py:32
  18.2 9.0 %collective-permute-start.13 = (bf16[256,256]{1,0:T(8,128)(2,1)S(1)}, bf16[256,256]{1,0:T(8,128)(2,1)S(1)}, u32[]{:S(2)}, u32[]{:S(2)}) collective-permute-start(bf16[256,256]{1,0:T(8,128)(2,1)S(1)} %get-tuple-element.38.refs_5_), channel_id=1, source_target_pairs={{0,192},{64,128},{128,64},{192,0},{1,193},{65,129},{129,65},{193,1... | collective-permute-start | bytes 393224 | tf_op jit(solution)/shard_map/ppermute | solution.py:32
  18.7 10.5 %collective-permute-start.10 = (bf16[272,128]{1,0:T(8,128)(2,1)S(1)}, bf16[272,128]{1,0:T(8,128)(2,1)S(1)}, u32[]{:S(2)}, u32[]{:S(2)}) collective-permute-start(bf16[272,128]{1,0:T(8,128)(2,1)S(1)} %get-tuple-element.58), channel_id=1, source_target_pairs={{0,48},{4,20},{16,32},{20,4},{32,16},{36,52},{48,0},{52,36},{1,49}... | collective-permute-start | bytes 208904 | tf_op jit(solution)/shard_map/ppermute | solution.py:38
  23.5 5.8 %collective-permute-start.11 = (bf16[272,128]{1,0:T(8,128)(2,1)S(1)}, bf16[272,128]{1,0:T(8,128)(2,1)S(1)}, u32[]{:S(2)}, u32[]{:S(2)}) collective-permute-start(bf16[272,128]{1,0:T(8,128)(2,1)S(1)} %get-tuple-element.57), channel_id=1, source_target_pairs={{0,4},{4,0},{1,5},{5,1},{2,6},{6,2},{3,7},{7,3},{8,12},{12,8},{9,1... | collective-permute-start | bytes 208904 | tf_op jit(solution)/shard_map/ppermute | solution.py:27
  23.5 7.5 %collective-permute-start.5 = (bf16[256,256]{1,0:T(8,128)(2,1)S(1)}, bf16[256,256]{1,0:T(8,128)(2,1)S(1)}, u32[]{:S(2)}, u32[]{:S(2)}) collective-permute-start(bf16[256,256]{1,0:T(8,128)(2,1)S(1)} %collective-permute-done.4.refs_4_), channel_id=1, source_target_pairs={{0,64},{64,0},{128,192},{192,128},{1,65},{65,1},{129,193},{193,129... | collective-permute-start | bytes 393224 | tf_op jit(solution)/shard_map/ppermute | solution.py:32
  25.0 7.1 %collective-permute-start.6 = (bf16[256,256]{1,0:T(8,128)(2,1)S(1)}, bf16[256,256]{1,0:T(8,128)(2,1)S(1)}, u32[]{:S(2)}, u32[]{:S(2)}) collective-permute-start(bf16[256,256]{1,0:T(8,128)(2,1)S(1)} %collective-permute-done.4.refs_4_), channel_id=1, source_target_pairs={{0,192},{64,128},{128,64},{192,0},{1,193},{65,129},{129,65},{193,1... | collective-permute-start | bytes 393224 | tf_op jit(solution)/shard_map/ppermute | solution.py:32
  27.1 5.6 %collective-permute-start.8 = (bf16[256,256]{1,0:T(8,128)(2,1)S(1)}, bf16[256,256]{1,0:T(8,128)(2,1)S(1)}, u32[]{:S(2)}, u32[]{:S(2)}) collective-permute-start(bf16[256,256]{1,0:T(8,128)(2,1)S(1)} %collective-permute-done.7.refs_6_), channel_id=1, source_target_pairs={{0,8},{8,0},{1,9},{9,1},{2,10},{10,2},{3,11},{11,3},{4,12},{12,4},... | collective-permute-start | bytes 393224 | tf_op jit(solution)/shard_map/ppermute | solution.py:32
  33.7 3.4 %collective-permute-start.15 = (bf16[144,256]{1,0:T(8,128)(2,1)S(1)}, bf16[144,256]{1,0:T(8,128)(2,1)S(1)}, u32[]{:S(2)}, u32[]{:S(2)}) collective-permute-start(bf16[144,256]{1,0:T(8,128)(2,1)S(1)} %get-tuple-element.48), channel_id=1, source_target_pairs={{0,4},{4,0},{1,5},{5,1},{2,6},{6,2},{3,7},{7,3},{8,12},{12,8},{9,1... | collective-permute-start | bytes 221192 | tf_op jit(solution)/shard_map/ppermute | solution.py:27
  33.8 10.1 %collective-permute-start.14 = (bf16[144,256]{1,0:T(8,128)(2,1)S(1)}, bf16[144,256]{1,0:T(8,128)(2,1)S(1)}, u32[]{:S(2)}, u32[]{:S(2)}) collective-permute-start(bf16[144,256]{1,0:T(8,128)(2,1)S(1)} %get-tuple-element.45), channel_id=1, source_target_pairs={{0,32},{16,48},{32,0},{48,16},{1,33},{17,49},{33,1},{49,17},{2,34}... | collective-permute-start | bytes 221192 | tf_op jit(solution)/shard_map/ppermute | solution.py:32
  36.5 11.8 %copy-start = (bf16[256,5120]{1,0:T(8,128)(2,1)S(1)}, bf16[256,5120]{1,0:T(8,128)(2,1)}, u32[]{:S(2)}) copy-start(bf16[256,5120]{1,0:T(8,128)(2,1)} %w_ref.1) | copy-start | bytes 7864324
  37.1 9.8 %collective-permute-start.16 = (bf16[288,256]{1,0:T(8,128)(2,1)S(1)}, bf16[288,256]{1,0:T(8,128)(2,1)S(1)}, u32[]{:S(2)}, u32[]{:S(2)}) collective-permute-start(bf16[288,256]{1,0:T(8,128)(2,1)S(1)} %shard_map.62), channel_id=1, source_target_pairs={{0,48},{4,20},{16,32},{20,4},{32,16},{36,52},{48,0},{52,36},{1,49}... | collective-permute-start | bytes 442376 | tf_op jit(solution)/shard_map/ppermute | solution.py:38
  47.0 1.4 %collective-permute-start.17 = (bf16[288,128]{1,0:T(8,128)(2,1)S(1)}, bf16[288,128]{1,0:T(8,128)(2,1)S(1)}, u32[]{:S(2)}, u32[]{:S(2)}) collective-permute-start(bf16[288,128]{1,0:T(8,128)(2,1)S(1)} %shard_map.63), channel_id=1, source_target_pairs={{0,4},{4,0},{1,5},{5,1},{2,6},{6,2},{3,7},{7,3},{8,12},{12,8},{9,1... | collective-permute-start | bytes 221192 | tf_op jit(solution)/shard_map/ppermute | solution.py:27
  49.0 7.1 %collective-permute-start.19 = (bf16[32,2560]{1,0:T(8,128)(2,1)S(1)}, bf16[32,2560]{1,0:T(8,128)(2,1)S(1)}, u32[]{:S(2)}, u32[]{:S(2)}) collective-permute-start(bf16[32,2560]{1,0:T(8,128)(2,1)S(1)} %get-tuple-element.56), channel_id=1, source_target_pairs={{0,1},{1,0},{2,3},{3,2},{4,5},{5,4},{6,7},{7,6},{8,9},{9,8},{10,11... | collective-permute-start | bytes 491528 | tf_op jit(solution)/shard_map/ppermute | solution.py:32
  49.1 8.3 %collective-permute-start.20 = (bf16[32,2560]{1,0:T(8,128)(2,1)S(1)}, bf16[32,2560]{1,0:T(8,128)(2,1)S(1)}, u32[]{:S(2)}, u32[]{:S(2)}) collective-permute-start(bf16[32,2560]{1,0:T(8,128)(2,1)S(1)} %get-tuple-element.55), channel_id=1, source_target_pairs={{0,3},{1,2},{2,1},{3,0},{4,7},{5,6},{6,5},{7,4},{8,11},{9,10},{10,... | collective-permute-start | bytes 491528 | tf_op jit(solution)/shard_map/ppermute | solution.py:32
  51.2 8.6 %collective-permute-start.18 = (bf16[32,2560]{1,0:T(8,128)(2,1)S(1)}, bf16[32,2560]{1,0:T(8,128)(2,1)S(1)}, u32[]{:S(2)}, u32[]{:S(2)}) collective-permute-start(bf16[32,2560]{1,0:T(8,128)(2,1)S(1)} %slice.20), channel_id=1, source_target_pairs={{0,1},{1,0},{2,3},{3,2},{4,5},{5,4},{6,7},{7,6},{8,9},{9,8},{10,11... | collective-permute-start | bytes 491528 | tf_op jit(solution)/shard_map/ppermute | solution.py:32
  52.6 7.7 %collective-permute-start.23 = (bf16[32,2560]{1,0:T(8,128)(2,1)S(1)}, bf16[32,2560]{1,0:T(8,128)(2,1)S(1)}, u32[]{:S(2)}, u32[]{:S(2)}) collective-permute-start(bf16[32,2560]{1,0:T(8,128)(2,1)S(1)} %slice.23), channel_id=1, source_target_pairs={{0,3},{1,2},{2,1},{3,0},{4,7},{5,6},{6,5},{7,4},{8,11},{9,10},{10,... | collective-permute-start | bytes 491528 | tf_op jit(solution)/shard_map/ppermute | solution.py:32
  57.5 6.6 %collective-permute-start.21 = (bf16[32,2560]{1,0:T(8,128)(2,1)S(1)}, bf16[32,2560]{1,0:T(8,128)(2,1)S(1)}, u32[]{:S(2)}, u32[]{:S(2)}) collective-permute-start(bf16[32,2560]{1,0:T(8,128)(2,1)S(1)} %get-tuple-element.53), channel_id=1, source_target_pairs={{0,3},{1,2},{2,1},{3,0},{4,7},{5,6},{6,5},{7,4},{8,11},{9,10},{10,... | collective-permute-start | bytes 491528 | tf_op jit(solution)/shard_map/ppermute | solution.py:32
  59.6 5.3 %collective-permute-start.22 = (bf16[32,2560]{1,0:T(8,128)(2,1)S(1)}, bf16[32,2560]{1,0:T(8,128)(2,1)S(1)}, u32[]{:S(2)}, u32[]{:S(2)}) collective-permute-start(bf16[32,2560]{1,0:T(8,128)(2,1)S(1)} %get-tuple-element.54), channel_id=1, source_target_pairs={{0,1},{1,0},{2,3},{3,2},{4,5},{5,4},{6,7},{7,6},{8,9},{9,8},{10,11... | collective-permute-start | bytes 491528 | tf_op jit(solution)/shard_map/ppermute | solution.py:32

commit v7 on v6

--- a/solution.py
+++ b/solution.py
@@ -235,21 +235,19 @@
     by_three_ref[...] = (three_ref[:, :half].astype(F32) + a_ref[...].astype(F32)).astype(BF)
 
 
-def sum_kernel(own_ref, a_ref, b_ref, c_ref, d_ref, out_ref, total_ref, sem):
+def sum_kernel(base, own_ref, a_ref, b_ref, *refs):
+    out_ref, total_ref, sem = refs[-3:]
     half = a_ref.shape[1]
     step = half // 2
     copies = []
-    for i, (one, two) in enumerate(((c_ref, d_ref), (a_ref, b_ref))):
-        base = half * (1 - i)
-        for start in range(0, half, step):
-            cols = slice(start, start + step)
-            spot = slice(base + start, base + start + step)
-            total = own_ref[:, spot].astype(F32) + one[:, cols].astype(F32)
-            total_ref[:, spot] = (total + two[:, cols].astype(F32)).astype(BF)
-            there = out_ref.at[:, pl.ds(base + start, step)]
-            here = total_ref.at[:, pl.ds(base + start, step)]
-            copies.append(pltpu.make_async_copy(here, there, sem.at[len(copies)]))
-            copies[-1].start()
+    for i in range(2):
+        cols = slice(i * step, (i + 1) * step)
+        total = own_ref[:, base + i * step : base + (i + 1) * step].astype(F32)
+        total += a_ref[:, cols].astype(F32) + b_ref[:, cols].astype(F32)
+        total_ref[:, cols] = total.astype(BF)
+        there = out_ref.at[:, pl.ds(base + i * step, step)]
+        copies.append(pltpu.make_async_copy(total_ref.at[:, pl.ds(i * step, step)], there, sem.at[i]))
+        copies[-1].start()
     for copy in copies:
         copy.wait()
 
@@ -381,14 +379,18 @@
     )(one, three, a, b)
     left_three = swapped(by_three, "y", 3)
     right_one = swapped(by_one, "y", 1)
-    return pl.pallas_call(
-        sum_kernel,
-        out_shape=shape(32, width),
-        in_specs=[VMEM] * 5,
-        out_specs=pl.BlockSpec(memory_space=pl.ANY),
-        scratch_shapes=[pltpu.VMEM((32, width), BF), pltpu.SemaphoreType.DMA((4,))],
-        compiler_params=PARAMS,
-    )(own, left_one, left_three, right_one, right_three)
+    out = ()
+    for base, pair in ((half, (right_one, right_three)), (0, (left_one, left_three))):
+        out = pl.pallas_call(
+            functools.partial(sum_kernel, base),
+            out_shape=(shape(32, width),),
+            in_specs=[VMEM] * 3 + [pl.BlockSpec(memory_space=pl.ANY)] * len(out),
+            out_specs=(pl.BlockSpec(memory_space=pl.ANY),),
+            scratch_shapes=[pltpu.VMEM((32, half), BF), pltpu.SemaphoreType.DMA((2,))],
+            input_output_aliases={3: 0} if out else {},
+            compiler_params=PARAMS,
+        )(own, *pair, *out)
+    return out[0]
 
 
 def solution(mesh):

time: 66 us -> 67.2 us (1.018)
    pallas_call x1 -> x2, Pallas kernels: 0.79 us -> 1.43 us  [body(): pl.pallas_call(functools.partial(sum_kernel, base), out_shape=(shape(32,...]
  transfers between devices with their start and end apart: 24 -> 24, of which waited for: 13 -> 13; matrix products, arithmetic and copies ran while one was open for 0% -> 0% of each run, Pallas kernels for 5% -> 6%
where the time goes in v7:
time: 67.2 us; the launch traced here: 67.1 us
  starting transfers between devices  35.7 us (53%)
  waiting for transfers between devices  23.9 us (36%)
  Pallas kernels  7.08 us (11%)
    ppermute x17, starting transfers between devices, swapped(): return lax.ppermute(value, axis, [(i, i ^ mask) for i in range(size)])  24.8 us
    ppermute x17, waiting for transfers between devices, swapped(): return lax.ppermute(value, axis, [(i, i ^ mask) for i in range(size)])  19 us
    ppermute x3, starting transfers between devices, swapped_by_core(): return lax.ppermute(value, (axis, 'c'), pairs)  10.6 us
    pallas_call x4, Pallas kernels, attend(): pl.pallas_call(functools.partial(attend_kernel, count, chunks, early, mer...  3.88 us
    ppermute x4, waiting for transfers between devices, moved(): lax.ppermute(value, axis, [(i, (i + by) % size) for i in range(size)])  2.62 us
    ppermute x3, waiting for transfers between devices, swapped_by_core(): return lax.ppermute(value, (axis, 'c'), pairs)  2.37 us
    pallas_call x2, Pallas kernels, body(): pl.pallas_call(functools.partial(sum_kernel, base), out_shape=(shape(32,...  1.43 us
  transfers between devices with their start and end apart: 24, of which 13 were waited for; matrix products, arithmetic and copies ran while one was open for 0% of the time, Pallas kernels for 6%

profile of v7, /device:TPU:32, one launch (start us, length us, event | category | flops | bytes accessed | tf_op | source)
XLA Modules:
  0.0 67.1 jit_solution(12410284394126369876)
XLA Ops:
  0.0 1.0 %shard_map.55 = (bf16[32,768]{1,0:T(8,128)(2,1)S(1)}, bf16[32,768]{1,0:T(8,128)(2,1)S(1)}, bf16[32,768]{1,0:T(8,128)(2,1)S(1)}, bf16[32,768]{1,0:T(8,128)(2,1)S(1)}, bf16[16,128]{1,0:T(8,128)(2,1)S(1)}) custom-call(bf16[32,1024]{1,0:T(8,128)(2,1)} %q_ref.1, bf16[32,1024]{1,0:T(8,128)(2,1)} %k_ref.1, bf16[32,1024]{1,0:T(8,128)(2,1)} %v_ref.1, ...), custom_call_target="tpu_custom_call" | custom-call | tf_op jit(solution)/shard_map/pallas_call | solution.py:293
  1.0 3.3 %collective-permute-start = (bf16[32,768]{1,0:T(8,128)(2,1)S(1)}, bf16[32,768]{1,0:T(8,128)(2,1)S(1)}, u32[]{:S(2)}, u32[]{:S(2)}) collective-permute-start(bf16[32,768]{1,0:T(8,128)(2,1)S(1)} %get-tuple-element.32), channel_id=1, source_target_pairs={{0,2},{1,3},{2,0},{3,1},{4,6},{5,7},{6,4},{7,5},{8,10},{9,11},{10,... | collective-permute-start | bytes 147464 | tf_op jit(solution)/shard_map/ppermute | solution.py:32
  4.2 1.1 %collective-permute-start.1 = (bf16[32,768]{1,0:T(8,128)(2,1)S(1)}, bf16[32,768]{1,0:T(8,128)(2,1)S(1)}, u32[]{:S(2)}, u32[]{:S(2)}) collective-permute-start(bf16[32,768]{1,0:T(8,128)(2,1)S(1)} %get-tuple-element.33), channel_id=1, source_target_pairs={{0,3},{1,2},{2,1},{3,0},{4,7},{5,6},{6,5},{7,4},{8,11},{9,10},{10,... | collective-permute-start | bytes 147464 | tf_op jit(solution)/shard_map/ppermute | solution.py:32
  5.3 1.3 %collective-permute-done.refs_1_ = bf16[32,768]{1,0:T(8,128)(2,1)S(1)} collective-permute-done((bf16[32,768]{1,0:T(8,128)(2,1)S(1)}, bf16[32,768]{1,0:T(8,128)(2,1)S(1)}, u32[]{:S(2)}, u32[]{:S(2)}) %collective-permute-start) | collective-permute-done | bytes 49184 | tf_op jit(solution)/shard_map/ppermute | solution.py:32
  6.6 2.9 %collective-permute-done.1.refs_2_ = bf16[32,768]{1,0:T(8,128)(2,1)S(1)} collective-permute-done((bf16[32,768]{1,0:T(8,128)(2,1)S(1)}, bf16[32,768]{1,0:T(8,128)(2,1)S(1)}, u32[]{:S(2)}, u32[]{:S(2)}) %collective-permute-start.1) | collective-permute-done | bytes 49184 | tf_op jit(solution)/shard_map/ppermute | solution.py:32
  9.7 1.4 %collective-permute-done.3.got_ref = bf16[144,512]{1,0:T(8,128)(2,1)S(1)} collective-permute-done((bf16[144,512]{1,0:T(8,128)(2,1)S(1)}, bf16[144,512]{1,0:T(8,128)(2,1)S(1)}, u32[]{:S(2)}, u32[]{:S(2)}) %collective-permute-start.3) | collective-permute-done | bytes 147488 | tf_op jit(solution)/shard_map/ppermute | solution.py:27
  11.1 3.4 %collective-permute-start.9 = (bf16[544,128]{1,0:T(8,128)(2,1)S(1)}, bf16[544,128]{1,0:T(8,128)(2,1)S(1)}, u32[]{:S(2)}, u32[]{:S(2)}) collective-permute-start(bf16[544,128]{1,0:T(8,128)(2,1)S(1)} %get-tuple-element.37.refs_2_.refs_0_), channel_id=1, source_target_pairs={{0,16},{4,52},{16,0},{20,36},{32,48},{36,20},{48,32},{52,4},{1,17}... | collective-permute-start | bytes 417800 | tf_op jit(solution)/shard_map/ppermute | solution.py:38
  14.5 3.0 %collective-permute-start.7 = (bf16[256,256]{1,0:T(8,128)(2,1)S(1)}, bf16[256,256]{1,0:T(8,128)(2,1)S(1)}, u32[]{:S(2)}, u32[]{:S(2)}) collective-permute-start(bf16[256,256]{1,0:T(8,128)(2,1)S(1)} %get-tuple-element.38.refs_5_), channel_id=1, source_target_pairs={{0,128},{64,192},{128,0},{192,64},{1,129},{65,193},{129,1},{193,65... | collective-permute-start | bytes 393224 | tf_op jit(solution)/shard_map/ppermute | solution.py:32
  18.7 4.7 %collective-permute-start.10 = (bf16[272,128]{1,0:T(8,128)(2,1)S(1)}, bf16[272,128]{1,0:T(8,128)(2,1)S(1)}, u32[]{:S(2)}, u32[]{:S(2)}) collective-permute-start(bf16[272,128]{1,0:T(8,128)(2,1)S(1)} %get-tuple-element.58), channel_id=1, source_target_pairs={{0,48},{4,20},{16,32},{20,4},{32,16},{36,52},{48,0},{52,36},{1,49}... | collective-permute-start | bytes 208904 | tf_op jit(solution)/shard_map/ppermute | solution.py:38
  23.5 1.6 %collective-permute-start.5 = (bf16[256,256]{1,0:T(8,128)(2,1)S(1)}, bf16[256,256]{1,0:T(8,128)(2,1)S(1)}, u32[]{:S(2)}, u32[]{:S(2)}) collective-permute-start(bf16[256,256]{1,0:T(8,128)(2,1)S(1)} %collective-permute-done.4.refs_4_), channel_id=1, source_target_pairs={{0,64},{64,0},{128,192},{192,128},{1,65},{65,1},{129,193},{193,129... | collective-permute-start | bytes 393224 | tf_op jit(solution)/shard_map/ppermute | solution.py:32
  25.0 2.1 %collective-permute-start.6 = (bf16[256,256]{1,0:T(8,128)(2,1)S(1)}, bf16[256,256]{1,0:T(8,128)(2,1)S(1)}, u32[]{:S(2)}, u32[]{:S(2)}) collective-permute-start(bf16[256,256]{1,0:T(8,128)(2,1)S(1)} %collective-permute-done.4.refs_4_), channel_id=1, source_target_pairs={{0,192},{64,128},{128,64},{192,0},{1,193},{65,129},{129,65},{193,1... | collective-permute-start | bytes 393224 | tf_op jit(solution)/shard_map/ppermute | solution.py:32
  27.1 2.1 %collective-permute-start.8 = (bf16[256,256]{1,0:T(8,128)(2,1)S(1)}, bf16[256,256]{1,0:T(8,128)(2,1)S(1)}, u32[]{:S(2)}, u32[]{:S(2)}) collective-permute-start(bf16[256,256]{1,0:T(8,128)(2,1)S(1)} %collective-permute-done.7.refs_6_), channel_id=1, source_target_pairs={{0,8},{8,0},{1,9},{9,1},{2,10},{10,2},{3,11},{11,3},{4,12},{12,4},... | collective-permute-start | bytes 393224 | tf_op jit(solution)/shard_map/ppermute | solution.py:32
  29.2 1.7 %shard_map.58 = (f32[128,256]{1,0:T(8,128)S(1)}, f32[8,256]{1,0:T(8,128)S(1)}, f32[128,256]{1,0:T(8,128)S(1)}, f32[8,256]{1,0:T(8,128)S(1)}, f32[128,256]{1,0:T(...) custom-call(bf16[272,128]{1,0:T(8,128)(2,1)S(1)} %collective-permute-done.10.refs_0_, ...), custom_call_target="tpu_custom_call" | custom-call | flops 5368709120 | bytes 2097152 | tf_op jit(solution)/shard_map/pallas_call | solution.py:272
  31.0 1.1 %collective-permute-done.6.refs_3_.refs_2_ = bf16[256,256]{1,0:T(8,128)(2,1)S(1)} collective-permute-done((bf16[256,256]{1,0:T(8,128)(2,1)S(1)}, bf16[256,256]{1,0:T(8,128)(2,1)S(1)}, u32[]{:S(2)}, u32[]{:S(2)}) %collective-permute-start.6) | collective-permute-done | bytes 131104 | tf_op jit(solution)/shard_map/ppermute | solution.py:32
  32.1 0.7 collective-permute-done.8.refs_4_.refs_3_
  32.7 0.9 %shard_map.59 = (bf16[144,256]{1,0:T(8,128)(2,1)S(1)}, bf16[144,256]{1,0:T(8,128)(2,1)S(1)}) custom-call(bf16[272,128]{1,0:T(8,128)(2,1)S(1)} %collective-permute-done.10.refs_0_, bf16[544,128]{1,0:T(8,128)(2,1)S(1)} %collective-permute-done.9.refs_3_.refs_1_, bf16[256,256]{1,0:T(8,128)(2,1)S(1)} %collective-permute-done.5.refs_2_.refs_1_, ...), custom_call_target="tpu_custom_call" | custom-call | flops 1610612736 | bytes 2097152 | tf_op jit(solution)/shard_map/pallas_call | solution.py:272
  33.8 2.7 %collective-permute-start.14 = (bf16[144,256]{1,0:T(8,128)(2,1)S(1)}, bf16[144,256]{1,0:T(8,128)(2,1)S(1)}, u32[]{:S(2)}, u32[]{:S(2)}) collective-permute-start(bf16[144,256]{1,0:T(8,128)(2,1)S(1)} %get-tuple-element.45), channel_id=1, source_target_pairs={{0,32},{16,48},{32,0},{48,16},{1,33},{17,49},{33,1},{49,17},{2,34}... | collective-permute-start | bytes 221192 | tf_op jit(solution)/shard_map/ppermute | solution.py:32
  37.1 2.5 %collective-permute-start.16 = (bf16[288,256]{1,0:T(8,128)(2,1)S(1)}, bf16[288,256]{1,0:T(8,128)(2,1)S(1)}, u32[]{:S(2)}, u32[]{:S(2)}) collective-permute-start(bf16[288,256]{1,0:T(8,128)(2,1)S(1)} %shard_map.62), channel_id=1, source_target_pairs={{0,48},{4,20},{16,32},{20,4},{32,16},{36,52},{48,0},{52,36},{1,49}... | collective-permute-start | bytes 442376 | tf_op jit(solution)/shard_map/ppermute | solution.py:38
  39.7 4.2 %collective-permute-done.14.refs_6_ = bf16[144,256]{1,0:T(8,128)(2,1)S(1)} collective-permute-done((bf16[144,256]{1,0:T(8,128)(2,1)S(1)}, bf16[144,256]{1,0:T(8,128)(2,1)S(1)}, u32[]{:S(2)}, u32[]{:S(2)}) %collective-permute-start.14) | collective-permute-done | bytes 73760 | tf_op jit(solution)/shard_map/ppermute | solution.py:32
  44.5 2.4 %collective-permute-done.16.side_ref = bf16[288,256]{1,0:T(8,128)(2,1)S(1)} collective-permute-done((bf16[288,256]{1,0:T(8,128)(2,1)S(1)}, bf16[288,256]{1,0:T(8,128)(2,1)S(1)}, u32[]{:S(2)}, u32[]{:S(2)}) %collective-permute-start.16) | collective-permute-done | bytes 147488 | tf_op jit(solution)/shard_map/ppermute | solution.py:38
  47.1 1.3 %collective-permute-done.17.got_ref = bf16[288,128]{1,0:T(8,128)(2,1)S(1)} collective-permute-done((bf16[288,128]{1,0:T(8,128)(2,1)S(1)}, bf16[288,128]{1,0:T(8,128)(2,1)S(1)}, u32[]{:S(2)}, u32[]{:S(2)}) %collective-permute-start.17) | collective-permute-done | bytes 73760 | tf_op jit(solution)/shard_map/ppermute | solution.py:27
  49.1 2.1 %collective-permute-start.20 = (bf16[32,2560]{1,0:T(8,128)(2,1)S(1)}, bf16[32,2560]{1,0:T(8,128)(2,1)S(1)}, u32[]{:S(2)}, u32[]{:S(2)}) collective-permute-start(bf16[32,2560]{1,0:T(8,128)(2,1)S(1)} %get-tuple-element.55), channel_id=1, source_target_pairs={{0,3},{1,2},{2,1},{3,0},{4,7},{5,6},{6,5},{7,4},{8,11},{9,10},{10,... | collective-permute-start | bytes 491528 | tf_op jit(solution)/shard_map/ppermute | solution.py:32
  51.2 1.3 %collective-permute-start.23 = (bf16[32,2560]{1,0:T(8,128)(2,1)S(1)}, bf16[32,2560]{1,0:T(8,128)(2,1)S(1)}, u32[]{:S(2)}, u32[]{:S(2)}) collective-permute-start(bf16[32,2560]{1,0:T(8,128)(2,1)S(1)} %slice.23), channel_id=1, source_target_pairs={{0,3},{1,2},{2,1},{3,0},{4,7},{5,6},{6,5},{7,4},{8,11},{9,10},{10,... | collective-permute-start | bytes 491528 | tf_op jit(solution)/shard_map/ppermute | solution.py:32
  52.5 2.8 %collective-permute-done.19.a_ref = bf16[32,2560]{1,0:T(8,128)(2,1)S(1)} collective-permute-done((bf16[32,2560]{1,0:T(8,128)(2,1)S(1)}, bf16[32,2560]{1,0:T(8,128)(2,1)S(1)}, u32[]{:S(2)}, u32[]{:S(2)}) %collective-permute-start.19) | collective-permute-done | bytes 163872 | tf_op jit(solution)/shard_map/ppermute | solution.py:32
  55.3 2.1 %collective-permute-done.20.b_ref = bf16[32,2560]{1,0:T(8,128)(2,1)S(1)} collective-permute-done((bf16[32,2560]{1,0:T(8,128)(2,1)S(1)}, bf16[32,2560]{1,0:T(8,128)(2,1)S(1)}, u32[]{:S(2)}, u32[]{:S(2)}) %collective-permute-start.20) | collective-permute-done | bytes 163872 | tf_op jit(solution)/shard_map/ppermute | solution.py:32
  57.5 0.8 %collective-permute-start.22 = (bf16[32,2560]{1,0:T(8,128)(2,1)S(1)}, bf16[32,2560]{1,0:T(8,128)(2,1)S(1)}, u32[]{:S(2)}, u32[]{:S(2)}) collective-permute-start(bf16[32,2560]{1,0:T(8,128)(2,1)S(1)} %get-tuple-element.54), channel_id=1, source_target_pairs={{0,1},{1,0},{2,3},{3,2},{4,5},{5,4},{6,7},{7,6},{8,9},{9,8},{10,11... | collective-permute-start | bytes 491528 | tf_op jit(solution)/shard_map/ppermute | solution.py:32
  58.3 1.4 %collective-permute-start.18 = (bf16[32,2560]{1,0:T(8,128)(2,1)S(1)}, bf16[32,2560]{1,0:T(8,128)(2,1)S(1)}, u32[]{:S(2)}, u32[]{:S(2)}) collective-permute-start(bf16[32,2560]{1,0:T(8,128)(2,1)S(1)} %slice.20), channel_id=1, source_target_pairs={{0,1},{1,0},{2,3},{3,2},{4,5},{5,4},{6,7},{7,6},{8,9},{9,8},{10,11... | collective-permute-start | bytes 491528 | tf_op jit(solution)/shard_map/ppermute | solution.py:32
  59.7 2.0 %collective-permute-start.21 = (bf16[32,2560]{1,0:T(8,128)(2,1)S(1)}, bf16[32,2560]{1,0:T(8,128)(2,1)S(1)}, u32[]{:S(2)}, u32[]{:S(2)}) collective-permute-start(bf16[32,2560]{1,0:T(8,128)(2,1)S(1)} %get-tuple-element.53), channel_id=1, source_target_pairs={{0,3},{1,2},{2,1},{3,0},{4,7},{5,6},{6,5},{7,4},{8,11},{9,10},{10,... | collective-permute-start | bytes 491528 | tf_op jit(solution)/shard_map/ppermute | solution.py:32
  61.7 2.2 %collective-permute-done.22.a_ref = bf16[32,2560]{1,0:T(8,128)(2,1)S(1)} collective-permute-done((bf16[32,2560]{1,0:T(8,128)(2,1)S(1)}, bf16[32,2560]{1,0:T(8,128)(2,1)S(1)}, u32[]{:S(2)}, u32[]{:S(2)}) %collective-permute-start.22) | collective-permute-done | bytes 163872 | tf_op jit(solution)/shard_map/ppermute | solution.py:32
  64.0 0.7 %shard_map.66.refs_0_ = bf16[32,5120]{1,0:T(8,128)(2,1)} custom-call(bf16[32,5120]{1,0:T(8,128)(2,1)S(1)} %get-tuple-element.49.own_ref, bf16[32,2560]{1,0:T(8,128)(2,1)S(1)} %collective-permute-done.22.a_ref, bf16[32,2560]{1,0:T(8,128)(2,1)S(1)} %collective-permute-done.23.b_ref), custom_call_target="tpu_custom_call" | custom-call | tf_op jit(solution)/shard_map/pallas_call | solution.py:384
  64.7 1.0 %collective-permute-done.18.a_ref = bf16[32,2560]{1,0:T(8,128)(2,1)S(1)} collective-permute-done((bf16[32,2560]{1,0:T(8,128)(2,1)S(1)}, bf16[32,2560]{1,0:T(8,128)(2,1)S(1)}, u32[]{:S(2)}, u32[]{:S(2)}) %collective-permute-start.18) | collective-permute-done | bytes 163872 | tf_op jit(solution)/shard_map/ppermute | solution.py:32
  66.2 0.7 %shard_map.67 = bf16[32,5120]{1,0:T(8,128)(2,1)} custom-call(bf16[32,5120]{1,0:T(8,128)(2,1)S(1)} %get-tuple-element.49.own_ref, bf16[32,2560]{1,0:T(8,128)(2,1)S(1)} %collective-permute-done.18.a_ref, bf16[32,2560]{1,0:T(8,128)(2,1)S(1)} %collective-permute-done.21.b_ref, bf16[32,5120]{1,0:T(8,128)(2,1)} %shard_map.66.refs_0_), custom_call_target="tpu_custom_call", output_to_operand_aliasing={{}: (3, {})} | custom-call | tf_op jit(solution)/shard_map/pallas_call | solution.py:384
  (35 shorter events, 4.3 us)
Async XLA Ops:
  1.0 5.7 %collective-permute-start = (bf16[32,768]{1,0:T(8,128)(2,1)S(1)}, bf16[32,768]{1,0:T(8,128)(2,1)S(1)}, u32[]{:S(2)}, u32[]{:S(2)}) collective-permute-start(bf16[32,768]{1,0:T(8,128)(2,1)S(1)} %get-tuple-element.32), channel_id=1, source_target_pairs={{0,2},{1,3},{2,0},{3,1},{4,6},{5,7},{6,4},{7,5},{8,10},{9,11},{10,... | collective-permute-start | bytes 147464 | tf_op jit(solution)/shard_map/ppermute | solution.py:32
  4.2 5.3 %collective-permute-start.1 = (bf16[32,768]{1,0:T(8,128)(2,1)S(1)}, bf16[32,768]{1,0:T(8,128)(2,1)S(1)}, u32[]{:S(2)}, u32[]{:S(2)}) collective-permute-start(bf16[32,768]{1,0:T(8,128)(2,1)S(1)} %get-tuple-element.33), channel_id=1, source_target_pairs={{0,3},{1,2},{2,1},{3,0},{4,7},{5,6},{6,5},{7,4},{8,11},{9,10},{10,... | collective-permute-start | bytes 147464 | tf_op jit(solution)/shard_map/ppermute | solution.py:32
  5.3 4.2 %collective-permute-start.2 = (bf16[32,768]{1,0:T(8,128)(2,1)S(1)}, bf16[32,768]{1,0:T(8,128)(2,1)S(1)}, u32[]{:S(2)}, u32[]{:S(2)}) collective-permute-start(bf16[32,768]{1,0:T(8,128)(2,1)S(1)} %get-tuple-element.34), channel_id=1, source_target_pairs={{0,1},{1,0},{2,3},{3,2},{4,5},{5,4},{6,7},{7,6},{8,9},{9,8},{10,11... | collective-permute-start | bytes 147464 | tf_op jit(solution)/shard_map/ppermute | solution.py:32
  9.6 1.5 %collective-permute-start.3 = (bf16[144,512]{1,0:T(8,128)(2,1)S(1)}, bf16[144,512]{1,0:T(8,128)(2,1)S(1)}, u32[]{:S(2)}, u32[]{:S(2)}) collective-permute-start(bf16[144,512]{1,0:T(8,128)(2,1)S(1)} %get-tuple-element.36), channel_id=1, source_target_pairs={{0,4},{4,0},{1,5},{5,1},{2,6},{6,2},{3,7},{7,3},{8,12},{12,8},{9,1... | collective-permute-start | bytes 442376 | tf_op jit(solution)/shard_map/ppermute | solution.py:27
  11.1 7.6 %collective-permute-start.9 = (bf16[544,128]{1,0:T(8,128)(2,1)S(1)}, bf16[544,128]{1,0:T(8,128)(2,1)S(1)}, u32[]{:S(2)}, u32[]{:S(2)}) collective-permute-start(bf16[544,128]{1,0:T(8,128)(2,1)S(1)} %get-tuple-element.37.refs_2_.refs_0_), channel_id=1, source_target_pairs={{0,16},{4,52},{16,0},{20,36},{32,48},{36,20},{48,32},{52,4},{1,17}... | collective-permute-start | bytes 417800 | tf_op jit(solution)/shard_map/ppermute | solution.py:38
  14.4 9.0 %collective-permute-start.4 = (bf16[256,256]{1,0:T(8,128)(2,1)S(1)}, bf16[256,256]{1,0:T(8,128)(2,1)S(1)}, u32[]{:S(2)}, u32[]{:S(2)}) collective-permute-start(bf16[256,256]{1,0:T(8,128)(2,1)S(1)} %get-tuple-element.38.refs_5_), channel_id=1, source_target_pairs={{0,8},{8,0},{1,9},{9,1},{2,10},{10,2},{3,11},{11,3},{4,12},{12,4},... | collective-permute-start | bytes 393224 | tf_op jit(solution)/shard_map/ppermute | solution.py:32
  14.5 8.9 %collective-permute-start.7 = (bf16[256,256]{1,0:T(8,128)(2,1)S(1)}, bf16[256,256]{1,0:T(8,128)(2,1)S(1)}, u32[]{:S(2)}, u32[]{:S(2)}) collective-permute-start(bf16[256,256]{1,0:T(8,128)(2,1)S(1)} %get-tuple-element.38.refs_5_), channel_id=1, source_target_pairs={{0,128},{64,192},{128,0},{192,64},{1,129},{65,193},{129,1},{193,65... | collective-permute-start | bytes 393224 | tf_op jit(solution)/shard_map/ppermute | solution.py:32
  17.6 7.5 %collective-permute-start.12 = (bf16[256,256]{1,0:T(8,128)(2,1)S(1)}, bf16[256,256]{1,0:T(8,128)(2,1)S(1)}, u32[]{:S(2)}, u32[]{:S(2)}) collective-permute-start(bf16[256,256]{1,0:T(8,128)(2,1)S(1)} %get-tuple-element.38.refs_5_), channel_id=1, source_target_pairs={{0,64},{64,0},{128,192},{192,128},{1,65},{65,1},{129,193},{193,129... | collective-permute-start | bytes 393224 | tf_op jit(solution)/shard_map/ppermute | solution.py:32
  18.2 9.0 %collective-permute-start.13 = (bf16[256,256]{1,0:T(8,128)(2,1)S(1)}, bf16[256,256]{1,0:T(8,128)(2,1)S(1)}, u32[]{:S(2)}, u32[]{:S(2)}) collective-permute-start(bf16[256,256]{1,0:T(8,128)(2,1)S(1)} %get-tuple-element.38.refs_5_), channel_id=1, source_target_pairs={{0,192},{64,128},{128,64},{192,0},{1,193},{65,129},{129,65},{193,1... | collective-permute-start | bytes 393224 | tf_op jit(solution)/shard_map/ppermute | solution.py:32
  18.7 10.5 %collective-permute-start.10 = (bf16[272,128]{1,0:T(8,128)(2,1)S(1)}, bf16[272,128]{1,0:T(8,128)(2,1)S(1)}, u32[]{:S(2)}, u32[]{:S(2)}) collective-permute-start(bf16[272,128]{1,0:T(8,128)(2,1)S(1)} %get-tuple-element.58), channel_id=1, source_target_pairs={{0,48},{4,20},{16,32},{20,4},{32,16},{36,52},{48,0},{52,36},{1,49}... | collective-permute-start | bytes 208904 | tf_op jit(solution)/shard_map/ppermute | solution.py:38
  23.5 5.8 %collective-permute-start.11 = (bf16[272,128]{1,0:T(8,128)(2,1)S(1)}, bf16[272,128]{1,0:T(8,128)(2,1)S(1)}, u32[]{:S(2)}, u32[]{:S(2)}) collective-permute-start(bf16[272,128]{1,0:T(8,128)(2,1)S(1)} %get-tuple-element.57), channel_id=1, source_target_pairs={{0,4},{4,0},{1,5},{5,1},{2,6},{6,2},{3,7},{7,3},{8,12},{12,8},{9,1... | collective-permute-start | bytes 208904 | tf_op jit(solution)/shard_map/ppermute | solution.py:27
  23.5 7.5 %collective-permute-start.5 = (bf16[256,256]{1,0:T(8,128)(2,1)S(1)}, bf16[256,256]{1,0:T(8,128)(2,1)S(1)}, u32[]{:S(2)}, u32[]{:S(2)}) collective-permute-start(bf16[256,256]{1,0:T(8,128)(2,1)S(1)} %collective-permute-done.4.refs_4_), channel_id=1, source_target_pairs={{0,64},{64,0},{128,192},{192,128},{1,65},{65,1},{129,193},{193,129... | collective-permute-start | bytes 393224 | tf_op jit(solution)/shard_map/ppermute | solution.py:32
  25.0 7.1 %collective-permute-start.6 = (bf16[256,256]{1,0:T(8,128)(2,1)S(1)}, bf16[256,256]{1,0:T(8,128)(2,1)S(1)}, u32[]{:S(2)}, u32[]{:S(2)}) collective-permute-start(bf16[256,256]{1,0:T(8,128)(2,1)S(1)} %collective-permute-done.4.refs_4_), channel_id=1, source_target_pairs={{0,192},{64,128},{128,64},{192,0},{1,193},{65,129},{129,65},{193,1... | collective-permute-start | bytes 393224 | tf_op jit(solution)/shard_map/ppermute | solution.py:32
  27.1 5.6 %collective-permute-start.8 = (bf16[256,256]{1,0:T(8,128)(2,1)S(1)}, bf16[256,256]{1,0:T(8,128)(2,1)S(1)}, u32[]{:S(2)}, u32[]{:S(2)}) collective-permute-start(bf16[256,256]{1,0:T(8,128)(2,1)S(1)} %collective-permute-done.7.refs_6_), channel_id=1, source_target_pairs={{0,8},{8,0},{1,9},{9,1},{2,10},{10,2},{3,11},{11,3},{4,12},{12,4},... | collective-permute-start | bytes 393224 | tf_op jit(solution)/shard_map/ppermute | solution.py:32
  33.7 3.4 %collective-permute-start.15 = (bf16[144,256]{1,0:T(8,128)(2,1)S(1)}, bf16[144,256]{1,0:T(8,128)(2,1)S(1)}, u32[]{:S(2)}, u32[]{:S(2)}) collective-permute-start(bf16[144,256]{1,0:T(8,128)(2,1)S(1)} %get-tuple-element.48), channel_id=1, source_target_pairs={{0,4},{4,0},{1,5},{5,1},{2,6},{6,2},{3,7},{7,3},{8,12},{12,8},{9,1... | collective-permute-start | bytes 221192 | tf_op jit(solution)/shard_map/ppermute | solution.py:27
  33.8 10.1 %collective-permute-start.14 = (bf16[144,256]{1,0:T(8,128)(2,1)S(1)}, bf16[144,256]{1,0:T(8,128)(2,1)S(1)}, u32[]{:S(2)}, u32[]{:S(2)}) collective-permute-start(bf16[144,256]{1,0:T(8,128)(2,1)S(1)} %get-tuple-element.45), channel_id=1, source_target_pairs={{0,32},{16,48},{32,0},{48,16},{1,33},{17,49},{33,1},{49,17},{2,34}... | collective-permute-start | bytes 221192 | tf_op jit(solution)/shard_map/ppermute | solution.py:32
  36.5 11.8 %copy-start = (bf16[256,5120]{1,0:T(8,128)(2,1)S(1)}, bf16[256,5120]{1,0:T(8,128)(2,1)}, u32[]{:S(2)}) copy-start(bf16[256,5120]{1,0:T(8,128)(2,1)} %w_ref.1) | copy-start | bytes 7864324
  37.1 9.8 %collective-permute-start.16 = (bf16[288,256]{1,0:T(8,128)(2,1)S(1)}, bf16[288,256]{1,0:T(8,128)(2,1)S(1)}, u32[]{:S(2)}, u32[]{:S(2)}) collective-permute-start(bf16[288,256]{1,0:T(8,128)(2,1)S(1)} %shard_map.62), channel_id=1, source_target_pairs={{0,48},{4,20},{16,32},{20,4},{32,16},{36,52},{48,0},{52,36},{1,49}... | collective-permute-start | bytes 442376 | tf_op jit(solution)/shard_map/ppermute | solution.py:38
  47.0 1.4 %collective-permute-start.17 = (bf16[288,128]{1,0:T(8,128)(2,1)S(1)}, bf16[288,128]{1,0:T(8,128)(2,1)S(1)}, u32[]{:S(2)}, u32[]{:S(2)}) collective-permute-start(bf16[288,128]{1,0:T(8,128)(2,1)S(1)} %shard_map.63), channel_id=1, source_target_pairs={{0,4},{4,0},{1,5},{5,1},{2,6},{6,2},{3,7},{7,3},{8,12},{12,8},{9,1... | collective-permute-start | bytes 221192 | tf_op jit(solution)/shard_map/ppermute | solution.py:27
  49.0 6.3 %collective-permute-start.19 = (bf16[32,2560]{1,0:T(8,128)(2,1)S(1)}, bf16[32,2560]{1,0:T(8,128)(2,1)S(1)}, u32[]{:S(2)}, u32[]{:S(2)}) collective-permute-start(bf16[32,2560]{1,0:T(8,128)(2,1)S(1)} %get-tuple-element.56), channel_id=1, source_target_pairs={{0,1},{1,0},{2,3},{3,2},{4,5},{5,4},{6,7},{7,6},{8,9},{9,8},{10,11... | collective-permute-start | bytes 491528 | tf_op jit(solution)/shard_map/ppermute | solution.py:32
  49.1 8.3 %collective-permute-start.20 = (bf16[32,2560]{1,0:T(8,128)(2,1)S(1)}, bf16[32,2560]{1,0:T(8,128)(2,1)S(1)}, u32[]{:S(2)}, u32[]{:S(2)}) collective-permute-start(bf16[32,2560]{1,0:T(8,128)(2,1)S(1)} %get-tuple-element.55), channel_id=1, source_target_pairs={{0,3},{1,2},{2,1},{3,0},{4,7},{5,6},{6,5},{7,4},{8,11},{9,10},{10,... | collective-permute-start | bytes 491528 | tf_op jit(solution)/shard_map/ppermute | solution.py:32
  51.2 10.5 %collective-permute-start.23 = (bf16[32,2560]{1,0:T(8,128)(2,1)S(1)}, bf16[32,2560]{1,0:T(8,128)(2,1)S(1)}, u32[]{:S(2)}, u32[]{:S(2)}) collective-permute-start(bf16[32,2560]{1,0:T(8,128)(2,1)S(1)} %slice.23), channel_id=1, source_target_pairs={{0,3},{1,2},{2,1},{3,0},{4,7},{5,6},{6,5},{7,4},{8,11},{9,10},{10,... | collective-permute-start | bytes 491528 | tf_op jit(solution)/shard_map/ppermute | solution.py:32
  57.5 6.5 %collective-permute-start.22 = (bf16[32,2560]{1,0:T(8,128)(2,1)S(1)}, bf16[32,2560]{1,0:T(8,128)(2,1)S(1)}, u32[]{:S(2)}, u32[]{:S(2)}) collective-permute-start(bf16[32,2560]{1,0:T(8,128)(2,1)S(1)} %get-tuple-element.54), channel_id=1, source_target_pairs={{0,1},{1,0},{2,3},{3,2},{4,5},{5,4},{6,7},{7,6},{8,9},{9,8},{10,11... | collective-permute-start | bytes 491528 | tf_op jit(solution)/shard_map/ppermute | solution.py:32
  58.3 7.4 %collective-permute-start.18 = (bf16[32,2560]{1,0:T(8,128)(2,1)S(1)}, bf16[32,2560]{1,0:T(8,128)(2,1)S(1)}, u32[]{:S(2)}, u32[]{:S(2)}) collective-permute-start(bf16[32,2560]{1,0:T(8,128)(2,1)S(1)} %slice.20), channel_id=1, source_target_pairs={{0,1},{1,0},{2,3},{3,2},{4,5},{5,4},{6,7},{7,6},{8,9},{9,8},{10,11... | collective-permute-start | bytes 491528 | tf_op jit(solution)/shard_map/ppermute | solution.py:32
  59.7 6.5 %collective-permute-start.21 = (bf16[32,2560]{1,0:T(8,128)(2,1)S(1)}, bf16[32,2560]{1,0:T(8,128)(2,1)S(1)}, u32[]{:S(2)}, u32[]{:S(2)}) collective-permute-start(bf16[32,2560]{1,0:T(8,128)(2,1)S(1)} %get-tuple-element.53), channel_id=1, source_target_pairs={{0,3},{1,2},{2,1},{3,0},{4,7},{5,6},{6,5},{7,4},{8,11},{9,10},{10,... | collective-permute-start | bytes 491528 | tf_op jit(solution)/shard_map/ppermute | solution.py:32
